TPU v7x, 512 devices: a whole 4x4x16 slice. The times are simulated.
512 devices in a mesh: vec: 32 (over x_lo, z), lat: 16 (over x_hi, y, core).
Axes of the slice: x: 4 (x_hi: 2, x_lo: 2; x = x_hi * 2 + x_lo), y: 4, z: 16, core: 2. Of those that a mesh axis runs over, the one named last changes fastest.
Arguments:
- perturb: float32 [128, 8, 384, 720], P('vec', None, 'lat'), may hold values from -6 to 6
- trajectory: bfloat16 [32, 3, 8, 384, 720], P('vec', None, None, 'lat'), may hold values from -3 to 3
- hour_slot: int32 [2], replicated, may hold values from 0 to 31, as said below
- sea_mask: int32 [384, 720], P('lat'), may hold values 0 or 1
Outputs:
- evolved: float32 [128, 8, 384, 720], P('vec', None, 'lat')
Inputs may be any that keep to these rules, and one draw needn't show every extreme that they name: `hour_slot`: 2 distinct indices of saved hours; one of them is always the last saved hour, 31.
All inputs are finite; a program needn't handle non-finite values. No bound on the sum of `sea_mask` on one device may be relied on, other than what follows from the above.
Results may differ from a plain program's by a relative error of at most 0.0003.
Values may be sent and summed in bfloat16 or wider, within the bound.
No kernel may reach another device: no remote copies, remote signals or barrier semaphores. Data moves between devices by JAX's collectives and lax.ppermute only.
A program may use at most 128 MiB of HBM per device.

v0:
```python
import jax
import jax.numpy as jnp
from jax import lax
from jax.sharding import PartitionSpec as P

HOURS = 2


def with_halo(cells, sides, width):
    for axis, dim in sides:
        count = lax.axis_size(axis)
        ends = count - 1
        head = lax.slice_in_dim(cells, 0, width, axis=dim)
        tail = lax.slice_in_dim(cells, cells.shape[dim] - width, cells.shape[dim], axis=dim)
        cells = jnp.concatenate(
            [
                lax.ppermute(tail, axis, [(i, (i + 1) % count) for i in range(ends)]),
                cells,
                lax.ppermute(head, axis, [((i + 1) % count, i) for i in range(ends)]),
            ],
            axis=dim,
        )
    return cells


def spread(value, axis, source):
    kept = jnp.where(lax.axis_index(axis) == source, value, 0).astype(value.dtype)
    return lax.psum(kept, axis)


def update_rows(padded, fields, ocean_mask):
    center = padded[:, :, 1:-1]
    northern = padded[:, :, 2:]
    southern = padded[:, :, :-2]
    eastern = jnp.roll(center, -1, axis=3)
    western = jnp.roll(center, 1, axis=3)
    upper_level = jnp.concatenate([center[:, :1], center[:, :-1]], axis=1)
    lower_level = jnp.concatenate([center[:, 1:], center[:, -1:]], axis=1)
    diffuse = 0.06 + 0.015 * fields[0]
    zonal_speed = 0.15 * fields[1]
    merid_speed = 0.15 * fields[2]
    change = diffuse * (eastern + western + northern + southern - 4.0 * center)
    change = change - zonal_speed * (eastern - western) - merid_speed * (northern - southern)
    change = change + 0.1 * (upper_level + lower_level - 2.0 * center)
    return ocean_mask * (center + change)


def with_edges(tracer):
    return with_halo(tracer, (("lat", 2),), 1)


def shards(perturb, trajectory, hour_slot, sea_mask):
    stored_count = trajectory.shape[0]
    ocean_mask = sea_mask.astype(jnp.float32)
    hour_fields = []
    for hour_step in range(HOURS):
        global_slot = hour_slot[hour_step]
        owner_index = global_slot // stored_count
        own_piece = lax.dynamic_index_in_dim(
            trajectory, global_slot % stored_count, 0, keepdims=False
        )
        received = spread(own_piece, "vec", owner_index)
        hour_fields.append(received.astype(jnp.float32))
    tracer = perturb
    for hour_step in range(HOURS):
        fields = hour_fields[hour_step]
        padded = with_edges(tracer)
        tracer = update_rows(padded, fields, ocean_mask)
    return tracer


def solution(mesh):
    return jax.shard_map(
        shards,
        mesh=mesh,
        in_specs=(
            P("vec", None, "lat", None),
            P("vec", None, None, "lat", None),
            P(),
            P("lat", None),
        ),
        out_specs=P("vec", None, "lat", None),
        check_vma=False,
    )
```

profile of v0, /device:TPU:25, one launch (start us, length us, event | category | flops | bytes accessed | tf_op | source)
XLA Modules:
  0.0 309.6 jit_solution(4449083001661980820)
XLA Ops:
  6.5 1.3 fusion.28
  9.2 2.5 select_bitcast_fusion
  11.7 2.4 copy.22
  14.1 0.7 fusion.25
  14.8 2.6 collective-permute-start
  17.4 6.6 %collective-permute-start.1 = (f32[4,8,1,720]{3,1,2,0:T(8,128)}, f32[4,8,1,720]{3,1,2,0:T(8,128)}, u32[]{:S(2)}, u32[]{:S(2)}) collective-permute-start(f32[4,8,1,720]{3,1,2,0:T(8,128)} %get-tuple-element.22), channel_id=1, source_target_pairs={{0,1},{1,2},{2,3},{3,4},{4,5},{5,6},{6,7},{7,8},{8,9},{9,10},{10,1... | collective-permute-start | bytes 276488 | tf_op jit(solution)/shard_map/ppermute | solution.py:17
  24.0 1.1 fusion.27
  25.4 1.0 copy.20
  26.6 2.9 fusion.23
  29.5 2.6 fusion.26
  32.1 223.9 %all-reduce.3.cloned.1.call-done = (bf16[3,8,24,720]{3,2,1,0:T(8,128)(2,1)}, bf16[3,8,24,720]{3,2,1,0:T(8,128)(2,1)}) async-done(((bf16[3,8,24,720]{3,2,1,0:T(8,128)(2,1)}, bf16[3,8,24,720]{3,2,1,0:T(8,128)(2,1)}), (bf16[3,8,24,720]{3,2,1,0:T(8,128)(2,1)}, bf16[3,8,24,720]{3,2,1,0:T(8,128)(2,1)})) %all-reduce.3.cloned.1.call-update) | async-done | bytes 1658896 | tf_op jit(solution)/shard_map/psum | solution.py:28
  256.0 1.5 convert_element_type.13
  258.3 0.9 copy-done.1
  259.3 0.7 copy-done.2
  260.0 0.6 copy-done
  260.6 4.4 %fusion.4 = f32[4,8,24,720]{3,1,2,0:T(8,128)S(1)} fusion(f32[4,8,24,720]{3,1,2,0:T(8,128)S(1)} %copy.22, f32[4,7,24,720]{3,1,2,0:T(8,128)S(1)} %copy-done.3, f32[4,1,24,720]{3,1,2,0:T(1,128)S(1)} %copy.18, f32[4,1,24,720]{3,1,2,0:T(1,128)S(1)} %copy-done.4, f32[4,7,24,720]{3,1,2,0:T(8,128)S(1)} %copy-done.2, f32[4,8,1,720]{3,1,2,0:T(8,128)} %collective-permute-done.1, ...), kind=kLoop, calls=%fused_computation.11 | loop fusion | flops 13824000 | bytes 15183360 | tf_op jit(solution)/shard_map/mul | solution.py:45
  265.0 0.4 fusion.21
  265.5 0.8 fusion.18
  266.3 0.4 fusion.22
  266.7 24.8 %collective-permute-start.2 = (f32[4,8,1,720]{3,1,2,0:T(8,128)S(1)}, f32[4,8,1,720]{3,1,2,0:T(8,128)S(1)}, u32[]{:S(2)}, u32[]{:S(2)}) collective-permute-start(f32[4,8,1,720]{3,1,2,0:T(8,128)S(1)} %get-tuple-element.11), channel_id=1, source_target_pairs={{1,0},{2,1},{3,2},{4,3},{5,4},{6,5},{7,6},{8,7},{9,8},{10,9},{11,1... | collective-permute-start | bytes 276488 | tf_op jit(solution)/shard_map/ppermute | solution.py:19
  291.4 4.1 %collective-permute-start.3 = (f32[4,8,1,720]{3,1,2,0:T(8,128)S(1)}, f32[4,8,1,720]{3,1,2,0:T(8,128)S(1)}, u32[]{:S(2)}, u32[]{:S(2)}) collective-permute-start(f32[4,8,1,720]{3,1,2,0:T(8,128)S(1)} %get-tuple-element.12), channel_id=1, source_target_pairs={{0,1},{1,2},{2,3},{3,4},{4,5},{5,6},{6,7},{7,8},{8,9},{9,10},{10,1... | collective-permute-start | bytes 276488 | tf_op jit(solution)/shard_map/ppermute | solution.py:17
  296.7 0.5 collective-permute-done.3
  297.2 3.4 %fusion.9 = f32[4,8,24,720]{3,1,2,0:T(8,128)S(1)} fusion(f32[4,8,24,720]{3,1,2,0:T(8,128)S(1)} %fusion.4, f32[4,7,24,720]{3,1,2,0:T(8,128)S(1)} %get-tuple-element.14, f32[4,1,24,720]{3,1,2,0:T(1,128)S(1)} %get-tuple-element.16, f32[4,1,24,720]{3,1,2,0:T(1,128)S(1)} %get-tuple-element.15, f32[4,7,24,720]{3,1,2,0:T(8,128)S(1)} %get-tuple-element.13, ...), kind=kLoop, calls=%fused_computation.19 | loop fusion | flops 13824000 | bytes 15183360 | tf_op jit(solution)/shard_map/mul | solution.py:45
  300.6 2.1 copy.26
  (30 shorter events, 2.4 us)
Async XLA Ops:
  6.5 249.5 %all-reduce.3.cloned.1.call-start = ((), (), s32[]{:S(2)}) async-start(), calls=%async_computation | async-start | bytes 3538944 | tf_op jit(solution)/shard_map/psum | solution.py:28
  14.1 12.3 %copy-start.6 = (s32[24,720]{1,0:T(8,128)S(1)}, s32[24,720]{1,0:T(8,128)}, u32[]{:S(2)}) copy-start(s32[24,720]{1,0:T(8,128)} %param.7) | copy-start | bytes 207364
  14.8 243.5 %collective-permute-start = (f32[4,8,1,720]{3,1,2,0:T(8,128)}, f32[4,8,1,720]{3,1,2,0:T(8,128)}, u32[]{:S(2)}, u32[]{:S(2)}) collective-permute-start(f32[4,8,1,720]{3,1,2,0:T(8,128)} %get-tuple-element.21), channel_id=1, source_target_pairs={{1,0},{2,1},{3,2},{4,3},{5,4},{6,5},{7,6},{8,7},{9,8},{10,9},{11,1... | collective-permute-start | bytes 276488 | tf_op jit(solution)/shard_map/ppermute | solution.py:19
  17.4 240.9 %collective-permute-start.1 = (f32[4,8,1,720]{3,1,2,0:T(8,128)}, f32[4,8,1,720]{3,1,2,0:T(8,128)}, u32[]{:S(2)}, u32[]{:S(2)}) collective-permute-start(f32[4,8,1,720]{3,1,2,0:T(8,128)} %get-tuple-element.22), channel_id=1, source_target_pairs={{0,1},{1,2},{2,3},{3,4},{4,5},{5,6},{6,7},{7,8},{8,9},{9,10},{10,1... | collective-permute-start | bytes 276488 | tf_op jit(solution)/shard_map/ppermute | solution.py:17
  256.0 2.3 copy-start.3
  256.0 2.3 copy-start.4
  257.5 1.8 copy-start.1
  257.5 2.5 copy-start.2
  257.7 2.9 copy-start
  265.5 30.1 %copy-start.5 = (bf16[3,8,24,720]{3,2,1,0:T(8,128)(2,1)S(1)}, bf16[3,8,24,720]{3,2,1,0:T(8,128)(2,1)}, u32[]{:S(2)}) copy-start(bf16[3,8,24,720]{3,2,1,0:T(8,128)(2,1)} %get-tuple-element.6) | copy-start | bytes 2488324
  266.7 30.0 %collective-permute-start.2 = (f32[4,8,1,720]{3,1,2,0:T(8,128)S(1)}, f32[4,8,1,720]{3,1,2,0:T(8,128)S(1)}, u32[]{:S(2)}, u32[]{:S(2)}) collective-permute-start(f32[4,8,1,720]{3,1,2,0:T(8,128)S(1)} %get-tuple-element.11), channel_id=1, source_target_pairs={{1,0},{2,1},{3,2},{4,3},{5,4},{6,5},{7,6},{8,7},{9,8},{10,9},{11,1... | collective-permute-start | bytes 276488 | tf_op jit(solution)/shard_map/ppermute | solution.py:19
  291.4 5.8 %collective-permute-start.3 = (f32[4,8,1,720]{3,1,2,0:T(8,128)S(1)}, f32[4,8,1,720]{3,1,2,0:T(8,128)S(1)}, u32[]{:S(2)}, u32[]{:S(2)}) collective-permute-start(f32[4,8,1,720]{3,1,2,0:T(8,128)S(1)} %get-tuple-element.12), channel_id=1, source_target_pairs={{0,1},{1,2},{2,3},{3,4},{4,5},{5,6},{6,7},{7,8},{8,9},{9,10},{10,1... | collective-permute-start | bytes 276488 | tf_op jit(solution)/shard_map/ppermute | solution.py:17
Sparse Core Ops, SparseCore 0:
  11.8 244.1 all-reduce.2
where the time goes:
time: 313 us; the launch traced here: 310 us
  waiting for transfers between devices  224 us (72%)
  starting transfers between devices  38.1 us (12%)
  local copies, waits for them, and re-layouts  19.8 us (6%)
  between operations  15 us (5%)
  other arithmetic  12.3 us (4%)
    psum x1, waiting for transfers between devices, spread(): return lax.psum(kept, axis)  224 us
    ppermute x2, starting transfers between devices, with_halo(): lax.ppermute(head, axis, [((i + 1) % count, i) for i in range(ends)])  27.3 us
    ppermute x2, starting transfers between devices, with_halo(): lax.ppermute(tail, axis, [(i, (i + 1) % count) for i in range(ends)])  10.7 us
    mul x2, other arithmetic, update_rows(): return ocean_mask * (center + change)  7.8 us
  transfers between devices with their start and end apart: 5, of which 2 were waited for; matrix products, arithmetic and copies ran while one was open for 5% of the time, Pallas kernels for 0%

commit v1 on v0

v1 whole, which is shorter than its diff:
```python
import jax
import jax.numpy as jnp
from jax import lax
from jax.experimental import pallas as pl
from jax.experimental.pallas import tpu as pltpu
from jax.sharding import PartitionSpec as P

LAST = 31
RING = 16
ROWS = 8


def lanes_next(x):
    return jnp.concatenate([x[..., 1:], x[..., :1]], axis=-1)


def lanes_prev(x):
    return jnp.concatenate([x[..., -1:], x[..., :-1]], axis=-1)


def advance(c, n, s, u, b, f0, f1, f2, mask):
    e, w = lanes_next(c), lanes_prev(c)
    diffuse = 0.06 + 0.015 * f0
    change = diffuse * (e + w + n + s - 4.0 * c)
    change = change - (0.15 * f1) * (e - w) - (0.15 * f2) * (n - s)
    change = change + 0.1 * (u + b - 2.0 * c)
    return mask * (c + change)


def steps_kernel(
    flag_ref, q_ref, south_ref, north_ref, mask_ref, mask_s_ref, mask_n_ref,
    edge_s_ref, edge_n_ref, *refs,
):
    chunks = len(refs[:-5]) // 2
    v_refs, w_refs = refs[:chunks], refs[chunks : 2 * chunks]
    out_ref, mid_ref, mid_s_ref, mid_n_ref, field_ref = refs[-5:]
    vecs, levs, rows, lon = q_ref.shape
    first_v = flag_ref[0] == 1
    row = lax.broadcasted_iota(jnp.int32, (rows, lon), 0)
    mask = mask_ref[...].astype(jnp.float32)

    def fields_of(level, hour):
        use_v = first_v if hour == 0 else jnp.logical_not(first_v)

        @pl.when(use_v)
        def _():
            for c in range(chunks):
                for k in range(3):
                    field_ref[k, c * ROWS : (c + 1) * ROWS] = v_refs[c][k, level].astype(jnp.float32)

        @pl.when(jnp.logical_not(use_v))
        def _():
            for c in range(chunks):
                for k in range(3):
                    field_ref[k, c * ROWS : (c + 1) * ROWS] = w_refs[c][k, level].astype(jnp.float32)

        return field_ref[0], field_ref[1], field_ref[2]

    def hour_of(src_ref, dst_ref, halo_s, halo_n, hour):
        def level_step(level, carry):
            f0, f1, f2 = fields_of(level, hour)
            up = jnp.maximum(level - 1, 0)
            low = jnp.minimum(level + 1, levs - 1)
            for v in range(vecs):
                c = src_ref[v, level]
                n = jnp.where(row == rows - 1, halo_n(v, level), pltpu.roll(c, rows - 1, 0))
                s = jnp.where(row == 0, halo_s(v, level), pltpu.roll(c, 1, 0))
                dst_ref[v, level] = advance(
                    c, n, s, src_ref[v, up], src_ref[v, low], f0, f1, f2, mask
                )
            return carry

        lax.fori_loop(0, levs, level_step, 0)

    lev = lax.broadcasted_iota(jnp.int32, (levs, lon), 0)

    def edge_rows(c, n, s, edge_ref, edge_mask_ref):
        u = jnp.where(lev == 0, c, pltpu.roll(c, 1, 0))
        b = jnp.where(lev == levs - 1, c, pltpu.roll(c, levs - 1, 0))
        f = [edge_ref[k].astype(jnp.float32) for k in range(3)]
        return advance(c, n, s, u, b, *f, edge_mask_ref[...].astype(jnp.float32))

    for v in range(vecs):
        first = jnp.concatenate([q_ref[v, z, 0:1] for z in range(levs)], axis=0)
        last = jnp.concatenate([q_ref[v, z, rows - 1 : rows] for z in range(levs)], axis=0)
        mid_s_ref[v] = edge_rows(south_ref[1, v], first, south_ref[0, v], edge_s_ref, mask_s_ref)
        mid_n_ref[v] = edge_rows(north_ref[0, v], north_ref[1, v], last, edge_n_ref, mask_n_ref)

    hour_of(
        q_ref, mid_ref,
        lambda v, z: south_ref[1, v, pl.ds(z, 1)],
        lambda v, z: north_ref[0, v, pl.ds(z, 1)],
        0,
    )
    hour_of(
        mid_ref, out_ref,
        lambda v, z: mid_s_ref[v, pl.ds(z, 1)],
        lambda v, z: mid_n_ref[v, pl.ds(z, 1)],
        1,
    )


def two_hours(flag, q, south, north, mask, mask_s, mask_n, edge_s, edge_n, vs, ws):
    vecs, levs, rows, lon = q.shape
    vmem = pl.BlockSpec(memory_space=pltpu.VMEM)
    args = [q, south, north, mask, mask_s, mask_n, edge_s, edge_n, *vs, *ws]
    return pl.pallas_call(
        steps_kernel,
        out_shape=jax.ShapeDtypeStruct(q.shape, jnp.float32),
        in_specs=[pl.BlockSpec(memory_space=pltpu.SMEM)] + [vmem] * len(args),
        out_specs=vmem,
        scratch_shapes=[
            pltpu.VMEM(q.shape, jnp.float32),
            pltpu.VMEM((vecs, levs, lon), jnp.float32),
            pltpu.VMEM((vecs, levs, lon), jnp.float32),
            pltpu.VMEM((3, rows, lon), jnp.float32),
        ],
        compiler_params=pltpu.CompilerParams(vmem_limit_bytes=40 * 1024 * 1024),
        name="two_hours",
    )(flag, *args)


TREE = (
    (((0, 4),), ((0, -4),)),
    (((4, 6), (-4, -6)), ((4, 2), (-4, -2))),
    (
        ((6, 7), (-6, -7), (2, 3), (-2, -3)),
        ((6, 5), (-6, -5), (2, 1), (-2, -1)),
        ((6, 8),),
    ),
)


def spread_from(other, hop, swap_edges):
    roots = (other % RING, LAST % RING)

    def pairs(moves):
        return [
            (x * RING + (roots[x] + a) % RING, x * RING + (roots[x] + b) % RING)
            for x in range(2)
            for a, b in moves
        ]

    swap = [(i, (i + RING) % (2 * RING)) for i in range(2 * RING)]

    def run(*chunks):
        vs, ws, tie = [], [], None
        for own in chunks:
            value = own if tie is None else own + tie
            if other >= RING:
                crossed = lax.ppermute(value, "vec", [(other, other - RING)])
                value = jnp.where(lax.axis_index("vec") == other - RING, crossed, value)
            for depth, level in enumerate(TREE):
                got = [lax.ppermute(value, "vec", pairs(moves)) for moves in level]
                if depth == 0:
                    tie = (got[0][0, 0, 0, 0] + got[1][0, 0, 0, 0]) * 0
                total = got[0]
                for more in got[1:]:
                    total = total + more
                value = jnp.where(hop <= depth, value, total)
            vs.append(value)
            ws.append(lax.ppermute(value, "vec", swap))
        return (*vs, *ws)

    return run


def shards(perturb, trajectory, hour_slot, sea_mask):
    lat = lax.axis_size("lat")
    me = lax.axis_index("vec")
    column, z = me // RING, me % RING
    other = hour_slot[0] + hour_slot[1] - LAST
    root = jnp.where(column == 1, LAST % RING, other % RING)
    away = (z - root) % RING
    away = jnp.minimum(away, RING - away)
    hop = jnp.where(away == 0, 0, jnp.where(away == 4, 1, jnp.where((away == 2) | (away == 6), 2, 3)))
    first_v = (hour_slot[0] == LAST) == (column == 1)

    northward = [(i, i + 1) for i in range(lat - 1)]
    southward = [(i + 1, i) for i in range(lat - 1)]

    def edge(rows):
        return jnp.moveaxis(rows, -2, 0)

    south = lax.ppermute(edge(perturb[:, :, -2:]), "lat", northward)
    north = lax.ppermute(edge(perturb[:, :, :2]), "lat", southward)
    ocean = sea_mask.astype(jnp.float32)
    mask_s = lax.ppermute(ocean[-1:], "lat", northward)
    mask_n = lax.ppermute(ocean[:1], "lat", southward)

    field = trajectory[0]
    rows = field.shape[2]
    chunks = [field[:, :, r : r + ROWS] for r in range(0, rows, ROWS)]
    spread = lax.switch(
        other,
        [spread_from(slot, hop, None) for slot in range(LAST)],
        *chunks,
    )
    vs, ws = spread[: len(chunks)], spread[len(chunks) :]
    lower = jnp.where(first_v, vs[0][:, :, 0], ws[0][:, :, 0])
    upper = jnp.where(first_v, vs[-1][:, :, -1], ws[-1][:, :, -1])
    edge_s = lax.ppermute(upper, "lat", northward)
    edge_n = lax.ppermute(lower, "lat", southward)
    return two_hours(
        first_v.astype(jnp.int32)[None],
        perturb, south, north, sea_mask, mask_s, mask_n, edge_s, edge_n, vs, ws,
    )


def solution(mesh):
    return jax.shard_map(
        shards,
        mesh=mesh,
        in_specs=(
            P("vec", None, "lat", None),
            P("vec", None, None, "lat", None),
            P(),
            P("lat", None),
        ),
        out_specs=P("vec", None, "lat", None),
        check_vma=False,
    )
```

time: 313 us -> 599 us (1.91)
  the two profiles are of different devices: /device:TPU:25 before, /device:TPU:1 now
where the time goes in v1:
time: 599 us; the launch traced here: 588 us
  starting transfers between devices  507 us (85%)
  loops' own time  26.3 us (4%)
  waiting for transfers between devices  14.9 us (2%)
  other arithmetic  14.5 us (2%)
  local copies, waits for them, and re-layouts  13.5 us (2%)
  Pallas kernels  9.18 us (2%)
    ppermute x21, starting transfers between devices, run(): got = [lax.ppermute(value, 'vec', pairs(moves)) for moves in level]  292 us
    ppermute x3, starting transfers between devices, run(): crossed = lax.ppermute(value, 'vec', [(other, other - RING)])  91.3 us
    another operation x1, loops' own time, shards(): lax.switch(other, [spread_from(slot, hop, None) for slot in range(LAST)],...  26.3 us
    ppermute x1, starting transfers between devices, shards(): south = lax.ppermute(edge(perturb[:, :, -2:]), 'lat', northward)  20.3 us
    ppermute x1, starting transfers between devices, shards(): edge_n = lax.ppermute(lower, 'lat', southward)  19.5 us
    ppermute x1, starting transfers between devices, shards(): north = lax.ppermute(edge(perturb[:, :, :2]), 'lat', southward)  19 us
    ppermute x1, starting transfers between devices, shards(): mask_n = lax.ppermute(ocean[:1], 'lat', southward)  19 us
    ppermute x1, starting transfers between devices, shards(): edge_s = lax.ppermute(upper, 'lat', northward)  19 us
  transfers between devices with their start and end apart: 33, of which 4 were waited for; matrix products, arithmetic and copies ran while one was open for 3% of the time, Pallas kernels for 0%

profile of v1, /device:TPU:1, one launch (start us, length us, event | category | flops | bytes accessed | tf_op | source)
XLA Modules:
  0.0 587.6 jit_solution(2727582555149083345)
XLA Ops:
  4.8 448.6 %conditional.1 = (bf16[3,8,8,720]{3,2,1,0:T(8,128)(2,1)}, bf16[3,8,8,720]{3,2,1,0:T(8,128)(2,1)}, bf16[3,8,8,720]{3,2,1,0:T(8,128)(2,1)}, bf16[3,8,8,720]{3,2,1,...) conditional(s32[]{:T(128)} %clamp.3, (s32[]{:T(128)}, ...), branch_computations={%region_0.1_spmd, %region_1.2_spmd, %region_2.3_spmd, %region_3.4_... | conditional | flops 3870741 | bytes 60827316 | solution.py:194
  15.7 21.8 %collective-permute-start.519 = (bf16[3,8,8,720]{3,2,1,0:T(8,128)(2,1)}, bf16[3,8,8,720]{3,2,1,0:T(8,128)(2,1)}, u32[]{:S(2)}, u32[]{:S(2)}) collective-permute-start(bf16[3,8,8,720]{3,2,1,0:T(8,128)(2,1)} %slice.1286), channel_id=1, source_target_pairs={{336,80},{337,81},{338,82},{339,83},{340,84},{341,85},{342,86},{34... | collective-permute-start | bytes 829448 | tf_op jit(solution)/shard_map/cond/branch_21_fun/ppermute | solution.py:151
  43.3 34.3 %collective-permute-start.527 = (bf16[3,8,8,720]{3,2,1,0:T(8,128)(2,1)S(1)}, bf16[3,8,8,720]{3,2,1,0:T(8,128)(2,1)S(1)}, u32[]{:S(2)}, u32[]{:S(2)}) collective-permute-start(bf16[3,8,8,720]{3,2,1,0:T(8,128)(2,1)S(1)} %slice_add_fusion.43), channel_id=1, source_target_pairs={{336,80},{337,81},{338,82},{339,83},{340,84},{341,85},{342,86},{34... | collective-permute-start | bytes 829448 | tf_op jit(solution)/shard_map/cond/branch_21_fun/ppermute | solution.py:151
  83.5 35.2 %collective-permute-start.535 = (bf16[3,8,8,720]{3,2,1,0:T(8,128)(2,1)}, bf16[3,8,8,720]{3,2,1,0:T(8,128)(2,1)}, u32[]{:S(2)}, u32[]{:S(2)}) collective-permute-start(bf16[3,8,8,720]{3,2,1,0:T(8,128)(2,1)} %slice_add_fusion.42), channel_id=1, source_target_pairs={{336,80},{337,81},{338,82},{339,83},{340,84},{341,85},{342,86},{34... | collective-permute-start | bytes 829448 | tf_op jit(solution)/shard_map/cond/branch_21_fun/ppermute | solution.py:151
  123.5 24.7 %collective-permute-start.523 = (bf16[3,8,8,720]{3,2,1,0:T(8,128)(2,1)S(1)}, bf16[3,8,8,720]{3,2,1,0:T(8,128)(2,1)S(1)}, u32[]{:S(2)}, u32[]{:S(2)}) collective-permute-start(bf16[3,8,8,720]{3,2,1,0:T(8,128)(2,1)S(1)} %add_select_fusion.197), channel_id=1, source_target_pairs={{144,112},{16,48},{304,272},{432,464},{145,113},{17,49},{305,273},... | collective-permute-start | bytes 829448 | tf_op jit(solution)/shard_map/cond/branch_21_fun/ppermute | solution.py:154
  148.2 19.1 %collective-permute-start.522 = (bf16[3,8,8,720]{3,2,1,0:T(8,128)(2,1)S(1)}, bf16[3,8,8,720]{3,2,1,0:T(8,128)(2,1)}, u32[]{:S(2)}, u32[]{:S(2)}) collective-permute-start(bf16[3,8,8,720]{3,2,1,0:T(8,128)(2,1)S(1)} %add_select_fusion.197), channel_id=1, source_target_pairs={{144,176},{16,240},{304,336},{432,400},{145,177},{17,241},{305,337... | collective-permute-start | bytes 829448 | tf_op jit(solution)/shard_map/cond/branch_21_fun/ppermute | solution.py:154
  168.4 18.4 %collective-permute-start.539 = (bf16[3,8,8,720]{3,2,1,0:T(8,128)(2,1)S(1)}, bf16[3,8,8,720]{3,2,1,0:T(8,128)(2,1)S(1)}, u32[]{:S(2)}, u32[]{:S(2)}) collective-permute-start(bf16[3,8,8,720]{3,2,1,0:T(8,128)(2,1)S(1)} %add_select_fusion.191), channel_id=1, source_target_pairs={{144,112},{16,48},{304,272},{432,464},{145,113},{17,49},{305,273},... | collective-permute-start | bytes 829448 | tf_op jit(solution)/shard_map/cond/branch_21_fun/ppermute | solution.py:154
  186.8 18.4 %collective-permute-start.538 = (bf16[3,8,8,720]{3,2,1,0:T(8,128)(2,1)S(1)}, bf16[3,8,8,720]{3,2,1,0:T(8,128)(2,1)S(1)}, u32[]{:S(2)}, u32[]{:S(2)}) collective-permute-start(bf16[3,8,8,720]{3,2,1,0:T(8,128)(2,1)S(1)} %add_select_fusion.191), channel_id=1, source_target_pairs={{144,176},{16,240},{304,336},{432,400},{145,177},{17,241},{305,337... | collective-permute-start | bytes 829448 | tf_op jit(solution)/shard_map/cond/branch_21_fun/ppermute | solution.py:154
  207.1 18.4 %collective-permute-start.526 = (bf16[3,8,8,720]{3,2,1,0:T(8,128)(2,1)S(1)}, bf16[3,8,8,720]{3,2,1,0:T(8,128)(2,1)S(1)}, u32[]{:S(2)}, u32[]{:S(2)}) collective-permute-start(bf16[3,8,8,720]{3,2,1,0:T(8,128)(2,1)S(1)} %add_select_fusion.196), channel_id=1, source_target_pairs={{176,208},{336,368},{177,209},{337,369},{178,210},{338,370},{179,2... | collective-permute-start | bytes 829448 | tf_op jit(solution)/shard_map/cond/branch_21_fun/ppermute | solution.py:154
  225.6 19.1 %collective-permute-start.531 = (bf16[3,8,8,720]{3,2,1,0:T(8,128)(2,1)S(1)}, bf16[3,8,8,720]{3,2,1,0:T(8,128)(2,1)}, u32[]{:S(2)}, u32[]{:S(2)}) collective-permute-start(bf16[3,8,8,720]{3,2,1,0:T(8,128)(2,1)S(1)} %add_select_fusion.194), channel_id=1, source_target_pairs={{144,112},{16,48},{304,272},{432,464},{145,113},{17,49},{305,273},... | collective-permute-start | bytes 829448 | tf_op jit(solution)/shard_map/cond/branch_21_fun/ppermute | solution.py:154
  244.7 19.1 %collective-permute-start.530 = (bf16[3,8,8,720]{3,2,1,0:T(8,128)(2,1)S(1)}, bf16[3,8,8,720]{3,2,1,0:T(8,128)(2,1)}, u32[]{:S(2)}, u32[]{:S(2)}) collective-permute-start(bf16[3,8,8,720]{3,2,1,0:T(8,128)(2,1)S(1)} %add_select_fusion.194), channel_id=1, source_target_pairs={{144,176},{16,240},{304,336},{432,400},{145,177},{17,241},{305,337... | collective-permute-start | bytes 829448 | tf_op jit(solution)/shard_map/cond/branch_21_fun/ppermute | solution.py:154
  263.8 18.4 %collective-permute-start.525 = (bf16[3,8,8,720]{3,2,1,0:T(8,128)(2,1)S(1)}, bf16[3,8,8,720]{3,2,1,0:T(8,128)(2,1)}, u32[]{:S(2)}, u32[]{:S(2)}) collective-permute-start(bf16[3,8,8,720]{3,2,1,0:T(8,128)(2,1)S(1)} %add_select_fusion.196), channel_id=1, source_target_pairs={{176,160},{240,0},{112,96},{48,64},{336,320},{400,416},{272,256},{... | collective-permute-start | bytes 829448 | tf_op jit(solution)/shard_map/cond/branch_21_fun/ppermute | solution.py:154
  282.1 19.8 %collective-permute-start.524 = (bf16[3,8,8,720]{3,2,1,0:T(8,128)(2,1)S(1)}, bf16[3,8,8,720]{3,2,1,0:T(8,128)(2,1)}, u32[]{:S(2)}, u32[]{:S(2)}) collective-permute-start(bf16[3,8,8,720]{3,2,1,0:T(8,128)(2,1)S(1)} %add_select_fusion.196), channel_id=1, source_target_pairs={{176,192},{240,224},{112,128},{48,32},{336,352},{400,384},{272,288... | collective-permute-start | bytes 829448 | tf_op jit(solution)/shard_map/cond/branch_21_fun/ppermute | solution.py:154
  302.7 18.8 %collective-permute-start.542 = (bf16[3,8,8,720]{3,2,1,0:T(8,128)(2,1)S(1)}, bf16[3,8,8,720]{3,2,1,0:T(8,128)(2,1)}, u32[]{:S(2)}, u32[]{:S(2)}) collective-permute-start(bf16[3,8,8,720]{3,2,1,0:T(8,128)(2,1)S(1)} %add_select_fusion.190), channel_id=1, source_target_pairs={{176,208},{336,368},{177,209},{337,369},{178,210},{338,370},{179,2... | collective-permute-start | bytes 829448 | tf_op jit(solution)/shard_map/cond/branch_21_fun/ppermute | solution.py:154
  321.6 18.4 %collective-permute-start.541 = (bf16[3,8,8,720]{3,2,1,0:T(8,128)(2,1)S(1)}, bf16[3,8,8,720]{3,2,1,0:T(8,128)(2,1)S(1)}, u32[]{:S(2)}, u32[]{:S(2)}) collective-permute-start(bf16[3,8,8,720]{3,2,1,0:T(8,128)(2,1)S(1)} %add_select_fusion.190), channel_id=1, source_target_pairs={{176,160},{240,0},{112,96},{48,64},{336,320},{400,416},{272,256},{... | collective-permute-start | bytes 829448 | tf_op jit(solution)/shard_map/cond/branch_21_fun/ppermute | solution.py:154
  339.9 18.4 %collective-permute-start.540 = (bf16[3,8,8,720]{3,2,1,0:T(8,128)(2,1)S(1)}, bf16[3,8,8,720]{3,2,1,0:T(8,128)(2,1)S(1)}, u32[]{:S(2)}, u32[]{:S(2)}) collective-permute-start(bf16[3,8,8,720]{3,2,1,0:T(8,128)(2,1)S(1)} %add_select_fusion.190), channel_id=1, source_target_pairs={{176,192},{240,224},{112,128},{48,32},{336,352},{400,384},{272,288... | collective-permute-start | bytes 829448 | tf_op jit(solution)/shard_map/cond/branch_21_fun/ppermute | solution.py:154
  359.5 18.4 %collective-permute-start.534 = (bf16[3,8,8,720]{3,2,1,0:T(8,128)(2,1)S(1)}, bf16[3,8,8,720]{3,2,1,0:T(8,128)(2,1)S(1)}, u32[]{:S(2)}, u32[]{:S(2)}) collective-permute-start(bf16[3,8,8,720]{3,2,1,0:T(8,128)(2,1)S(1)} %add_select_fusion.193), channel_id=1, source_target_pairs={{176,208},{336,368},{177,209},{337,369},{178,210},{338,370},{179,2... | collective-permute-start | bytes 829448 | tf_op jit(solution)/shard_map/cond/branch_21_fun/ppermute | solution.py:154
  377.8 18.4 %collective-permute-start.533 = (bf16[3,8,8,720]{3,2,1,0:T(8,128)(2,1)S(1)}, bf16[3,8,8,720]{3,2,1,0:T(8,128)(2,1)S(1)}, u32[]{:S(2)}, u32[]{:S(2)}) collective-permute-start(bf16[3,8,8,720]{3,2,1,0:T(8,128)(2,1)S(1)} %add_select_fusion.193), channel_id=1, source_target_pairs={{176,160},{240,0},{112,96},{48,64},{336,320},{400,416},{272,256},{... | collective-permute-start | bytes 829448 | tf_op jit(solution)/shard_map/cond/branch_21_fun/ppermute | solution.py:154
  396.2 18.4 %collective-permute-start.532 = (bf16[3,8,8,720]{3,2,1,0:T(8,128)(2,1)S(1)}, bf16[3,8,8,720]{3,2,1,0:T(8,128)(2,1)S(1)}, u32[]{:S(2)}, u32[]{:S(2)}) collective-permute-start(bf16[3,8,8,720]{3,2,1,0:T(8,128)(2,1)S(1)} %add_select_fusion.193), channel_id=1, source_target_pairs={{176,192},{240,224},{112,128},{48,32},{336,352},{400,384},{272,288... | collective-permute-start | bytes 829448 | tf_op jit(solution)/shard_map/cond/branch_21_fun/ppermute | solution.py:154
  453.5 20.3 %collective-permute-start.789 = (f32[2,4,8,720]{3,2,1,0:T(8,128)}, f32[2,4,8,720]{3,2,1,0:T(8,128)S(1)}, u32[]{:S(2)}, u32[]{:S(2)}) collective-permute-start(f32[2,4,8,720]{3,2,1,0:T(8,128)} %bitcast.628), channel_id=1, source_target_pairs={{0,1},{1,2},{2,3},{3,4},{4,5},{5,6},{6,7},{7,8},{8,9},{9,10},{10,1... | collective-permute-start | bytes 552968 | tf_op jit(solution)/shard_map/ppermute | solution.py:185
  473.8 19.0 %collective-permute-start.790 = (f32[2,4,8,720]{3,2,1,0:T(8,128)S(1)}, f32[2,4,8,720]{3,2,1,0:T(8,128)S(1)}, u32[]{:S(2)}, u32[]{:S(2)}) collective-permute-start(f32[2,4,8,720]{3,2,1,0:T(8,128)S(1)} %bitcast.629), channel_id=1, source_target_pairs={{1,0},{2,1},{3,2},{4,3},{5,4},{6,5},{7,6},{8,7},{9,8},{10,9},{11,1... | collective-permute-start | bytes 552968 | tf_op jit(solution)/shard_map/ppermute | solution.py:186
  493.5 19.5 %collective-permute-start.794 = (bf16[3,8,720]{2,1,0:T(8,128)(2,1)S(1)}, bf16[3,8,720]{2,1,0:T(8,128)(2,1)S(1)}, u32[]{:S(2)}, u32[]{:S(2)}) collective-permute-start(bf16[3,8,720]{2,1,0:T(8,128)(2,1)S(1)} %broadcast_select_fusion.45), channel_id=1, source_target_pairs={{1,0},{2,1},{3,2},{4,3},{5,4},{6,5},{7,6},{8,7},{9,8},{10,9},{11,1... | collective-permute-start | bytes 103688 | tf_op jit(solution)/shard_map/ppermute | solution.py:203
  513.7 19.0 %collective-permute-start.793 = (bf16[3,8,720]{2,1,0:T(8,128)(2,1)S(1)}, bf16[3,8,720]{2,1,0:T(8,128)(2,1)S(1)}, u32[]{:S(2)}, u32[]{:S(2)}) collective-permute-start(bf16[3,8,720]{2,1,0:T(8,128)(2,1)S(1)} %broadcast_select_fusion.46), channel_id=1, source_target_pairs={{0,1},{1,2},{2,3},{3,4},{4,5},{5,6},{6,7},{7,8},{8,9},{9,10},{10,1... | collective-permute-start | bytes 103688 | tf_op jit(solution)/shard_map/ppermute | solution.py:202
  532.8 19.0 %collective-permute-start.792 = (f32[1,720]{1,0:T(1,128)S(1)}, f32[1,720]{1,0:T(1,128)S(1)}, u32[]{:S(2)}, u32[]{:S(2)}) collective-permute-start(f32[1,720]{1,0:T(1,128)S(1)} %get-tuple-element.1148), channel_id=1, source_target_pairs={{1,0},{2,1},{3,2},{4,3},{5,4},{6,5},{7,6},{8,7},{9,8},{10,9},{11,1... | collective-permute-start | bytes 8648 | tf_op jit(solution)/shard_map/ppermute | solution.py:189
  (113 shorter events, 84.6 us)
Async XLA Ops:
  43.3 34.3 %collective-permute-start.527 = (bf16[3,8,8,720]{3,2,1,0:T(8,128)(2,1)S(1)}, bf16[3,8,8,720]{3,2,1,0:T(8,128)(2,1)S(1)}, u32[]{:S(2)}, u32[]{:S(2)}) collective-permute-start(bf16[3,8,8,720]{3,2,1,0:T(8,128)(2,1)S(1)} %slice_add_fusion.43), channel_id=1, source_target_pairs={{336,80},{337,81},{338,82},{339,83},{340,84},{341,85},{342,86},{34... | collective-permute-start | bytes 829448 | tf_op jit(solution)/shard_map/cond/branch_21_fun/ppermute | solution.py:151
  83.5 35.2 %collective-permute-start.535 = (bf16[3,8,8,720]{3,2,1,0:T(8,128)(2,1)}, bf16[3,8,8,720]{3,2,1,0:T(8,128)(2,1)}, u32[]{:S(2)}, u32[]{:S(2)}) collective-permute-start(bf16[3,8,8,720]{3,2,1,0:T(8,128)(2,1)} %slice_add_fusion.42), channel_id=1, source_target_pairs={{336,80},{337,81},{338,82},{339,83},{340,84},{341,85},{342,86},{34... | collective-permute-start | bytes 829448 | tf_op jit(solution)/shard_map/cond/branch_21_fun/ppermute | solution.py:151
  119.5 47.8 %collective-permute-start.537 = (bf16[3,8,8,720]{3,2,1,0:T(8,128)(2,1)}, bf16[3,8,8,720]{3,2,1,0:T(8,128)(2,1)}, u32[]{:S(2)}, u32[]{:S(2)}) collective-permute-start(bf16[3,8,8,720]{3,2,1,0:T(8,128)(2,1)} %broadcast_select_fusion.15), channel_id=1, source_target_pairs={{80,16},{496,432},{81,17},{497,433},{82,18},{498,434},{83,19},{499... | collective-permute-start | bytes 829448 | tf_op jit(solution)/shard_map/cond/branch_21_fun/ppermute | solution.py:154
  121.0 46.3 %collective-permute-start.536 = (bf16[3,8,8,720]{3,2,1,0:T(8,128)(2,1)}, bf16[3,8,8,720]{3,2,1,0:T(8,128)(2,1)}, u32[]{:S(2)}, u32[]{:S(2)}) collective-permute-start(bf16[3,8,8,720]{3,2,1,0:T(8,128)(2,1)} %broadcast_select_fusion.15), channel_id=1, source_target_pairs={{80,144},{496,304},{81,145},{497,305},{82,146},{498,306},{83,147},... | collective-permute-start | bytes 829448 | tf_op jit(solution)/shard_map/cond/branch_21_fun/ppermute | solution.py:154
  123.5 81.8 %collective-permute-start.523 = (bf16[3,8,8,720]{3,2,1,0:T(8,128)(2,1)S(1)}, bf16[3,8,8,720]{3,2,1,0:T(8,128)(2,1)S(1)}, u32[]{:S(2)}, u32[]{:S(2)}) collective-permute-start(bf16[3,8,8,720]{3,2,1,0:T(8,128)(2,1)S(1)} %add_select_fusion.197), channel_id=1, source_target_pairs={{144,112},{16,48},{304,272},{432,464},{145,113},{17,49},{305,273},... | collective-permute-start | bytes 829448 | tf_op jit(solution)/shard_map/cond/branch_21_fun/ppermute | solution.py:154
  148.2 57.8 %collective-permute-start.522 = (bf16[3,8,8,720]{3,2,1,0:T(8,128)(2,1)S(1)}, bf16[3,8,8,720]{3,2,1,0:T(8,128)(2,1)}, u32[]{:S(2)}, u32[]{:S(2)}) collective-permute-start(bf16[3,8,8,720]{3,2,1,0:T(8,128)(2,1)S(1)} %add_select_fusion.197), channel_id=1, source_target_pairs={{144,176},{16,240},{304,336},{432,400},{145,177},{17,241},{305,337... | collective-permute-start | bytes 829448 | tf_op jit(solution)/shard_map/cond/branch_21_fun/ppermute | solution.py:154
  168.4 95.3 %collective-permute-start.539 = (bf16[3,8,8,720]{3,2,1,0:T(8,128)(2,1)S(1)}, bf16[3,8,8,720]{3,2,1,0:T(8,128)(2,1)S(1)}, u32[]{:S(2)}, u32[]{:S(2)}) collective-permute-start(bf16[3,8,8,720]{3,2,1,0:T(8,128)(2,1)S(1)} %add_select_fusion.191), channel_id=1, source_target_pairs={{144,112},{16,48},{304,272},{432,464},{145,113},{17,49},{305,273},... | collective-permute-start | bytes 829448 | tf_op jit(solution)/shard_map/cond/branch_21_fun/ppermute | solution.py:154
  186.8 95.3 %collective-permute-start.538 = (bf16[3,8,8,720]{3,2,1,0:T(8,128)(2,1)S(1)}, bf16[3,8,8,720]{3,2,1,0:T(8,128)(2,1)S(1)}, u32[]{:S(2)}, u32[]{:S(2)}) collective-permute-start(bf16[3,8,8,720]{3,2,1,0:T(8,128)(2,1)S(1)} %add_select_fusion.191), channel_id=1, source_target_pairs={{144,176},{16,240},{304,336},{432,400},{145,177},{17,241},{305,337... | collective-permute-start | bytes 829448 | tf_op jit(solution)/shard_map/cond/branch_21_fun/ppermute | solution.py:154
  207.1 94.9 %collective-permute-start.526 = (bf16[3,8,8,720]{3,2,1,0:T(8,128)(2,1)S(1)}, bf16[3,8,8,720]{3,2,1,0:T(8,128)(2,1)S(1)}, u32[]{:S(2)}, u32[]{:S(2)}) collective-permute-start(bf16[3,8,8,720]{3,2,1,0:T(8,128)(2,1)S(1)} %add_select_fusion.196), channel_id=1, source_target_pairs={{176,208},{336,368},{177,209},{337,369},{178,210},{338,370},{179,2... | collective-permute-start | bytes 829448 | tf_op jit(solution)/shard_map/cond/branch_21_fun/ppermute | solution.py:154
  225.6 96.0 %collective-permute-start.531 = (bf16[3,8,8,720]{3,2,1,0:T(8,128)(2,1)S(1)}, bf16[3,8,8,720]{3,2,1,0:T(8,128)(2,1)}, u32[]{:S(2)}, u32[]{:S(2)}) collective-permute-start(bf16[3,8,8,720]{3,2,1,0:T(8,128)(2,1)S(1)} %add_select_fusion.194), channel_id=1, source_target_pairs={{144,112},{16,48},{304,272},{432,464},{145,113},{17,49},{305,273},... | collective-permute-start | bytes 829448 | tf_op jit(solution)/shard_map/cond/branch_21_fun/ppermute | solution.py:154
  244.7 95.2 %collective-permute-start.530 = (bf16[3,8,8,720]{3,2,1,0:T(8,128)(2,1)S(1)}, bf16[3,8,8,720]{3,2,1,0:T(8,128)(2,1)}, u32[]{:S(2)}, u32[]{:S(2)}) collective-permute-start(bf16[3,8,8,720]{3,2,1,0:T(8,128)(2,1)S(1)} %add_select_fusion.194), channel_id=1, source_target_pairs={{144,176},{16,240},{304,336},{432,400},{145,177},{17,241},{305,337... | collective-permute-start | bytes 829448 | tf_op jit(solution)/shard_map/cond/branch_21_fun/ppermute | solution.py:154
  263.8 95.7 %collective-permute-start.525 = (bf16[3,8,8,720]{3,2,1,0:T(8,128)(2,1)S(1)}, bf16[3,8,8,720]{3,2,1,0:T(8,128)(2,1)}, u32[]{:S(2)}, u32[]{:S(2)}) collective-permute-start(bf16[3,8,8,720]{3,2,1,0:T(8,128)(2,1)S(1)} %add_select_fusion.196), channel_id=1, source_target_pairs={{176,160},{240,0},{112,96},{48,64},{336,320},{400,416},{272,256},{... | collective-permute-start | bytes 829448 | tf_op jit(solution)/shard_map/cond/branch_21_fun/ppermute | solution.py:154
  282.1 95.7 %collective-permute-start.524 = (bf16[3,8,8,720]{3,2,1,0:T(8,128)(2,1)S(1)}, bf16[3,8,8,720]{3,2,1,0:T(8,128)(2,1)}, u32[]{:S(2)}, u32[]{:S(2)}) collective-permute-start(bf16[3,8,8,720]{3,2,1,0:T(8,128)(2,1)S(1)} %add_select_fusion.196), channel_id=1, source_target_pairs={{176,192},{240,224},{112,128},{48,32},{336,352},{400,384},{272,288... | collective-permute-start | bytes 829448 | tf_op jit(solution)/shard_map/cond/branch_21_fun/ppermute | solution.py:154
  302.7 93.5 %collective-permute-start.542 = (bf16[3,8,8,720]{3,2,1,0:T(8,128)(2,1)S(1)}, bf16[3,8,8,720]{3,2,1,0:T(8,128)(2,1)}, u32[]{:S(2)}, u32[]{:S(2)}) collective-permute-start(bf16[3,8,8,720]{3,2,1,0:T(8,128)(2,1)S(1)} %add_select_fusion.190), channel_id=1, source_target_pairs={{176,208},{336,368},{177,209},{337,369},{178,210},{338,370},{179,2... | collective-permute-start | bytes 829448 | tf_op jit(solution)/shard_map/cond/branch_21_fun/ppermute | solution.py:154
  321.6 95.0 %collective-permute-start.541 = (bf16[3,8,8,720]{3,2,1,0:T(8,128)(2,1)S(1)}, bf16[3,8,8,720]{3,2,1,0:T(8,128)(2,1)S(1)}, u32[]{:S(2)}, u32[]{:S(2)}) collective-permute-start(bf16[3,8,8,720]{3,2,1,0:T(8,128)(2,1)S(1)} %add_select_fusion.190), channel_id=1, source_target_pairs={{176,160},{240,0},{112,96},{48,64},{336,320},{400,416},{272,256},{... | collective-permute-start | bytes 829448 | tf_op jit(solution)/shard_map/cond/branch_21_fun/ppermute | solution.py:154
  339.9 80.0 %collective-permute-start.540 = (bf16[3,8,8,720]{3,2,1,0:T(8,128)(2,1)S(1)}, bf16[3,8,8,720]{3,2,1,0:T(8,128)(2,1)S(1)}, u32[]{:S(2)}, u32[]{:S(2)}) collective-permute-start(bf16[3,8,8,720]{3,2,1,0:T(8,128)(2,1)S(1)} %add_select_fusion.190), channel_id=1, source_target_pairs={{176,192},{240,224},{112,128},{48,32},{336,352},{400,384},{272,288... | collective-permute-start | bytes 829448 | tf_op jit(solution)/shard_map/cond/branch_21_fun/ppermute | solution.py:154
  359.5 64.2 %collective-permute-start.534 = (bf16[3,8,8,720]{3,2,1,0:T(8,128)(2,1)S(1)}, bf16[3,8,8,720]{3,2,1,0:T(8,128)(2,1)S(1)}, u32[]{:S(2)}, u32[]{:S(2)}) collective-permute-start(bf16[3,8,8,720]{3,2,1,0:T(8,128)(2,1)S(1)} %add_select_fusion.193), channel_id=1, source_target_pairs={{176,208},{336,368},{177,209},{337,369},{178,210},{338,370},{179,2... | collective-permute-start | bytes 829448 | tf_op jit(solution)/shard_map/cond/branch_21_fun/ppermute | solution.py:154
  377.8 45.8 %collective-permute-start.533 = (bf16[3,8,8,720]{3,2,1,0:T(8,128)(2,1)S(1)}, bf16[3,8,8,720]{3,2,1,0:T(8,128)(2,1)S(1)}, u32[]{:S(2)}, u32[]{:S(2)}) collective-permute-start(bf16[3,8,8,720]{3,2,1,0:T(8,128)(2,1)S(1)} %add_select_fusion.193), channel_id=1, source_target_pairs={{176,160},{240,0},{112,96},{48,64},{336,320},{400,416},{272,256},{... | collective-permute-start | bytes 829448 | tf_op jit(solution)/shard_map/cond/branch_21_fun/ppermute | solution.py:154
  396.2 27.5 %collective-permute-start.532 = (bf16[3,8,8,720]{3,2,1,0:T(8,128)(2,1)S(1)}, bf16[3,8,8,720]{3,2,1,0:T(8,128)(2,1)S(1)}, u32[]{:S(2)}, u32[]{:S(2)}) collective-permute-start(bf16[3,8,8,720]{3,2,1,0:T(8,128)(2,1)S(1)} %add_select_fusion.193), channel_id=1, source_target_pairs={{176,192},{240,224},{112,128},{48,32},{336,352},{400,384},{272,288... | collective-permute-start | bytes 829448 | tf_op jit(solution)/shard_map/cond/branch_21_fun/ppermute | solution.py:154
  453.5 124.3 %collective-permute-start.789 = (f32[2,4,8,720]{3,2,1,0:T(8,128)}, f32[2,4,8,720]{3,2,1,0:T(8,128)S(1)}, u32[]{:S(2)}, u32[]{:S(2)}) collective-permute-start(f32[2,4,8,720]{3,2,1,0:T(8,128)} %bitcast.628), channel_id=1, source_target_pairs={{0,1},{1,2},{2,3},{3,4},{4,5},{5,6},{6,7},{7,8},{8,9},{9,10},{10,1... | collective-permute-start | bytes 552968 | tf_op jit(solution)/shard_map/ppermute | solution.py:185
  473.8 104.0 %collective-permute-start.790 = (f32[2,4,8,720]{3,2,1,0:T(8,128)S(1)}, f32[2,4,8,720]{3,2,1,0:T(8,128)S(1)}, u32[]{:S(2)}, u32[]{:S(2)}) collective-permute-start(f32[2,4,8,720]{3,2,1,0:T(8,128)S(1)} %bitcast.629), channel_id=1, source_target_pairs={{1,0},{2,1},{3,2},{4,3},{5,4},{6,5},{7,6},{8,7},{9,8},{10,9},{11,1... | collective-permute-start | bytes 552968 | tf_op jit(solution)/shard_map/ppermute | solution.py:186
  493.5 84.3 %collective-permute-start.794 = (bf16[3,8,720]{2,1,0:T(8,128)(2,1)S(1)}, bf16[3,8,720]{2,1,0:T(8,128)(2,1)S(1)}, u32[]{:S(2)}, u32[]{:S(2)}) collective-permute-start(bf16[3,8,720]{2,1,0:T(8,128)(2,1)S(1)} %broadcast_select_fusion.45), channel_id=1, source_target_pairs={{1,0},{2,1},{3,2},{4,3},{5,4},{6,5},{7,6},{8,7},{9,8},{10,9},{11,1... | collective-permute-start | bytes 103688 | tf_op jit(solution)/shard_map/ppermute | solution.py:203
  513.7 64.1 %collective-permute-start.793 = (bf16[3,8,720]{2,1,0:T(8,128)(2,1)S(1)}, bf16[3,8,720]{2,1,0:T(8,128)(2,1)S(1)}, u32[]{:S(2)}, u32[]{:S(2)}) collective-permute-start(bf16[3,8,720]{2,1,0:T(8,128)(2,1)S(1)} %broadcast_select_fusion.46), channel_id=1, source_target_pairs={{0,1},{1,2},{2,3},{3,4},{4,5},{5,6},{6,7},{7,8},{8,9},{9,10},{10,1... | collective-permute-start | bytes 103688 | tf_op jit(solution)/shard_map/ppermute | solution.py:202
  554.7 23.1 %collective-permute-start.791 = (f32[1,720]{1,0:T(1,128)S(1)}, f32[1,720]{1,0:T(1,128)S(1)}, u32[]{:S(2)}, u32[]{:S(2)}) collective-permute-start(f32[1,720]{1,0:T(1,128)S(1)} %get-tuple-element.1149), channel_id=1, source_target_pairs={{0,1},{1,2},{2,3},{3,4},{4,5},{5,6},{6,7},{7,8},{8,9},{9,10},{10,1... | collective-permute-start | bytes 8648 | tf_op jit(solution)/shard_map/ppermute | solution.py:188
  (26 other events, 1607.2 us)

commit v2 on v0

v2 whole, which is shorter than its diff:
```python
import jax
import jax.numpy as jnp
from jax import lax
from jax.experimental import pallas as pl
from jax.experimental.pallas import tpu as pltpu
from jax.sharding import PartitionSpec as P

COLUMNS = 2
RING = 16
LANES = 128
FIELDS = 3
CUT = 40
PIECE = 112
VMEM_LIMIT = 48 * 1024 * 1024


def tile_parts(rows, half):
    total = FIELDS * rows
    base = 3 * half
    return (
        (base, 0, total, 0, 0),
        (base + 1, 0, CUT, 0, total),
        (base + 1, CUT, total, 1, 0),
        (base + 2, 0, total, 1, total - CUT),
    )


def field_parts(rows, half):
    parts = []
    for tile, start, stop, column, at in tile_parts(rows, half):
        for k in range(FIELDS):
            lo, hi = max(start, k * rows), min(stop, (k + 1) * rows)
            if lo < hi:
                parts.append((k, tile, lo - k * rows, hi - k * rows, column, at + lo - start))
    return parts


def pack_kernel(field_ref, piece_ref):
    _, levs, rows, lon = field_ref.shape[1:]
    for level in range(levs):
        for half in range(2):
            for k, tile, lo, hi, column, at in field_parts(rows, half):
                p = column * RING + level * 2 + half
                left, right = tile * LANES, min((tile + 1) * LANES, lon)
                piece_ref[p, at : at + hi - lo, : right - left] = field_ref[0, k, level, lo:hi, left:right]


def pack(trajectory):
    return pl.pallas_call(
        pack_kernel,
        out_shape=jax.ShapeDtypeStruct((COLUMNS * RING, PIECE, LANES), trajectory.dtype),
        in_specs=[pl.BlockSpec(memory_space=pltpu.VMEM)],
        out_specs=pl.BlockSpec(memory_space=pltpu.VMEM),
        compiler_params=pltpu.CompilerParams(vmem_limit_bytes=VMEM_LIMIT),
        name="pack",
    )(trajectory)


def lanes_next(x):
    return jnp.concatenate([x[..., 1:], x[..., :1]], axis=-1)


def lanes_prev(x):
    return jnp.concatenate([x[..., -1:], x[..., :-1]], axis=-1)


def advance(c, n, s, u, b, f0, f1, f2, mask):
    e, w = lanes_next(c), lanes_prev(c)
    diffuse = 0.06 + 0.015 * f0
    change = diffuse * (e + w + n + s - 4.0 * c)
    change = change - (0.15 * f1) * (e - w) - (0.15 * f2) * (n - s)
    change = change + 0.1 * (u + b - 2.0 * c)
    return mask * (c + change)


def hour_kernel(
    column_ref, q_ref, south_ref, north_ref, mask_ref, own_ref, other_ref,
    out_ref, first_ref, last_ref, field_ref,
):
    vecs, levs, rows, lon = q_ref.shape
    row = lax.broadcasted_iota(jnp.int32, (rows, lon), 0)
    mask = mask_ref[...].astype(jnp.float32)
    own_column = column_ref[0]

    def level_step(level, carry):
        for own in range(COLUMNS):

            @pl.when(own_column == own)
            def _():
                for half in range(2):
                    for k, tile, lo, hi, column, at in field_parts(rows, half):
                        piece_ref = own_ref if column == own else other_ref
                        field_ref[k, lo:hi, tile * LANES : (tile + 1) * LANES] = piece_ref[
                            level * 2 + half, at : at + hi - lo
                        ].astype(jnp.float32)

        f0, f1, f2 = (field_ref[k, :, :lon] for k in range(FIELDS))
        up = jnp.maximum(level - 1, 0)
        low = jnp.minimum(level + 1, levs - 1)
        for v in range(vecs):
            c = q_ref[v, level]
            n = jnp.where(row == rows - 1, north_ref[v, pl.ds(level, 1)], pltpu.roll(c, rows - 1, 0))
            s = jnp.where(row == 0, south_ref[v, pl.ds(level, 1)], pltpu.roll(c, 1, 0))
            new = advance(c, n, s, q_ref[v, up], q_ref[v, low], f0, f1, f2, mask)
            out_ref[v, level] = new
            first_ref[v, pl.ds(level, 1)] = new[:1]
            last_ref[v, pl.ds(level, 1)] = new[rows - 1 :]
        return carry

    lax.fori_loop(0, levs, level_step, 0)


def one_hour(column, q, south, north, mask, own, other):
    vecs, levs, rows, lon = q.shape
    vmem = pl.BlockSpec(memory_space=pltpu.VMEM)
    edge = jax.ShapeDtypeStruct((vecs, levs, lon), jnp.float32)
    return pl.pallas_call(
        hour_kernel,
        out_shape=(jax.ShapeDtypeStruct(q.shape, jnp.float32), edge, edge),
        in_specs=[pl.BlockSpec(memory_space=pltpu.SMEM)] + [vmem] * 6,
        out_specs=(vmem, vmem, vmem),
        scratch_shapes=[pltpu.VMEM((FIELDS, rows, 6 * LANES), jnp.float32)],
        compiler_params=pltpu.CompilerParams(vmem_limit_bytes=VMEM_LIMIT),
        cost_estimate=pl.CostEstimate(flops=25 * q.size, bytes_accessed=8 * q.size, transcendentals=0),
        name="one_hour",
    )(column, q, south, north, mask, own, other)


def shards(perturb, trajectory, hour_slot, sea_mask):
    lat = lax.axis_size("lat")
    column = lax.axis_index("vec") // RING
    northward = [(i, i + 1) for i in range(lat - 1)]
    southward = [(i + 1, i) for i in range(lat - 1)]
    rings = [[c * RING + z for z in range(RING)] for c in range(COLUMNS)]
    swap = [(i, (i + RING) % (COLUMNS * RING)) for i in range(COLUMNS * RING)]

    def halos(first, last):
        return lax.ppermute(last, "lat", northward), lax.ppermute(first, "lat", southward)

    pieces = lax.all_to_all(pack(trajectory), "vec", 0, 0, tiled=True)
    picked = jnp.stack([lax.dynamic_index_in_dim(pieces, hour_slot[h], 0, keepdims=False) for h in range(2)])
    gathered = lax.all_gather(picked, "vec", axis=0, axis_index_groups=rings)
    own = [gathered[:, h] for h in range(2)]
    other = [lax.ppermute(half, "vec", swap) for half in own]

    q = perturb
    first, last = q[:, :, 0], q[:, :, -1]
    which = column.astype(jnp.int32)[None]
    for h in range(2):
        south, north = halos(first, last)
        q, first, last = one_hour(which, q, south, north, sea_mask, own[h], other[h])
    return q


def solution(mesh):
    return jax.shard_map(
        shards,
        mesh=mesh,
        in_specs=(
            P("vec", None, "lat", None),
            P("vec", None, None, "lat", None),
            P(),
            P("lat", None),
        ),
        out_specs=P("vec", None, "lat", None),
        check_vma=False,
    )
```

time: 313 us -> 144 us (0.46); the launches traced: 310 us -> 144 us
  waiting for transfers between devices: 224 us -> 55.2 us
  blocking collectives: 0 us -> 29.9 us
  local copies, waits for them, and re-layouts: 19.8 us -> 3.34 us
  other arithmetic: 12.3 us -> 0.01 us
  between operations: 15 us -> 3.84 us
  Pallas kernels: 0 us -> 10.8 us
    psum x1 -> x0, waiting for transfers between devices: 224 us -> none  [spread(): return lax.psum(kept, axis)]
    all_to_all x0 -> x1, waiting for transfers between devices: none -> 40.3 us  [shards(): pieces = lax.all_to_all(pack(trajectory), 'vec', 0, 0, tiled=True)]
    all_gather x0 -> x1, blocking collectives: none -> 29.9 us  [shards(): gathered = lax.all_gather(picked, 'vec', axis=0, axis_index_groups=rings)]
    all_to_all x0 -> x1, starting transfers between devices: none -> 16.3 us  [shards(): pieces = lax.all_to_all(pack(trajectory), 'vec', 0, 0, tiled=True)]
    ppermute x4 -> x6, waiting for transfers between devices: 0.5 us -> 14.9 us  [the longest x2 14.5 us: halos(): lax.ppermute(first, 'lat', southward)]
    ppermute x4 -> x6, starting transfers between devices: 38.1 us -> 24.4 us  [the longest x2 14.8 us: halos(): lax.ppermute(last, 'lat', northward)]
    slice x13 -> x2, local copies, waits for them, and re-layouts: 11.8 us -> 0.8 us  [the longest x1 0.66 us: shards(): hour_slot[h]]
    pallas_call x0 -> x3, Pallas kernels: none -> 10.8 us  [the longest x2 9.72 us: one_hour(): pl.pallas_call(hour_kernel, out_shape=(jax.ShapeDtypeStruct(q.shape, jnp....]
  transfers between devices with their start and end apart: 5 -> 7, of which waited for: 2 -> 4; matrix products, arithmetic and copies ran while one was open for 5% -> 1% of each run, Pallas kernels for 0% -> 3%
where the time goes in v2:
time: 144 us
  waiting for transfers between devices  55.2 us (38%)
  starting transfers between devices  40.7 us (28%)
  blocking collectives  29.9 us (21%)
  Pallas kernels  10.8 us (8%)
  between operations  3.84 us (3%)
  local copies, waits for them, and re-layouts  3.34 us (2%)
    all_to_all x1, waiting for transfers between devices, shards(): pieces = lax.all_to_all(pack(trajectory), 'vec', 0, 0, tiled=True)  40.3 us
    all_gather x1, blocking collectives, shards(): gathered = lax.all_gather(picked, 'vec', axis=0, axis_index_groups=rings)  29.9 us
    all_to_all x1, starting transfers between devices, shards(): pieces = lax.all_to_all(pack(trajectory), 'vec', 0, 0, tiled=True)  16.3 us
    ppermute x2, starting transfers between devices, halos(): lax.ppermute(last, 'lat', northward)  14.8 us
    ppermute x2, waiting for transfers between devices, halos(): lax.ppermute(first, 'lat', southward)  14.5 us
    pallas_call x2, Pallas kernels, one_hour(): pl.pallas_call(hour_kernel, out_shape=(jax.ShapeDtypeStruct(q.shape, jnp....  9.72 us
    ppermute x2, starting transfers between devices, shards(): other = [lax.ppermute(half, 'vec', swap) for half in own]  5.28 us
    ppermute x2, starting transfers between devices, halos(): lax.ppermute(first, 'lat', southward)  4.3 us
  transfers between devices with their start and end apart: 7, of which 4 were waited for; matrix products, arithmetic and copies ran while one was open for 1% of the time, Pallas kernels for 3%

profile of v2, /device:TPU:25, one launch (start us, length us, event | category | flops | bytes accessed | tf_op | source)
XLA Modules:
  0.0 143.8 jit_solution(14862348031149450816)
XLA Ops:
  0.0 1.2 copy-done.1
  1.2 1.1 pack.1
  2.2 16.3 %all-to-all-start = ((bf16[32,112,128]{2,1,0:T(8,128)(2,1)}), bf16[32,112,128]{2,1,0:T(8,128)(2,1)S(1)}, u32[]{:S(2)}, u32[]{:S(2)}) async-start(bf16[32,112,128]{2,1,0:T(8,128)(2,1)} %pack.1), calls=%async_computation | async-start | bytes 1835008 | tf_op jit(solution)/shard_map/all_to_all | solution.py:140
  18.5 0.0 copy-start.2
  18.5 0.7 fusion.1
  22.9 40.3 %all-to-all-done = bf16[32,112,128]{2,1,0:T(8,128)(2,1)S(1)} async-done(((bf16[32,112,128]{2,1,0:T(8,128)(2,1)}), bf16[32,112,128]{2,1,0:T(8,128)(2,1)S(1)}, u32[]{:S(2)}, u32[]{:S(2)}) %all-to-all-start) | async-done | bytes 917536 | tf_op jit(solution)/shard_map/all_to_all | solution.py:140
  63.2 29.9 %all-gather = bf16[32,112,128]{2,1,0:T(8,128)(2,1)S(1)} all-gather(bf16[2,112,128]{2,1,0:T(8,128)(2,1)S(1)} %pad_maximum_fusion), channel_id=2, replica_groups={{0,16,32,48,64,80,96,112,128,144,160,176,192,208,224,240},{256,272,288,..., dimensions={0}, use_global_device_ids=true | all-gather | bytes 974848 | tf_op jit(solution)/shard_map/all_gather | solution.py:142
  93.1 0.1 slice_bitcast_fusion
  93.2 1.9 %collective-permute-start.2 = (bf16[16,112,128]{2,1,0:T(8,128)(2,1)S(1)}, bf16[16,112,128]{2,1,0:T(8,128)(2,1)}, u32[]{:S(2)}, u32[]{:S(2)}) collective-permute-start(bf16[16,112,128]{2,1,0:T(8,128)(2,1)S(1)} %get-tuple-element.16.own_ref), channel_id=1, source_target_pairs={{0,256},{16,272},{32,288},{48,304},{64,320},{80,336},{96,352},{112... | collective-permute-start | bytes 1376264 | tf_op jit(solution)/shard_map/ppermute | solution.py:144
  95.1 3.4 %collective-permute-start.5 = (bf16[16,112,128]{2,1,0:T(8,128)(2,1)S(1)}, bf16[16,112,128]{2,1,0:T(8,128)(2,1)}, u32[]{:S(2)}, u32[]{:S(2)}) collective-permute-start(bf16[16,112,128]{2,1,0:T(8,128)(2,1)S(1)} %get-tuple-element.15.own_ref), channel_id=1, source_target_pairs={{0,256},{16,272},{32,288},{48,304},{64,320},{80,336},{96,352},{112... | collective-permute-start | bytes 1376264 | tf_op jit(solution)/shard_map/ppermute | solution.py:144
  98.5 0.1 fusion
  98.6 0.6 copy.22
  99.3 12.9 %collective-permute-start = (f32[4,8,720]{2,1,0:T(8,128)}, f32[4,8,720]{2,1,0:T(8,128)S(1)}, u32[]{:S(2)}, u32[]{:S(2)}) collective-permute-start(f32[4,8,720]{2,1,0:T(8,128)} %bitcast.17), channel_id=1, source_target_pairs={{0,1},{1,2},{2,3},{3,4},{4,5},{5,6},{6,7},{7,8},{8,9},{9,10},{10,1... | collective-permute-start | bytes 276488 | tf_op jit(solution)/shard_map/ppermute | solution.py:138
  112.2 0.6 copy.21
  112.8 1.9 %collective-permute-start.1 = (f32[4,8,720]{2,1,0:T(8,128)}, f32[4,8,720]{2,1,0:T(8,128)S(1)}, u32[]{:S(2)}, u32[]{:S(2)}) collective-permute-start(f32[4,8,720]{2,1,0:T(8,128)} %bitcast.16), channel_id=1, source_target_pairs={{1,0},{2,1},{3,2},{4,3},{5,4},{6,5},{7,6},{8,7},{9,8},{10,9},{11,1... | collective-permute-start | bytes 276488 | tf_op jit(solution)/shard_map/ppermute | solution.py:138
  114.7 0.4 collective-permute-done.south_ref
  115.1 7.4 %collective-permute-done.1.north_ref = f32[4,8,720]{2,1,0:T(8,128)S(1)} collective-permute-done((f32[4,8,720]{2,1,0:T(8,128)}, f32[4,8,720]{2,1,0:T(8,128)S(1)}, u32[]{:S(2)}, u32[]{:S(2)}) %collective-permute-start.1) | collective-permute-done | bytes 92192 | tf_op jit(solution)/shard_map/ppermute | solution.py:138
  122.6 0.0 collective-permute-done.2.other_ref
  122.6 4.1 %one_hour.2 = (f32[4,8,24,720]{3,2,1,0:T(8,128)S(1)}, f32[4,8,720]{2,1,0:T(8,128)S(1)}, f32[4,8,720]{2,1,0:T(8,128)S(1)}) custom-call(s32[1]{0:T(128)} %bitcast.column_ref, f32[4,8,24,720]{3,2,1,0:T(8,128)S(1)} %copy-done, f32[4,8,720]{2,1,0:T(8,128)S(1)} %collective-permute-done.south_ref, f32[4,8,720]{2,1,0:T(8,128)S(1)} %collective-permute-done.1.north_ref, ...), custom_call_target="tpu_custom_call" | custom-call | flops 13824000 | bytes 4423680 | tf_op jit(solution)/shard_map/one_hour/pallas_call | solution.py:117
  126.7 1.9 %collective-permute-start.3 = (f32[4,8,720]{2,1,0:T(8,128)S(1)}, f32[4,8,720]{2,1,0:T(8,128)S(1)}, u32[]{:S(2)}, u32[]{:S(2)}) collective-permute-start(f32[4,8,720]{2,1,0:T(8,128)S(1)} %get-tuple-element.10), channel_id=1, source_target_pairs={{0,1},{1,2},{2,3},{3,4},{4,5},{5,6},{6,7},{7,8},{8,9},{9,10},{10,1... | collective-permute-start | bytes 276488 | tf_op jit(solution)/shard_map/ppermute | solution.py:138
  128.6 2.4 %collective-permute-start.4 = (f32[4,8,720]{2,1,0:T(8,128)S(1)}, f32[4,8,720]{2,1,0:T(8,128)S(1)}, u32[]{:S(2)}, u32[]{:S(2)}) collective-permute-start(f32[4,8,720]{2,1,0:T(8,128)S(1)} %get-tuple-element.11), channel_id=1, source_target_pairs={{1,0},{2,1},{3,2},{4,3},{5,4},{6,5},{7,6},{8,7},{9,8},{10,9},{11,1... | collective-permute-start | bytes 276488 | tf_op jit(solution)/shard_map/ppermute | solution.py:138
  131.0 0.0 collective-permute-done.5.other_ref
  131.1 7.1 %collective-permute-done.4.north_ref = f32[4,8,720]{2,1,0:T(8,128)S(1)} collective-permute-done((f32[4,8,720]{2,1,0:T(8,128)S(1)}, f32[4,8,720]{2,1,0:T(8,128)S(1)}, u32[]{:S(2)}, u32[]{:S(2)}) %collective-permute-start.4) | collective-permute-done | bytes 92192 | tf_op jit(solution)/shard_map/ppermute | solution.py:138
  138.2 5.6 %one_hour.3 = (f32[4,8,24,720]{3,2,1,0:T(8,128)}, f32[4,8,720]{2,1,0:T(8,128)}, f32[4,8,720]{2,1,0:T(8,128)}) custom-call(s32[1]{0:T(128)} %bitcast.column_ref, f32[4,8,24,720]{3,2,1,0:T(8,128)S(1)} %get-tuple-element.9.q_ref, f32[4,8,720]{2,1,0:T(8,128)S(1)} %collective-permute-done.3.south_ref, f32[4,8,720]{2,1,0:T(8,128)S(1)} %collective-permute-done.4.north_ref, ...), custom_call_target="tpu_custom_call" | custom-call | flops 13824000 | bytes 4423680 | tf_op jit(solution)/shard_map/one_hour/pallas_call | solution.py:117
  (9 shorter events, 0.0 us)
Async XLA Ops:
  0.0 1.2 copy-start.1
  1.2 17.4 %copy-start.3 = (s32[2]{0:T(128)S(1)}, s32[2]{0:T(128)}, u32[]{:S(2)}) copy-start(s32[2]{0:T(128)} %param.6) | copy-start | bytes 28
  2.2 96.2 %copy-start = (f32[4,8,24,720]{3,2,1,0:T(8,128)S(1)}, f32[4,8,24,720]{3,2,1,0:T(8,128)}, u32[]{:S(2)}) copy-start(f32[4,8,24,720]{3,2,1,0:T(8,128)} %q_ref.1) | copy-start | bytes 6635524
  2.2 60.9 %all-to-all-start = ((bf16[32,112,128]{2,1,0:T(8,128)(2,1)}), bf16[32,112,128]{2,1,0:T(8,128)(2,1)S(1)}, u32[]{:S(2)}, u32[]{:S(2)}) async-start(bf16[32,112,128]{2,1,0:T(8,128)(2,1)} %pack.1), calls=%async_computation | async-start | bytes 1835008 | tf_op jit(solution)/shard_map/all_to_all | solution.py:140
  18.5 104.0 %copy-start.2 = (s32[24,720]{1,0:T(8,128)S(1)}, s32[24,720]{1,0:T(8,128)}, u32[]{:S(2)}) copy-start(s32[24,720]{1,0:T(8,128)} %mask_ref.3) | copy-start | bytes 207364
  93.2 29.4 %collective-permute-start.2 = (bf16[16,112,128]{2,1,0:T(8,128)(2,1)S(1)}, bf16[16,112,128]{2,1,0:T(8,128)(2,1)}, u32[]{:S(2)}, u32[]{:S(2)}) collective-permute-start(bf16[16,112,128]{2,1,0:T(8,128)(2,1)S(1)} %get-tuple-element.16.own_ref), channel_id=1, source_target_pairs={{0,256},{16,272},{32,288},{48,304},{64,320},{80,336},{96,352},{112... | collective-permute-start | bytes 1376264 | tf_op jit(solution)/shard_map/ppermute | solution.py:144
  95.1 35.9 %collective-permute-start.5 = (bf16[16,112,128]{2,1,0:T(8,128)(2,1)S(1)}, bf16[16,112,128]{2,1,0:T(8,128)(2,1)}, u32[]{:S(2)}, u32[]{:S(2)}) collective-permute-start(bf16[16,112,128]{2,1,0:T(8,128)(2,1)S(1)} %get-tuple-element.15.own_ref), channel_id=1, source_target_pairs={{0,256},{16,272},{32,288},{48,304},{64,320},{80,336},{96,352},{112... | collective-permute-start | bytes 1376264 | tf_op jit(solution)/shard_map/ppermute | solution.py:144
  99.3 15.9 %collective-permute-start = (f32[4,8,720]{2,1,0:T(8,128)}, f32[4,8,720]{2,1,0:T(8,128)S(1)}, u32[]{:S(2)}, u32[]{:S(2)}) collective-permute-start(f32[4,8,720]{2,1,0:T(8,128)} %bitcast.17), channel_id=1, source_target_pairs={{0,1},{1,2},{2,3},{3,4},{4,5},{5,6},{6,7},{7,8},{8,9},{9,10},{10,1... | collective-permute-start | bytes 276488 | tf_op jit(solution)/shard_map/ppermute | solution.py:138
  112.8 9.7 %collective-permute-start.1 = (f32[4,8,720]{2,1,0:T(8,128)}, f32[4,8,720]{2,1,0:T(8,128)S(1)}, u32[]{:S(2)}, u32[]{:S(2)}) collective-permute-start(f32[4,8,720]{2,1,0:T(8,128)} %bitcast.16), channel_id=1, source_target_pairs={{1,0},{2,1},{3,2},{4,3},{5,4},{6,5},{7,6},{8,7},{9,8},{10,9},{11,1... | collective-permute-start | bytes 276488 | tf_op jit(solution)/shard_map/ppermute | solution.py:138
  126.7 4.4 %collective-permute-start.3 = (f32[4,8,720]{2,1,0:T(8,128)S(1)}, f32[4,8,720]{2,1,0:T(8,128)S(1)}, u32[]{:S(2)}, u32[]{:S(2)}) collective-permute-start(f32[4,8,720]{2,1,0:T(8,128)S(1)} %get-tuple-element.10), channel_id=1, source_target_pairs={{0,1},{1,2},{2,3},{3,4},{4,5},{5,6},{6,7},{7,8},{8,9},{9,10},{10,1... | collective-permute-start | bytes 276488 | tf_op jit(solution)/shard_map/ppermute | solution.py:138
  128.6 9.5 %collective-permute-start.4 = (f32[4,8,720]{2,1,0:T(8,128)S(1)}, f32[4,8,720]{2,1,0:T(8,128)S(1)}, u32[]{:S(2)}, u32[]{:S(2)}) collective-permute-start(f32[4,8,720]{2,1,0:T(8,128)S(1)} %get-tuple-element.11), channel_id=1, source_target_pairs={{1,0},{2,1},{3,2},{4,3},{5,4},{6,5},{7,6},{8,7},{9,8},{10,9},{11,1... | collective-permute-start | bytes 276488 | tf_op jit(solution)/shard_map/ppermute | solution.py:138

commit v3 on v2

--- a/solution.py
+++ b/solution.py
@@ -64,18 +64,60 @@
     return jnp.concatenate([x[..., -1:], x[..., :-1]], axis=-1)
 
 
-def advance(c, n, s, u, b, f0, f1, f2, mask):
-    e, w = lanes_next(c), lanes_prev(c)
-    diffuse = 0.06 + 0.015 * f0
-    change = diffuse * (e + w + n + s - 4.0 * c)
-    change = change - (0.15 * f1) * (e - w) - (0.15 * f2) * (n - s)
-    change = change + 0.1 * (u + b - 2.0 * c)
-    return mask * (c + change)
+def weights(f0, f1, f2, mask):
+    diffuse = mask * (0.06 + 0.015 * f0)
+    zonal, merid = mask * (0.15 * f1), mask * (0.15 * f2)
+    return (
+        0.8 * mask - 4.0 * diffuse,
+        diffuse - zonal,
+        diffuse + zonal,
+        diffuse - merid,
+        diffuse + merid,
+        0.1 * mask,
+    )
+
+
+def advance(c, n, s, u, b, weight):
+    wc, we, ww, wn, ws, wl = weight
+    return (wc * c + we * lanes_next(c) + ww * lanes_prev(c)) + (wn * n + ws * s + wl * (u + b))
+
+
+def rows_kernel(
+    column_ref, q_ref, south_ref, north_ref, mask_ref, own_ref, other_ref, first_ref, last_ref, field_ref
+):
+    vecs, levs, rows, lon = q_ref.shape
+    lev = lax.broadcasted_iota(jnp.int32, (levs, lon), 0)
+    own_column = column_ref[0]
+
+    def row_of(v, r):
+        return jnp.concatenate([q_ref[v, z, r : r + 1] for z in range(levs)], axis=0)
+
+    for out_ref, r, step in ((first_ref, 0, 1), (last_ref, rows - 1, -1)):
+        for own in range(COLUMNS):
+
+            @pl.when(own_column == own)
+            def _():
+                for half in range(2):
+                    for k, tile, lo, hi, column, at in field_parts(rows, half):
+                        if lo <= r < hi:
+                            piece_ref = own_ref if column == own else other_ref
+                            base = at + (r - lo) // 8 * 8
+                            for z in range(levs):
+                                eight = piece_ref[z * 2 + half, base : base + 8].astype(jnp.float32)
+                                i = (r - lo) % 8
+                                field_ref[k, z : z + 1, tile * LANES : (tile + 1) * LANES] = eight[i : i + 1]
+
+        weight = weights(*(field_ref[k, :, :lon] for k in range(FIELDS)), mask_ref[r : r + 1].astype(jnp.float32))
+        for v in range(vecs):
+            c, inner = row_of(v, r), row_of(v, r + step)
+            n, s = (inner, south_ref[v]) if r == 0 else (north_ref[v], inner)
+            u = jnp.where(lev == 0, c, pltpu.roll(c, 1, 0))
+            b = jnp.where(lev == levs - 1, c, pltpu.roll(c, levs - 1, 0))
+            out_ref[v] = advance(c, n, s, u, b, weight)
 
 
 def hour_kernel(
-    column_ref, q_ref, south_ref, north_ref, mask_ref, own_ref, other_ref,
-    out_ref, first_ref, last_ref, field_ref,
+    column_ref, q_ref, south_ref, north_ref, mask_ref, own_ref, other_ref, out_ref, field_ref
 ):
     vecs, levs, rows, lon = q_ref.shape
     row = lax.broadcasted_iota(jnp.int32, (rows, lon), 0)
@@ -94,36 +136,46 @@
                             level * 2 + half, at : at + hi - lo
                         ].astype(jnp.float32)
 
-        f0, f1, f2 = (field_ref[k, :, :lon] for k in range(FIELDS))
+        weight = weights(*(field_ref[k, :, :lon] for k in range(FIELDS)), mask)
         up = jnp.maximum(level - 1, 0)
         low = jnp.minimum(level + 1, levs - 1)
         for v in range(vecs):
             c = q_ref[v, level]
             n = jnp.where(row == rows - 1, north_ref[v, pl.ds(level, 1)], pltpu.roll(c, rows - 1, 0))
             s = jnp.where(row == 0, south_ref[v, pl.ds(level, 1)], pltpu.roll(c, 1, 0))
-            new = advance(c, n, s, q_ref[v, up], q_ref[v, low], f0, f1, f2, mask)
-            out_ref[v, level] = new
-            first_ref[v, pl.ds(level, 1)] = new[:1]
-            last_ref[v, pl.ds(level, 1)] = new[rows - 1 :]
+            out_ref[v, level] = advance(c, n, s, q_ref[v, up], q_ref[v, low], weight)
         return carry
 
     lax.fori_loop(0, levs, level_step, 0)
 
 
-def one_hour(column, q, south, north, mask, own, other):
-    vecs, levs, rows, lon = q.shape
+def on_band(kernel, name, outs, field_rows, flops, args):
     vmem = pl.BlockSpec(memory_space=pltpu.VMEM)
+    lon = args[1].shape[-1]
+    bytes_accessed = sum(a.size * a.dtype.itemsize for a in (*args, *outs))
+    return pl.pallas_call(
+        kernel,
+        out_shape=outs,
+        in_specs=[pl.BlockSpec(memory_space=pltpu.SMEM)] + [vmem] * (len(args) - 1),
+        out_specs=tuple(vmem for _ in outs),
+        scratch_shapes=[pltpu.VMEM((FIELDS, field_rows, -(-lon // LANES) * LANES), jnp.float32)],
+        compiler_params=pltpu.CompilerParams(vmem_limit_bytes=VMEM_LIMIT),
+        cost_estimate=pl.CostEstimate(flops=flops, bytes_accessed=bytes_accessed, transcendentals=0),
+        name=name,
+    )(*args)
+
+
+def edge_rows(*args):
+    vecs, levs, _, lon = args[1].shape
     edge = jax.ShapeDtypeStruct((vecs, levs, lon), jnp.float32)
-    return pl.pallas_call(
-        hour_kernel,
-        out_shape=(jax.ShapeDtypeStruct(q.shape, jnp.float32), edge, edge),
-        in_specs=[pl.BlockSpec(memory_space=pltpu.SMEM)] + [vmem] * 6,
-        out_specs=(vmem, vmem, vmem),
-        scratch_shapes=[pltpu.VMEM((FIELDS, rows, 6 * LANES), jnp.float32)],
-        compiler_params=pltpu.CompilerParams(vmem_limit_bytes=VMEM_LIMIT),
-        cost_estimate=pl.CostEstimate(flops=25 * q.size, bytes_accessed=8 * q.size, transcendentals=0),
-        name="one_hour",
-    )(column, q, south, north, mask, own, other)
+    return on_band(rows_kernel, "edge_rows", (edge, edge), levs, 30 * edge.size, args)
+
+
+def one_hour(*args):
+    q = args[1]
+    return on_band(
+        hour_kernel, "one_hour", (jax.ShapeDtypeStruct(q.shape, q.dtype),), q.shape[2], 20 * q.size, args
+    )[0]
 
 
 def shards(perturb, trajectory, hour_slot, sea_mask):
@@ -137,19 +189,19 @@
     def halos(first, last):
         return lax.ppermute(last, "lat", northward), lax.ppermute(first, "lat", southward)
 
+    which = column.astype(jnp.int32)[None]
+    halo = halos(perturb[:, :, 0], perturb[:, :, -1])
+
     pieces = lax.all_to_all(pack(trajectory), "vec", 0, 0, tiled=True)
     picked = jnp.stack([lax.dynamic_index_in_dim(pieces, hour_slot[h], 0, keepdims=False) for h in range(2)])
+    picked = picked + (sum(h[0, 0, 0] for h in halo) * 0).astype(picked.dtype)
     gathered = lax.all_gather(picked, "vec", axis=0, axis_index_groups=rings)
     own = [gathered[:, h] for h in range(2)]
     other = [lax.ppermute(half, "vec", swap) for half in own]
 
-    q = perturb
-    first, last = q[:, :, 0], q[:, :, -1]
-    which = column.astype(jnp.int32)[None]
-    for h in range(2):
-        south, north = halos(first, last)
-        q, first, last = one_hour(which, q, south, north, sea_mask, own[h], other[h])
-    return q
+    args = (which, perturb, *halo, sea_mask, own[0], other[0])
+    halo = halos(*edge_rows(*args))
+    return one_hour(which, one_hour(*args), *halo, sea_mask, own[1], other[1])
 
 
 def solution(mesh):

time: 144 us -> 134 us (0.931)
  waiting for transfers between devices: 55.2 us -> 37.4 us
  starting transfers between devices: 40.7 us -> 44.5 us
  between operations: 3.84 us -> 5.39 us
    all_to_all x1, waiting for transfers between devices: 40.3 us -> 25.8 us  [shards(): pieces = lax.all_to_all(pack(trajectory), 'vec', 0, 0, tiled=True)]
    ppermute x2, waiting for transfers between devices: 14.5 us -> 7.54 us  [halos(): lax.ppermute(first, 'lat', southward)]
    ppermute x2, starting transfers between devices: 14.8 us -> 19.3 us  [halos(): lax.ppermute(last, 'lat', northward)]
    ppermute x2, waiting for transfers between devices: 0.01 us -> 4.02 us  [shards(): other = [lax.ppermute(half, 'vec', swap) for half in own]]
    pallas_call x2 -> x3, Pallas kernels: 9.72 us -> 10.5 us  [on_band(): pl.pallas_call(kernel, out_shape=outs, in_specs=[pl.BlockSpec(memory_spac...]
  transfers between devices with their start and end apart: 7 -> 7, of which waited for: 4 -> 4; matrix products, arithmetic and copies ran while one was open for 1% -> 2% of each run, Pallas kernels for 3% -> 4%
where the time goes in v3:
time: 134 us; the launch traced here: 133 us
  starting transfers between devices  44.5 us (33%)
  waiting for transfers between devices  37.4 us (28%)
  blocking collectives  29.9 us (22%)
  Pallas kernels  11.6 us (9%)
  between operations  5.39 us (4%)
  local copies, waits for them, and re-layouts  4.52 us (3%)
    all_gather x1, blocking collectives, shards(): gathered = lax.all_gather(picked, 'vec', axis=0, axis_index_groups=rings)  29.9 us
    all_to_all x1, waiting for transfers between devices, shards(): pieces = lax.all_to_all(pack(trajectory), 'vec', 0, 0, tiled=True)  25.8 us
    ppermute x2, starting transfers between devices, halos(): lax.ppermute(last, 'lat', northward)  19.3 us
    all_to_all x1, starting transfers between devices, shards(): pieces = lax.all_to_all(pack(trajectory), 'vec', 0, 0, tiled=True)  16.1 us
    pallas_call x3, Pallas kernels, on_band(): pl.pallas_call(kernel, out_shape=outs, in_specs=[pl.BlockSpec(memory_spac...  10.5 us
    ppermute x2, waiting for transfers between devices, halos(): lax.ppermute(first, 'lat', southward)  7.54 us
    ppermute x2, starting transfers between devices, shards(): other = [lax.ppermute(half, 'vec', swap) for half in own]  5.28 us
    ppermute x2, waiting for transfers between devices, shards(): other = [lax.ppermute(half, 'vec', swap) for half in own]  4.02 us
  transfers between devices with their start and end apart: 7, of which 4 were waited for; matrix products, arithmetic and copies ran while one was open for 2% of the time, Pallas kernels for 4%

profile of v3, /device:TPU:25, one launch (start us, length us, event | category | flops | bytes accessed | tf_op | source)
XLA Modules:
  0.0 133.3 jit_solution(5685753945982710059)
XLA Ops:
  0.0 1.3 copy-done.1
  1.3 1.1 pack.1
  2.4 16.1 %all-to-all-start = ((bf16[32,112,128]{2,1,0:T(8,128)(2,1)}), bf16[32,112,128]{2,1,0:T(8,128)(2,1)S(1)}, u32[]{:S(2)}, u32[]{:S(2)}) async-start(bf16[32,112,128]{2,1,0:T(8,128)(2,1)} %pack.1), calls=%async_computation | async-start | bytes 1835008 | tf_op jit(solution)/shard_map/all_to_all | solution.py:195
  18.6 0.1 fusion
  18.7 0.6 copy.12
  19.4 4.8 %collective-permute-start = (f32[4,8,720]{2,1,0:T(8,128)}, f32[4,8,720]{2,1,0:T(8,128)S(1)}, u32[]{:S(2)}, u32[]{:S(2)}) collective-permute-start(f32[4,8,720]{2,1,0:T(8,128)} %bitcast.17), channel_id=1, source_target_pairs={{0,1},{1,2},{2,3},{3,4},{4,5},{5,6},{6,7},{7,8},{8,9},{9,10},{10,1... | collective-permute-start | bytes 276488 | tf_op jit(solution)/shard_map/ppermute | solution.py:190
  24.2 0.6 copy.11
  24.9 1.9 %collective-permute-start.1 = (f32[4,8,720]{2,1,0:T(8,128)}, f32[4,8,720]{2,1,0:T(8,128)S(1)}, u32[]{:S(2)}, u32[]{:S(2)}) collective-permute-start(f32[4,8,720]{2,1,0:T(8,128)} %bitcast.16), channel_id=1, source_target_pairs={{1,0},{2,1},{3,2},{4,3},{5,4},{6,5},{7,6},{8,7},{9,8},{10,9},{11,1... | collective-permute-start | bytes 276488 | tf_op jit(solution)/shard_map/ppermute | solution.py:190
  26.8 0.6 fusion.1
  31.4 0.5 slice.32
  31.9 3.7 %collective-permute-done.1.north_ref = f32[4,8,720]{2,1,0:T(8,128)S(1)} collective-permute-done((f32[4,8,720]{2,1,0:T(8,128)}, f32[4,8,720]{2,1,0:T(8,128)S(1)}, u32[]{:S(2)}, u32[]{:S(2)}) %collective-permute-start.1) | collective-permute-done | bytes 92192 | tf_op jit(solution)/shard_map/ppermute | solution.py:190
  35.6 0.5 slice.33
  37.4 25.8 %all-to-all-done = bf16[32,112,128]{2,1,0:T(8,128)(2,1)S(1)} async-done(((bf16[32,112,128]{2,1,0:T(8,128)(2,1)}), bf16[32,112,128]{2,1,0:T(8,128)(2,1)S(1)}, u32[]{:S(2)}, u32[]{:S(2)}) %all-to-all-start) | async-done | bytes 917536 | tf_op jit(solution)/shard_map/all_to_all | solution.py:195
  63.2 29.9 %all_gather.4 = bf16[16,2,112,128]{3,2,0,1:T(8,128)(2,1)S(1)} all-gather(bf16[1,2,112,128]{3,2,0,1:T(8,128)(2,1)S(1)} %maximum_add_fusion), channel_id=1, replica_groups={{0,16,32,48,64,80,96,112,128,144,160,176,192,208,224,240},{256,272,288,..., dimensions={0}, use_global_device_ids=true | all-gather | bytes 974848 | tf_op jit(solution)/shard_map/all_gather | solution.py:198
  93.1 0.1 slice_bitcast_fusion
  93.2 1.9 %collective-permute-start.2 = (bf16[16,112,128]{2,1,0:T(8,128)(2,1)S(1)}, bf16[16,112,128]{2,1,0:T(8,128)(2,1)}, u32[]{:S(2)}, u32[]{:S(2)}) collective-permute-start(bf16[16,112,128]{2,1,0:T(8,128)(2,1)S(1)} %get-tuple-element.12.own_ref), channel_id=1, source_target_pairs={{0,256},{16,272},{32,288},{48,304},{64,320},{80,336},{96,352},{112... | collective-permute-start | bytes 1376264 | tf_op jit(solution)/shard_map/ppermute | solution.py:200
  95.1 3.4 %collective-permute-start.5 = (bf16[16,112,128]{2,1,0:T(8,128)(2,1)S(1)}, bf16[16,112,128]{2,1,0:T(8,128)(2,1)}, u32[]{:S(2)}, u32[]{:S(2)}) collective-permute-start(bf16[16,112,128]{2,1,0:T(8,128)(2,1)S(1)} %get-tuple-element.11.own_ref), channel_id=1, source_target_pairs={{0,256},{16,272},{32,288},{48,304},{64,320},{80,336},{96,352},{112... | collective-permute-start | bytes 1376264 | tf_op jit(solution)/shard_map/ppermute | solution.py:200
  98.5 4.0 %collective-permute-done.2.other_ref = bf16[16,112,128]{2,1,0:T(8,128)(2,1)} collective-permute-done((bf16[16,112,128]{2,1,0:T(8,128)(2,1)S(1)}, bf16[16,112,128]{2,1,0:T(8,128)(2,1)}, u32[]{:S(2)}, u32[]{:S(2)}) %collective-permute-start.2) | collective-permute-done | bytes 458784 | tf_op jit(solution)/shard_map/ppermute | solution.py:200
  102.5 1.5 %edge_rows.1 = (f32[4,8,720]{2,1,0:T(8,128)S(1)}, f32[4,8,720]{2,1,0:T(8,128)S(1)}) custom-call(s32[1]{0:T(128)} %bitcast.column_ref, f32[4,8,24,720]{3,2,1,0:T(8,128)S(1)} %copy-done, f32[4,8,720]{2,1,0:T(8,128)S(1)} %collective-permute-done.south_ref, f32[4,8,720]{2,1,0:T(8,128)S(1)} %collective-permute-done.1.north_ref, s32[24,720]{1,0:T(8,128)S(1)} %copy-done.2, ...), custom_call_target="tpu_custom_call" | custom-call | flops 691200 | bytes 3567108 | tf_op jit(solution)/shard_map/edge_rows/pallas_call | solution.py:156
  104.0 14.4 %collective-permute-start.3 = (f32[4,8,720]{2,1,0:T(8,128)S(1)}, f32[4,8,720]{2,1,0:T(8,128)S(1)}, u32[]{:S(2)}, u32[]{:S(2)}) collective-permute-start(f32[4,8,720]{2,1,0:T(8,128)S(1)} %get-tuple-element.7), channel_id=1, source_target_pairs={{0,1},{1,2},{2,3},{3,4},{4,5},{5,6},{6,7},{7,8},{8,9},{9,10},{10,1... | collective-permute-start | bytes 276488 | tf_op jit(solution)/shard_map/ppermute | solution.py:190
  118.5 1.9 %collective-permute-start.4 = (f32[4,8,720]{2,1,0:T(8,128)S(1)}, f32[4,8,720]{2,1,0:T(8,128)S(1)}, u32[]{:S(2)}, u32[]{:S(2)}) collective-permute-start(f32[4,8,720]{2,1,0:T(8,128)S(1)} %get-tuple-element.8), channel_id=1, source_target_pairs={{1,0},{2,1},{3,2},{4,3},{5,4},{6,5},{7,6},{8,7},{9,8},{10,9},{11,1... | collective-permute-start | bytes 276488 | tf_op jit(solution)/shard_map/ppermute | solution.py:190
  120.4 3.8 %one_hour.2.q_ref = f32[4,8,24,720]{3,2,1,0:T(8,128)S(1)} custom-call(s32[1]{0:T(128)} %bitcast.column_ref, f32[4,8,24,720]{3,2,1,0:T(8,128)S(1)} %copy-done, f32[4,8,720]{2,1,0:T(8,128)S(1)} %collective-permute-done.south_ref, f32[4,8,720]{2,1,0:T(8,128)S(1)} %collective-permute-done.1.north_ref, s32[24,720]{1,0:T(8,128)S(1)} %copy-done.2, ...), custom_call_target="tpu_custom_call" | custom-call | flops 11059200 | bytes 5594628 | tf_op jit(solution)/shard_map/one_hour/pallas_call | solution.py:156
  124.2 3.8 %collective-permute-done.4.north_ref = f32[4,8,720]{2,1,0:T(8,128)S(1)} collective-permute-done((f32[4,8,720]{2,1,0:T(8,128)S(1)}, f32[4,8,720]{2,1,0:T(8,128)S(1)}, u32[]{:S(2)}, u32[]{:S(2)}) %collective-permute-start.4) | collective-permute-done | bytes 92192 | tf_op jit(solution)/shard_map/ppermute | solution.py:190
  128.0 5.3 %one_hour.3 = f32[4,8,24,720]{3,2,1,0:T(8,128)} custom-call(s32[1]{0:T(128)} %bitcast.column_ref, f32[4,8,24,720]{3,2,1,0:T(8,128)S(1)} %one_hour.2.q_ref, f32[4,8,720]{2,1,0:T(8,128)S(1)} %collective-permute-done.3.south_ref, f32[4,8,720]{2,1,0:T(8,128)S(1)} %collective-permute-done.4.north_ref, s32[24,720]{1,0:T(8,128)S(1)} %copy-done.2, ...), custom_call_target="tpu_custom_call" | custom-call | flops 11059200 | bytes 5594628 | tf_op jit(solution)/shard_map/one_hour/pallas_call | solution.py:156
  (12 shorter events, 0.0 us)
Async XLA Ops:
  0.0 18.5 %copy-start = (f32[4,8,24,720]{3,2,1,0:T(8,128)S(1)}, f32[4,8,24,720]{3,2,1,0:T(8,128)}, u32[]{:S(2)}) copy-start(f32[4,8,24,720]{3,2,1,0:T(8,128)} %q_ref.3) | copy-start | bytes 6635524
  0.0 1.3 copy-start.1
  1.3 25.5 %copy-start.3 = (s32[2]{0:T(128)S(1)}, s32[2]{0:T(128)}, u32[]{:S(2)}) copy-start(s32[2]{0:T(128)} %param.6) | copy-start | bytes 28
  2.4 60.8 %all-to-all-start = ((bf16[32,112,128]{2,1,0:T(8,128)(2,1)}), bf16[32,112,128]{2,1,0:T(8,128)(2,1)S(1)}, u32[]{:S(2)}, u32[]{:S(2)}) async-start(bf16[32,112,128]{2,1,0:T(8,128)(2,1)} %pack.1), calls=%async_computation | async-start | bytes 1835008 | tf_op jit(solution)/shard_map/all_to_all | solution.py:195
  18.5 84.0 %copy-start.2 = (s32[24,720]{1,0:T(8,128)S(1)}, s32[24,720]{1,0:T(8,128)}, u32[]{:S(2)}) copy-start(s32[24,720]{1,0:T(8,128)} %mask_ref.5) | copy-start | bytes 207364
  19.4 12.0 %collective-permute-start = (f32[4,8,720]{2,1,0:T(8,128)}, f32[4,8,720]{2,1,0:T(8,128)S(1)}, u32[]{:S(2)}, u32[]{:S(2)}) collective-permute-start(f32[4,8,720]{2,1,0:T(8,128)} %bitcast.17), channel_id=1, source_target_pairs={{0,1},{1,2},{2,3},{3,4},{4,5},{5,6},{6,7},{7,8},{8,9},{9,10},{10,1... | collective-permute-start | bytes 276488 | tf_op jit(solution)/shard_map/ppermute | solution.py:190
  24.9 10.7 %collective-permute-start.1 = (f32[4,8,720]{2,1,0:T(8,128)}, f32[4,8,720]{2,1,0:T(8,128)S(1)}, u32[]{:S(2)}, u32[]{:S(2)}) collective-permute-start(f32[4,8,720]{2,1,0:T(8,128)} %bitcast.16), channel_id=1, source_target_pairs={{1,0},{2,1},{3,2},{4,3},{5,4},{6,5},{7,6},{8,7},{9,8},{10,9},{11,1... | collective-permute-start | bytes 276488 | tf_op jit(solution)/shard_map/ppermute | solution.py:190
  93.2 9.3 %collective-permute-start.2 = (bf16[16,112,128]{2,1,0:T(8,128)(2,1)S(1)}, bf16[16,112,128]{2,1,0:T(8,128)(2,1)}, u32[]{:S(2)}, u32[]{:S(2)}) collective-permute-start(bf16[16,112,128]{2,1,0:T(8,128)(2,1)S(1)} %get-tuple-element.12.own_ref), channel_id=1, source_target_pairs={{0,256},{16,272},{32,288},{48,304},{64,320},{80,336},{96,352},{112... | collective-permute-start | bytes 1376264 | tf_op jit(solution)/shard_map/ppermute | solution.py:200
  95.1 29.0 %collective-permute-start.5 = (bf16[16,112,128]{2,1,0:T(8,128)(2,1)S(1)}, bf16[16,112,128]{2,1,0:T(8,128)(2,1)}, u32[]{:S(2)}, u32[]{:S(2)}) collective-permute-start(bf16[16,112,128]{2,1,0:T(8,128)(2,1)S(1)} %get-tuple-element.11.own_ref), channel_id=1, source_target_pairs={{0,256},{16,272},{32,288},{48,304},{64,320},{80,336},{96,352},{112... | collective-permute-start | bytes 1376264 | tf_op jit(solution)/shard_map/ppermute | solution.py:200
  104.0 20.1 %collective-permute-start.3 = (f32[4,8,720]{2,1,0:T(8,128)S(1)}, f32[4,8,720]{2,1,0:T(8,128)S(1)}, u32[]{:S(2)}, u32[]{:S(2)}) collective-permute-start(f32[4,8,720]{2,1,0:T(8,128)S(1)} %get-tuple-element.7), channel_id=1, source_target_pairs={{0,1},{1,2},{2,3},{3,4},{4,5},{5,6},{6,7},{7,8},{8,9},{9,10},{10,1... | collective-permute-start | bytes 276488 | tf_op jit(solution)/shard_map/ppermute | solution.py:190
  118.5 9.5 %collective-permute-start.4 = (f32[4,8,720]{2,1,0:T(8,128)S(1)}, f32[4,8,720]{2,1,0:T(8,128)S(1)}, u32[]{:S(2)}, u32[]{:S(2)}) collective-permute-start(f32[4,8,720]{2,1,0:T(8,128)S(1)} %get-tuple-element.8), channel_id=1, source_target_pairs={{1,0},{2,1},{3,2},{4,3},{5,4},{6,5},{7,6},{8,7},{9,8},{10,9},{11,1... | collective-permute-start | bytes 276488 | tf_op jit(solution)/shard_map/ppermute | solution.py:190

commit v4 on v3

--- a/solution.py
+++ b/solution.py
@@ -35,25 +35,33 @@
     return parts
 
 
-def pack_kernel(field_ref, piece_ref):
+def pack_kernel(column_ref, field_ref, keep_ref, send_ref):
     _, levs, rows, lon = field_ref.shape[1:]
-    for level in range(levs):
-        for half in range(2):
-            for k, tile, lo, hi, column, at in field_parts(rows, half):
-                p = column * RING + level * 2 + half
-                left, right = tile * LANES, min((tile + 1) * LANES, lon)
-                piece_ref[p, at : at + hi - lo, : right - left] = field_ref[0, k, level, lo:hi, left:right]
-
-
-def pack(trajectory):
+    for own in range(COLUMNS):
+
+        @pl.when(column_ref[0] == own)
+        def _():
+            for level in range(levs):
+                for half in range(2):
+                    for k, tile, lo, hi, column, at in field_parts(rows, half):
+                        piece_ref = keep_ref if column == own else send_ref
+                        left, right = tile * LANES, min((tile + 1) * LANES, lon)
+                        piece_ref[level * 2 + half, at : at + hi - lo, : right - left] = field_ref[
+                            0, k, level, lo:hi, left:right
+                        ]
+
+
+def pack(column, trajectory):
+    half = jax.ShapeDtypeStruct((RING, PIECE, LANES), trajectory.dtype)
+    vmem = pl.BlockSpec(memory_space=pltpu.VMEM)
     return pl.pallas_call(
         pack_kernel,
-        out_shape=jax.ShapeDtypeStruct((COLUMNS * RING, PIECE, LANES), trajectory.dtype),
-        in_specs=[pl.BlockSpec(memory_space=pltpu.VMEM)],
-        out_specs=pl.BlockSpec(memory_space=pltpu.VMEM),
+        out_shape=(half, half),
+        in_specs=[pl.BlockSpec(memory_space=pltpu.SMEM), vmem],
+        out_specs=(vmem, vmem),
         compiler_params=pltpu.CompilerParams(vmem_limit_bytes=VMEM_LIMIT),
         name="pack",
-    )(trajectory)
+    )(column, trajectory)
 
 
 def lanes_next(x):
@@ -192,8 +200,25 @@
     which = column.astype(jnp.int32)[None]
     halo = halos(perturb[:, :, 0], perturb[:, :, -1])
 
-    pieces = lax.all_to_all(pack(trajectory), "vec", 0, 0, tiled=True)
-    picked = jnp.stack([lax.dynamic_index_in_dim(pieces, hour_slot[h], 0, keepdims=False) for h in range(2)])
+    end, last_hour = RING - 1, COLUMNS * RING - 1
+    spare = end - 1
+    keep, send = pack(which, trajectory)
+    crossed = lax.ppermute(send, "vec", [p for p in swap if p[0] != end])
+    moved = jnp.where(
+        column == 0,
+        lax.ppermute(keep, "vec", [(end, spare)]),
+        lax.ppermute(send, "vec", [(end, RING + spare)]),
+    )
+    asked = hour_slot[0] + hour_slot[1] - last_hour
+    z = lax.axis_index("vec") % RING
+    from_column = jnp.where(z == end, 1, asked // RING)
+    offered = jnp.where(
+        (z == spare) & (asked == end), moved, jnp.where(from_column == column, keep, crossed)
+    )
+    place = jnp.where(hour_slot == end, spare, hour_slot % RING)
+
+    pieces = lax.all_to_all(offered, "vec", 0, 0, axis_index_groups=rings, tiled=True)
+    picked = jnp.stack([lax.dynamic_index_in_dim(pieces, place[h], 0, keepdims=False) for h in range(2)])
     picked = picked + (sum(h[0, 0, 0] for h in halo) * 0).astype(picked.dtype)
     gathered = lax.all_gather(picked, "vec", axis=0, axis_index_groups=rings)
     own = [gathered[:, h] for h in range(2)]

time: 134 us -> 129 us (0.963)
  waiting for transfers between devices: 37.4 us -> 17.8 us
  starting transfers between devices: 44.5 us -> 60.3 us
  Pallas kernels: 11.6 us -> 7.66 us
  other arithmetic: 0.01 us -> 1.89 us
    all_to_all x1, waiting for transfers between devices: 25.8 us -> 0.01 us  [shards(): lax.all_to_all(offered, 'vec', 0, 0, axis_index_groups=rings, tiled=True)]
    ppermute x2, starting transfers between devices: 5.28 us -> 11.7 us  [shards(): other = [lax.ppermute(half, 'vec', swap) for half in own]]
    ppermute x0 -> x3, waiting for transfers between devices: none -> 6.24 us  [the longest x1 6.23 us: shards(): crossed = lax.ppermute(send, 'vec', [p for p in swap if p[0] != end])]
    ppermute x0 -> x3, starting transfers between devices: none -> 6 us  [the longest x1 3.1 us: shards(): crossed = lax.ppermute(send, 'vec', [p for p in swap if p[0] != end])]
    pallas_call x3, Pallas kernels: 10.5 us -> 7.51 us  [on_band(): pl.pallas_call(kernel, out_shape=outs, in_specs=[pl.BlockSpec(memory_spac...]
    select_n x0 -> x2, other arithmetic: none -> 1.88 us  [the longest x1 1.87 us: shards(): jnp.where((z == spare) & (asked == end), moved, jnp.where(from_column ==...]
    ppermute x2, starting transfers between devices: 19.3 us -> 21.1 us  [halos(): lax.ppermute(last, 'lat', northward)]
    all_to_all x1, starting transfers between devices: 16.1 us -> 17.7 us  [shards(): lax.all_to_all(offered, 'vec', 0, 0, axis_index_groups=rings, tiled=True)]
  transfers between devices with their start and end apart: 7 -> 10, of which waited for: 4 -> 4; matrix products, arithmetic and copies ran while one was open for 2% -> 2% of each run, Pallas kernels for 4% -> 3%
where the time goes in v4:
time: 129 us; the launch traced here: 128 us
  starting transfers between devices  60.3 us (47%)
  blocking collectives  29.3 us (23%)
  waiting for transfers between devices  17.8 us (14%)
  Pallas kernels  7.66 us (6%)
  between operations  6.47 us (5%)
  local copies, waits for them, and re-layouts  4.56 us (4%)
  other arithmetic  1.89 us (1%)
    all_gather x1, blocking collectives, shards(): gathered = lax.all_gather(picked, 'vec', axis=0, axis_index_groups=rings)  29.3 us
    ppermute x2, starting transfers between devices, halos(): lax.ppermute(last, 'lat', northward)  21.1 us
    all_to_all x1, starting transfers between devices, shards(): lax.all_to_all(offered, 'vec', 0, 0, axis_index_groups=rings, tiled=True)  17.7 us
    ppermute x2, starting transfers between devices, shards(): other = [lax.ppermute(half, 'vec', swap) for half in own]  11.7 us
    ppermute x2, waiting for transfers between devices, halos(): lax.ppermute(first, 'lat', southward)  7.67 us
    pallas_call x3, Pallas kernels, on_band(): pl.pallas_call(kernel, out_shape=outs, in_specs=[pl.BlockSpec(memory_spac...  7.51 us
    ppermute x1, waiting for transfers between devices, shards(): crossed = lax.ppermute(send, 'vec', [p for p in swap if p[0] != end])  6.23 us
    ppermute x2, waiting for transfers between devices, shards(): other = [lax.ppermute(half, 'vec', swap) for half in own]  3.93 us
  transfers between devices with their start and end apart: 10, of which 4 were waited for; matrix products, arithmetic and copies ran while one was open for 2% of the time, Pallas kernels for 3%

profile of v4, /device:TPU:25, one launch (start us, length us, event | category | flops | bytes accessed | tf_op | source)
XLA Modules:
  0.0 128.1 jit_solution(4306585831973100237)
XLA Ops:
  0.0 1.3 %copy-done.1 = bf16[1,3,8,24,720]{4,3,2,1,0:T(8,128)(2,1)S(1)} copy-done((bf16[1,3,8,24,720]{4,3,2,1,0:T(8,128)(2,1)S(1)}, bf16[1,3,8,24,720]{4,3,2,1,0:T(8,128)(2,1)}, u32[]{:S(2)}) %copy-start.1) | copy-done | bytes 829464
  1.5 1.4 %collective-permute-start.2 = (bf16[16,112,128]{2,1,0:T(8,128)(2,1)S(1)}, bf16[16,112,128]{2,1,0:T(8,128)(2,1)}, u32[]{:S(2)}, u32[]{:S(2)}) collective-permute-start(bf16[16,112,128]{2,1,0:T(8,128)(2,1)S(1)} %get-tuple-element.9), channel_id=1, source_target_pairs={{240,224},{241,225},{242,226},{243,227},{244,228},{245,229},{246,2... | collective-permute-start | bytes 1376264 | tf_op jit(solution)/shard_map/ppermute | solution.py:209
  2.9 3.1 %collective-permute-start.4 = (bf16[16,112,128]{2,1,0:T(8,128)(2,1)S(1)}, bf16[16,112,128]{2,1,0:T(8,128)(2,1)}, u32[]{:S(2)}, u32[]{:S(2)}) collective-permute-start(bf16[16,112,128]{2,1,0:T(8,128)(2,1)S(1)} %get-tuple-element.10), channel_id=1, source_target_pairs={{0,256},{16,272},{32,288},{48,304},{64,320},{80,336},{96,352},{112... | collective-permute-start | bytes 1376264 | tf_op jit(solution)/shard_map/ppermute | solution.py:206
  6.0 1.5 %collective-permute-start.3 = (bf16[16,112,128]{2,1,0:T(8,128)(2,1)S(1)}, bf16[16,112,128]{2,1,0:T(8,128)(2,1)}, u32[]{:S(2)}, u32[]{:S(2)}) collective-permute-start(bf16[16,112,128]{2,1,0:T(8,128)(2,1)S(1)} %get-tuple-element.10), channel_id=1, source_target_pairs={{240,480},{241,481},{242,482},{243,483},{244,484},{245,485},{246,4... | collective-permute-start | bytes 1376264 | tf_op jit(solution)/shard_map/ppermute | solution.py:210
  7.5 1.3 %fusion.3 = (s32[1]{0:T(128)}, s32[1]{0:T(128)}) fusion(s32[2]{0:T(128)} %param.6), kind=kLoop, calls=%fused_computation.15 | loop fusion | bytes 16 | tf_op jit(solution)/shard_map/slice | solution.py:212
  10.1 6.2 %collective-permute-done.4 = bf16[16,112,128]{2,1,0:T(8,128)(2,1)} collective-permute-done((bf16[16,112,128]{2,1,0:T(8,128)(2,1)S(1)}, bf16[16,112,128]{2,1,0:T(8,128)(2,1)}, u32[]{:S(2)}, u32[]{:S(2)}) %collective-permute-start.4) | collective-permute-done | bytes 458784 | tf_op jit(solution)/shard_map/ppermute | solution.py:206
  16.3 1.9 %select_select_fusion = bf16[16,112,128]{2,1,0:T(8,128)(2,1)} fusion(bf16[16,112,128]{2,1,0:T(8,128)(2,1)S(1)} %get-tuple-element.9, bf16[16,112,128]{2,1,0:T(8,128)(2,1)} %collective-permute-done.4, bf16[16,112,128]{2,1,0:T(8,128)(2,1)} %collective-permute-done.2, bf16[16,112,128]{2,1,0:T(8,128)(2,1)} %collective-permute-done.3, pred[]{:T(512)S(6)} %eq.26, ...), kind=kLoop, calls=%fused_computation.2 | loop fusion | flops 688128 | bytes 2293763 | tf_op jit(solution)/shard_map/jit(_where)/select_n | solution.py:215
  18.2 17.7 %all-to-all-start = ((bf16[16,112,128]{2,1,0:T(8,128)(2,1)}), bf16[16,112,128]{2,1,0:T(8,128)(2,1)S(1)}, u32[]{:S(2)}, u32[]{:S(2)}) async-start(bf16[16,112,128]{2,1,0:T(8,128)(2,1)} %select_select_fusion), calls=%async_computation | async-start | bytes 917504 | tf_op jit(solution)/shard_map/all_to_all | solution.py:220
  36.1 7.9 %collective-permute-start = (f32[4,8,720]{2,1,0:T(8,128)S(1)}, f32[4,8,720]{2,1,0:T(8,128)S(1)}, u32[]{:S(2)}, u32[]{:S(2)}) collective-permute-start(f32[4,8,720]{2,1,0:T(8,128)S(1)} %bitcast.19), channel_id=1, source_target_pairs={{0,1},{1,2},{2,3},{3,4},{4,5},{5,6},{6,7},{7,8},{8,9},{9,10},{10,1... | collective-permute-start | bytes 276488 | tf_op jit(solution)/shard_map/ppermute | solution.py:198
  44.0 1.9 %collective-permute-start.1 = (f32[4,8,720]{2,1,0:T(8,128)S(1)}, f32[4,8,720]{2,1,0:T(8,128)S(1)}, u32[]{:S(2)}, u32[]{:S(2)}) collective-permute-start(f32[4,8,720]{2,1,0:T(8,128)S(1)} %bitcast.20), channel_id=1, source_target_pairs={{1,0},{2,1},{3,2},{4,3},{5,4},{6,5},{7,6},{8,7},{9,8},{10,9},{11,1... | collective-permute-start | bytes 276488 | tf_op jit(solution)/shard_map/ppermute | solution.py:198
  46.0 0.6 fusion.2
  50.4 0.5 slice.40
  50.9 2.8 %collective-permute-done.1.north_ref = f32[4,8,720]{2,1,0:T(8,128)S(1)} collective-permute-done((f32[4,8,720]{2,1,0:T(8,128)S(1)}, f32[4,8,720]{2,1,0:T(8,128)S(1)}, u32[]{:S(2)}, u32[]{:S(2)}) %collective-permute-start.1) | collective-permute-done | bytes 92192 | tf_op jit(solution)/shard_map/ppermute | solution.py:198
  53.7 0.5 slice.41
  55.6 29.3 %all_gather.4 = bf16[16,2,112,128]{3,2,0,1:T(8,128)(2,1)S(1)} all-gather(bf16[1,2,112,128]{3,2,0,1:T(8,128)(2,1)S(1)} %maximum_add_fusion), channel_id=1, replica_groups={{0,16,32,48,64,80,96,112,128,144,160,176,192,208,224,240},{256,272,288,..., dimensions={0}, use_global_device_ids=true | all-gather | bytes 974848 | tf_op jit(solution)/shard_map/all_gather | solution.py:223
  85.0 9.7 %collective-permute-start.5 = (bf16[16,112,128]{2,1,0:T(8,128)(2,1)S(1)}, bf16[16,112,128]{2,1,0:T(8,128)(2,1)S(1)}, u32[]{:S(2)}, u32[]{:S(2)}) collective-permute-start(bf16[16,112,128]{2,1,0:T(8,128)(2,1)S(1)} %get-tuple-element.16.own_ref), channel_id=1, source_target_pairs={{0,256},{16,272},{32,288},{48,304},{64,320},{80,336},{96,352},{112... | collective-permute-start | bytes 1376264 | tf_op jit(solution)/shard_map/ppermute | solution.py:225
  94.7 1.9 %collective-permute-start.8 = (bf16[16,112,128]{2,1,0:T(8,128)(2,1)S(1)}, bf16[16,112,128]{2,1,0:T(8,128)(2,1)S(1)}, u32[]{:S(2)}, u32[]{:S(2)}) collective-permute-start(bf16[16,112,128]{2,1,0:T(8,128)(2,1)S(1)} %get-tuple-element.15.own_ref), channel_id=1, source_target_pairs={{0,256},{16,272},{32,288},{48,304},{64,320},{80,336},{96,352},{112... | collective-permute-start | bytes 1376264 | tf_op jit(solution)/shard_map/ppermute | solution.py:225
  96.6 3.9 %collective-permute-done.5.other_ref = bf16[16,112,128]{2,1,0:T(8,128)(2,1)S(1)} collective-permute-done((bf16[16,112,128]{2,1,0:T(8,128)(2,1)S(1)}, bf16[16,112,128]{2,1,0:T(8,128)(2,1)S(1)}, u32[]{:S(2)}, u32[]{:S(2)}) %collective-permute-start.5) | collective-permute-done | bytes 458784 | tf_op jit(solution)/shard_map/ppermute | solution.py:225
  100.6 0.5 edge_rows.1
  101.1 13.2 %collective-permute-start.6 = (f32[4,8,720]{2,1,0:T(8,128)S(1)}, f32[4,8,720]{2,1,0:T(8,128)S(1)}, u32[]{:S(2)}, u32[]{:S(2)}) collective-permute-start(f32[4,8,720]{2,1,0:T(8,128)S(1)} %get-tuple-element.11), channel_id=1, source_target_pairs={{0,1},{1,2},{2,3},{3,4},{4,5},{5,6},{6,7},{7,8},{8,9},{9,10},{10,1... | collective-permute-start | bytes 276488 | tf_op jit(solution)/shard_map/ppermute | solution.py:198
  114.3 1.9 %collective-permute-start.7 = (f32[4,8,720]{2,1,0:T(8,128)S(1)}, f32[4,8,720]{2,1,0:T(8,128)S(1)}, u32[]{:S(2)}, u32[]{:S(2)}) collective-permute-start(f32[4,8,720]{2,1,0:T(8,128)S(1)} %get-tuple-element.12), channel_id=1, source_target_pairs={{1,0},{2,1},{3,2},{4,3},{5,4},{6,5},{7,6},{8,7},{9,8},{10,9},{11,1... | collective-permute-start | bytes 276488 | tf_op jit(solution)/shard_map/ppermute | solution.py:198
  116.2 2.7 %one_hour.2.q_ref = f32[4,8,24,720]{3,2,1,0:T(8,128)S(1)} custom-call(s32[1]{0:T(128)} %bitcast.column_ref, f32[4,8,24,720]{3,2,1,0:T(8,128)S(1)} %copy-done, f32[4,8,720]{2,1,0:T(8,128)S(1)} %collective-permute-done.south_ref, f32[4,8,720]{2,1,0:T(8,128)S(1)} %collective-permute-done.1.north_ref, s32[24,720]{1,0:T(8,128)S(1)} %copy-done.2, ...), custom_call_target="tpu_custom_call" | custom-call | flops 11059200 | bytes 5594628 | tf_op jit(solution)/shard_map/one_hour/pallas_call | solution.py:164
  119.0 4.9 %collective-permute-done.7.north_ref = f32[4,8,720]{2,1,0:T(8,128)S(1)} collective-permute-done((f32[4,8,720]{2,1,0:T(8,128)S(1)}, f32[4,8,720]{2,1,0:T(8,128)S(1)}, u32[]{:S(2)}, u32[]{:S(2)}) %collective-permute-start.7) | collective-permute-done | bytes 92192 | tf_op jit(solution)/shard_map/ppermute | solution.py:198
  123.8 4.3 %one_hour.3 = f32[4,8,24,720]{3,2,1,0:T(8,128)} custom-call(s32[1]{0:T(128)} %bitcast.column_ref, f32[4,8,24,720]{3,2,1,0:T(8,128)S(1)} %one_hour.2.q_ref, f32[4,8,720]{2,1,0:T(8,128)S(1)} %collective-permute-done.6.south_ref, f32[4,8,720]{2,1,0:T(8,128)S(1)} %collective-permute-done.7.north_ref, s32[24,720]{1,0:T(8,128)S(1)} %copy-done.2, ...), custom_call_target="tpu_custom_call" | custom-call | flops 11059200 | bytes 5594628 | tf_op jit(solution)/shard_map/one_hour/pallas_call | solution.py:164
  (21 shorter events, 0.4 us)
Async XLA Ops:
  0.0 35.9 %copy-start = (f32[4,8,24,720]{3,2,1,0:T(8,128)S(1)}, f32[4,8,24,720]{3,2,1,0:T(8,128)}, u32[]{:S(2)}) copy-start(f32[4,8,24,720]{3,2,1,0:T(8,128)} %q_ref.3) | copy-start | bytes 6635524
  0.0 1.3 %copy-start.1 = (bf16[1,3,8,24,720]{4,3,2,1,0:T(8,128)(2,1)S(1)}, bf16[1,3,8,24,720]{4,3,2,1,0:T(8,128)(2,1)}, u32[]{:S(2)}) copy-start(bf16[1,3,8,24,720]{4,3,2,1,0:T(8,128)(2,1)} %field_ref.1) | copy-start | bytes 2488324
  1.3 44.6 %copy-start.3 = (s32[2]{0:T(128)S(1)}, s32[2]{0:T(128)}, u32[]{:S(2)}) copy-start(s32[2]{0:T(128)} %param.6) | copy-start | bytes 28
  1.5 8.6 %collective-permute-start.2 = (bf16[16,112,128]{2,1,0:T(8,128)(2,1)S(1)}, bf16[16,112,128]{2,1,0:T(8,128)(2,1)}, u32[]{:S(2)}, u32[]{:S(2)}) collective-permute-start(bf16[16,112,128]{2,1,0:T(8,128)(2,1)S(1)} %get-tuple-element.9), channel_id=1, source_target_pairs={{240,224},{241,225},{242,226},{243,227},{244,228},{245,229},{246,2... | collective-permute-start | bytes 1376264 | tf_op jit(solution)/shard_map/ppermute | solution.py:209
  2.9 13.4 %collective-permute-start.4 = (bf16[16,112,128]{2,1,0:T(8,128)(2,1)S(1)}, bf16[16,112,128]{2,1,0:T(8,128)(2,1)}, u32[]{:S(2)}, u32[]{:S(2)}) collective-permute-start(bf16[16,112,128]{2,1,0:T(8,128)(2,1)S(1)} %get-tuple-element.10), channel_id=1, source_target_pairs={{0,256},{16,272},{32,288},{48,304},{64,320},{80,336},{96,352},{112... | collective-permute-start | bytes 1376264 | tf_op jit(solution)/shard_map/ppermute | solution.py:206
  6.0 10.3 %collective-permute-start.3 = (bf16[16,112,128]{2,1,0:T(8,128)(2,1)S(1)}, bf16[16,112,128]{2,1,0:T(8,128)(2,1)}, u32[]{:S(2)}, u32[]{:S(2)}) collective-permute-start(bf16[16,112,128]{2,1,0:T(8,128)(2,1)S(1)} %get-tuple-element.10), channel_id=1, source_target_pairs={{240,480},{241,481},{242,482},{243,483},{244,484},{245,485},{246,4... | collective-permute-start | bytes 1376264 | tf_op jit(solution)/shard_map/ppermute | solution.py:210
  18.2 82.4 %copy-start.2 = (s32[24,720]{1,0:T(8,128)S(1)}, s32[24,720]{1,0:T(8,128)}, u32[]{:S(2)}) copy-start(s32[24,720]{1,0:T(8,128)} %mask_ref.5) | copy-start | bytes 207364
  18.2 37.3 %all-to-all-start = ((bf16[16,112,128]{2,1,0:T(8,128)(2,1)}), bf16[16,112,128]{2,1,0:T(8,128)(2,1)S(1)}, u32[]{:S(2)}, u32[]{:S(2)}) async-start(bf16[16,112,128]{2,1,0:T(8,128)(2,1)} %select_select_fusion), calls=%async_computation | async-start | bytes 917504 | tf_op jit(solution)/shard_map/all_to_all | solution.py:220
  36.1 14.3 %collective-permute-start = (f32[4,8,720]{2,1,0:T(8,128)S(1)}, f32[4,8,720]{2,1,0:T(8,128)S(1)}, u32[]{:S(2)}, u32[]{:S(2)}) collective-permute-start(f32[4,8,720]{2,1,0:T(8,128)S(1)} %bitcast.19), channel_id=1, source_target_pairs={{0,1},{1,2},{2,3},{3,4},{4,5},{5,6},{6,7},{7,8},{8,9},{9,10},{10,1... | collective-permute-start | bytes 276488 | tf_op jit(solution)/shard_map/ppermute | solution.py:198
  44.0 9.7 %collective-permute-start.1 = (f32[4,8,720]{2,1,0:T(8,128)S(1)}, f32[4,8,720]{2,1,0:T(8,128)S(1)}, u32[]{:S(2)}, u32[]{:S(2)}) collective-permute-start(f32[4,8,720]{2,1,0:T(8,128)S(1)} %bitcast.20), channel_id=1, source_target_pairs={{1,0},{2,1},{3,2},{4,3},{5,4},{6,5},{7,6},{8,7},{9,8},{10,9},{11,1... | collective-permute-start | bytes 276488 | tf_op jit(solution)/shard_map/ppermute | solution.py:198
  85.0 15.6 %collective-permute-start.5 = (bf16[16,112,128]{2,1,0:T(8,128)(2,1)S(1)}, bf16[16,112,128]{2,1,0:T(8,128)(2,1)S(1)}, u32[]{:S(2)}, u32[]{:S(2)}) collective-permute-start(bf16[16,112,128]{2,1,0:T(8,128)(2,1)S(1)} %get-tuple-element.16.own_ref), channel_id=1, source_target_pairs={{0,256},{16,272},{32,288},{48,304},{64,320},{80,336},{96,352},{112... | collective-permute-start | bytes 1376264 | tf_op jit(solution)/shard_map/ppermute | solution.py:225
  94.7 24.2 %collective-permute-start.8 = (bf16[16,112,128]{2,1,0:T(8,128)(2,1)S(1)}, bf16[16,112,128]{2,1,0:T(8,128)(2,1)S(1)}, u32[]{:S(2)}, u32[]{:S(2)}) collective-permute-start(bf16[16,112,128]{2,1,0:T(8,128)(2,1)S(1)} %get-tuple-element.15.own_ref), channel_id=1, source_target_pairs={{0,256},{16,272},{32,288},{48,304},{64,320},{80,336},{96,352},{112... | collective-permute-start | bytes 1376264 | tf_op jit(solution)/shard_map/ppermute | solution.py:225
  101.1 17.9 %collective-permute-start.6 = (f32[4,8,720]{2,1,0:T(8,128)S(1)}, f32[4,8,720]{2,1,0:T(8,128)S(1)}, u32[]{:S(2)}, u32[]{:S(2)}) collective-permute-start(f32[4,8,720]{2,1,0:T(8,128)S(1)} %get-tuple-element.11), channel_id=1, source_target_pairs={{0,1},{1,2},{2,3},{3,4},{4,5},{5,6},{6,7},{7,8},{8,9},{9,10},{10,1... | collective-permute-start | bytes 276488 | tf_op jit(solution)/shard_map/ppermute | solution.py:198
  114.3 9.5 %collective-permute-start.7 = (f32[4,8,720]{2,1,0:T(8,128)S(1)}, f32[4,8,720]{2,1,0:T(8,128)S(1)}, u32[]{:S(2)}, u32[]{:S(2)}) collective-permute-start(f32[4,8,720]{2,1,0:T(8,128)S(1)} %get-tuple-element.12), channel_id=1, source_target_pairs={{1,0},{2,1},{3,2},{4,3},{5,4},{6,5},{7,6},{8,7},{9,8},{10,9},{11,1... | collective-permute-start | bytes 276488 | tf_op jit(solution)/shard_map/ppermute | solution.py:198

commit v5 on v4

--- a/solution.py
+++ b/solution.py
@@ -201,21 +201,15 @@
     halo = halos(perturb[:, :, 0], perturb[:, :, -1])
 
     end, last_hour = RING - 1, COLUMNS * RING - 1
-    spare = end - 1
     keep, send = pack(which, trajectory)
-    crossed = lax.ppermute(send, "vec", [p for p in swap if p[0] != end])
-    moved = jnp.where(
-        column == 0,
-        lax.ppermute(keep, "vec", [(end, spare)]),
-        lax.ppermute(send, "vec", [(end, RING + spare)]),
-    )
+    crossed = lax.ppermute(send, "vec", swap)
+    moved = lax.ppermute(keep, "vec", [(c * RING + end, c * RING + end - 1) for c in range(COLUMNS)])
     asked = hour_slot[0] + hour_slot[1] - last_hour
+    both = asked == end
     z = lax.axis_index("vec") % RING
-    from_column = jnp.where(z == end, 1, asked // RING)
-    offered = jnp.where(
-        (z == spare) & (asked == end), moved, jnp.where(from_column == column, keep, crossed)
-    )
-    place = jnp.where(hour_slot == end, spare, hour_slot % RING)
+    own_there = jnp.where(z == end, (column == 1) & ~both, asked // RING == column)
+    offered = jnp.where((z == end - 1) & both, moved, jnp.where(own_there, keep, crossed))
+    place = jnp.where(both & (hour_slot // RING == column), end - 1, hour_slot % RING)
 
     pieces = lax.all_to_all(offered, "vec", 0, 0, axis_index_groups=rings, tiled=True)
     picked = jnp.stack([lax.dynamic_index_in_dim(pieces, place[h], 0, keepdims=False) for h in range(2)])

time: 129 us -> 124 us (0.961)
  starting transfers between devices: 60.3 us -> 49.9 us
  blocking collectives: 29.3 us -> 32.5 us
  waiting for transfers between devices: 17.8 us -> 20.4 us
    ppermute x2, starting transfers between devices: 11.7 us -> 5.28 us  [shards(): other = [lax.ppermute(half, 'vec', swap) for half in own]]
    all_gather x1, blocking collectives: 29.3 us -> 32.5 us  [shards(): gathered = lax.all_gather(picked, 'vec', axis=0, axis_index_groups=rings)]
    all_to_all x1, starting transfers between devices: 17.7 us -> 15 us  [shards(): lax.all_to_all(offered, 'vec', 0, 0, axis_index_groups=rings, tiled=True)]
    all_to_all x1, waiting for transfers between devices: 0.01 us -> 1.99 us  [shards(): lax.all_to_all(offered, 'vec', 0, 0, axis_index_groups=rings, tiled=True)]
    ppermute x3 -> x2, starting transfers between devices: 6 us -> 4.55 us  [the longest x1 3.11 us: shards(): crossed = lax.ppermute(send, 'vec', swap)]
    ppermute x3 -> x2, waiting for transfers between devices: 6.24 us -> 6.24 us  [the longest x1 6.24 us: shards(): crossed = lax.ppermute(send, 'vec', swap)]
  transfers between devices with their start and end apart: 10 -> 9, of which waited for: 4 -> 5; matrix products, arithmetic and copies ran while one was open for 2% -> 3% of each run, Pallas kernels for 3% -> 3%
where the time goes in v5:
time: 124 us; the launch traced here: 123 us
  starting transfers between devices  49.9 us (40%)
  blocking collectives  32.5 us (26%)
  waiting for transfers between devices  20.4 us (16%)
  Pallas kernels  7.66 us (6%)
  between operations  6.2 us (5%)
  local copies, waits for them, and re-layouts  4.5 us (4%)
  other arithmetic  1.87 us (2%)
    all_gather x1, blocking collectives, shards(): gathered = lax.all_gather(picked, 'vec', axis=0, axis_index_groups=rings)  32.5 us
    ppermute x2, starting transfers between devices, halos(): lax.ppermute(last, 'lat', northward)  21.2 us
    all_to_all x1, starting transfers between devices, shards(): lax.all_to_all(offered, 'vec', 0, 0, axis_index_groups=rings, tiled=True)  15 us
    ppermute x2, waiting for transfers between devices, halos(): lax.ppermute(first, 'lat', southward)  7.95 us
    pallas_call x3, Pallas kernels, on_band(): pl.pallas_call(kernel, out_shape=outs, in_specs=[pl.BlockSpec(memory_spac...  7.51 us
    ppermute x1, waiting for transfers between devices, shards(): crossed = lax.ppermute(send, 'vec', swap)  6.24 us
    ppermute x2, starting transfers between devices, shards(): other = [lax.ppermute(half, 'vec', swap) for half in own]  5.28 us
    ppermute x2, waiting for transfers between devices, shards(): other = [lax.ppermute(half, 'vec', swap) for half in own]  4.22 us
  transfers between devices with their start and end apart: 9, of which 5 were waited for; matrix products, arithmetic and copies ran while one was open for 3% of the time, Pallas kernels for 3%

profile of v5, /device:TPU:25, one launch (start us, length us, event | category | flops | bytes accessed | tf_op | source)
XLA Modules:
  0.0 123.1 jit_solution(1681882635760855562)
XLA Ops:
  0.0 1.3 %copy-done.1 = bf16[1,3,8,24,720]{4,3,2,1,0:T(8,128)(2,1)S(1)} copy-done((bf16[1,3,8,24,720]{4,3,2,1,0:T(8,128)(2,1)S(1)}, bf16[1,3,8,24,720]{4,3,2,1,0:T(8,128)(2,1)}, u32[]{:S(2)}) %copy-start.1) | copy-done | bytes 829464
  1.5 3.1 %collective-permute-start.3 = (bf16[16,112,128]{2,1,0:T(8,128)(2,1)S(1)}, bf16[16,112,128]{2,1,0:T(8,128)(2,1)}, u32[]{:S(2)}, u32[]{:S(2)}) collective-permute-start(bf16[16,112,128]{2,1,0:T(8,128)(2,1)S(1)} %get-tuple-element.10), channel_id=1, source_target_pairs={{0,256},{16,272},{32,288},{48,304},{64,320},{80,336},{96,352},{112... | collective-permute-start | bytes 1376264 | tf_op jit(solution)/shard_map/ppermute | solution.py:205
  4.6 1.4 %collective-permute-start.2 = (bf16[16,112,128]{2,1,0:T(8,128)(2,1)S(1)}, bf16[16,112,128]{2,1,0:T(8,128)(2,1)}, u32[]{:S(2)}, u32[]{:S(2)}) collective-permute-start(bf16[16,112,128]{2,1,0:T(8,128)(2,1)S(1)} %get-tuple-element.9), channel_id=1, source_target_pairs={{240,224},{496,480},{241,225},{497,481},{242,226},{498,482},{243,2... | collective-permute-start | bytes 1376264 | tf_op jit(solution)/shard_map/ppermute | solution.py:206
  6.0 1.3 %fusion.2 = (s32[1]{0:T(128)}, s32[1]{0:T(128)}) fusion(s32[2]{0:T(128)} %param.6), kind=kLoop, calls=%fused_computation.16 | loop fusion | bytes 16 | tf_op jit(solution)/shard_map/slice | solution.py:207
  8.6 6.2 %collective-permute-done.3 = bf16[16,112,128]{2,1,0:T(8,128)(2,1)} collective-permute-done((bf16[16,112,128]{2,1,0:T(8,128)(2,1)S(1)}, bf16[16,112,128]{2,1,0:T(8,128)(2,1)}, u32[]{:S(2)}, u32[]{:S(2)}) %collective-permute-start.3) | collective-permute-done | bytes 458784 | tf_op jit(solution)/shard_map/ppermute | solution.py:205
  14.9 1.9 %select_select_fusion = bf16[16,112,128]{2,1,0:T(8,128)(2,1)} fusion(bf16[16,112,128]{2,1,0:T(8,128)(2,1)} %collective-permute-done.2, bf16[16,112,128]{2,1,0:T(8,128)(2,1)S(1)} %get-tuple-element.9, bf16[16,112,128]{2,1,0:T(8,128)(2,1)} %collective-permute-done.3, pred[]{:T(512)S(6)} %select_n.58, pred[]{:T(512)S(6)} %and.39), kind=kLoop, calls=%fused_computation.2 | loop fusion | flops 458752 | bytes 1835010 | tf_op jit(solution)/shard_map/jit(_where)/select_n | solution.py:211
  16.7 15.0 %all-to-all-start = ((bf16[16,112,128]{2,1,0:T(8,128)(2,1)}), bf16[16,112,128]{2,1,0:T(8,128)(2,1)S(1)}, u32[]{:S(2)}, u32[]{:S(2)}) async-start(bf16[16,112,128]{2,1,0:T(8,128)(2,1)} %select_select_fusion), calls=%async_computation | async-start | bytes 917504 | tf_op jit(solution)/shard_map/all_to_all | solution.py:214
  32.0 6.0 %collective-permute-start = (f32[4,8,720]{2,1,0:T(8,128)S(1)}, f32[4,8,720]{2,1,0:T(8,128)S(1)}, u32[]{:S(2)}, u32[]{:S(2)}) collective-permute-start(f32[4,8,720]{2,1,0:T(8,128)S(1)} %bitcast.19), channel_id=1, source_target_pairs={{0,1},{1,2},{2,3},{3,4},{4,5},{5,6},{6,7},{7,8},{8,9},{9,10},{10,1... | collective-permute-start | bytes 276488 | tf_op jit(solution)/shard_map/ppermute | solution.py:198
  38.0 1.9 %collective-permute-start.1 = (f32[4,8,720]{2,1,0:T(8,128)S(1)}, f32[4,8,720]{2,1,0:T(8,128)S(1)}, u32[]{:S(2)}, u32[]{:S(2)}) collective-permute-start(f32[4,8,720]{2,1,0:T(8,128)S(1)} %bitcast.20), channel_id=1, source_target_pairs={{1,0},{2,1},{3,2},{4,3},{5,4},{6,5},{7,6},{8,7},{9,8},{10,9},{11,1... | collective-permute-start | bytes 276488 | tf_op jit(solution)/shard_map/ppermute | solution.py:198
  40.0 0.6 fusion.1
  44.1 0.5 slice.40
  44.6 3.1 %collective-permute-done.1.north_ref = f32[4,8,720]{2,1,0:T(8,128)S(1)} collective-permute-done((f32[4,8,720]{2,1,0:T(8,128)S(1)}, f32[4,8,720]{2,1,0:T(8,128)S(1)}, u32[]{:S(2)}, u32[]{:S(2)}) %collective-permute-start.1) | collective-permute-done | bytes 92192 | tf_op jit(solution)/shard_map/ppermute | solution.py:198
  47.7 0.5 slice.41
  49.5 2.0 %all-to-all-done = bf16[16,112,128]{2,1,0:T(8,128)(2,1)S(1)} async-done(((bf16[16,112,128]{2,1,0:T(8,128)(2,1)}), bf16[16,112,128]{2,1,0:T(8,128)(2,1)S(1)}, u32[]{:S(2)}, u32[]{:S(2)}) %all-to-all-start) | async-done | bytes 458784 | tf_op jit(solution)/shard_map/all_to_all | solution.py:214
  51.5 32.5 %all_gather.4 = bf16[16,2,112,128]{3,2,0,1:T(8,128)(2,1)S(1)} all-gather(bf16[1,2,112,128]{3,2,0,1:T(8,128)(2,1)S(1)} %maximum_add_fusion), channel_id=1, replica_groups={{0,16,32,48,64,80,96,112,128,144,160,176,192,208,224,240},{256,272,288,..., dimensions={0}, use_global_device_ids=true | all-gather | bytes 974848 | tf_op jit(solution)/shard_map/all_gather | solution.py:217
  84.1 2.1 %collective-permute-start.4 = (bf16[16,112,128]{2,1,0:T(8,128)(2,1)S(1)}, bf16[16,112,128]{2,1,0:T(8,128)(2,1)S(1)}, u32[]{:S(2)}, u32[]{:S(2)}) collective-permute-start(bf16[16,112,128]{2,1,0:T(8,128)(2,1)S(1)} %get-tuple-element.16.own_ref), channel_id=1, source_target_pairs={{0,256},{16,272},{32,288},{48,304},{64,320},{80,336},{96,352},{112... | collective-permute-start | bytes 1376264 | tf_op jit(solution)/shard_map/ppermute | solution.py:219
  86.2 3.2 %collective-permute-start.7 = (bf16[16,112,128]{2,1,0:T(8,128)(2,1)S(1)}, bf16[16,112,128]{2,1,0:T(8,128)(2,1)S(1)}, u32[]{:S(2)}, u32[]{:S(2)}) collective-permute-start(bf16[16,112,128]{2,1,0:T(8,128)(2,1)S(1)} %get-tuple-element.15.own_ref), channel_id=1, source_target_pairs={{0,256},{16,272},{32,288},{48,304},{64,320},{80,336},{96,352},{112... | collective-permute-start | bytes 1376264 | tf_op jit(solution)/shard_map/ppermute | solution.py:219
  89.4 4.2 %collective-permute-done.4.other_ref = bf16[16,112,128]{2,1,0:T(8,128)(2,1)S(1)} collective-permute-done((bf16[16,112,128]{2,1,0:T(8,128)(2,1)S(1)}, bf16[16,112,128]{2,1,0:T(8,128)(2,1)S(1)}, u32[]{:S(2)}, u32[]{:S(2)}) %collective-permute-start.4) | collective-permute-done | bytes 458784 | tf_op jit(solution)/shard_map/ppermute | solution.py:219
  93.6 0.5 edge_rows.1
  94.1 15.2 %collective-permute-start.5 = (f32[4,8,720]{2,1,0:T(8,128)S(1)}, f32[4,8,720]{2,1,0:T(8,128)S(1)}, u32[]{:S(2)}, u32[]{:S(2)}) collective-permute-start(f32[4,8,720]{2,1,0:T(8,128)S(1)} %get-tuple-element.11), channel_id=1, source_target_pairs={{0,1},{1,2},{2,3},{3,4},{4,5},{5,6},{6,7},{7,8},{8,9},{9,10},{10,1... | collective-permute-start | bytes 276488 | tf_op jit(solution)/shard_map/ppermute | solution.py:198
  109.3 1.9 %collective-permute-start.6 = (f32[4,8,720]{2,1,0:T(8,128)S(1)}, f32[4,8,720]{2,1,0:T(8,128)S(1)}, u32[]{:S(2)}, u32[]{:S(2)}) collective-permute-start(f32[4,8,720]{2,1,0:T(8,128)S(1)} %get-tuple-element.12), channel_id=1, source_target_pairs={{1,0},{2,1},{3,2},{4,3},{5,4},{6,5},{7,6},{8,7},{9,8},{10,9},{11,1... | collective-permute-start | bytes 276488 | tf_op jit(solution)/shard_map/ppermute | solution.py:198
  111.2 2.7 %one_hour.2.q_ref = f32[4,8,24,720]{3,2,1,0:T(8,128)S(1)} custom-call(s32[1]{0:T(128)} %bitcast.column_ref, f32[4,8,24,720]{3,2,1,0:T(8,128)S(1)} %copy-done, f32[4,8,720]{2,1,0:T(8,128)S(1)} %collective-permute-done.south_ref, f32[4,8,720]{2,1,0:T(8,128)S(1)} %collective-permute-done.1.north_ref, s32[24,720]{1,0:T(8,128)S(1)} %copy-done.2, ...), custom_call_target="tpu_custom_call" | custom-call | flops 11059200 | bytes 5594628 | tf_op jit(solution)/shard_map/one_hour/pallas_call | solution.py:164
  114.0 4.9 %collective-permute-done.6.north_ref = f32[4,8,720]{2,1,0:T(8,128)S(1)} collective-permute-done((f32[4,8,720]{2,1,0:T(8,128)S(1)}, f32[4,8,720]{2,1,0:T(8,128)S(1)}, u32[]{:S(2)}, u32[]{:S(2)}) %collective-permute-start.6) | collective-permute-done | bytes 92192 | tf_op jit(solution)/shard_map/ppermute | solution.py:198
  118.8 4.3 %one_hour.3 = f32[4,8,24,720]{3,2,1,0:T(8,128)} custom-call(s32[1]{0:T(128)} %bitcast.column_ref, f32[4,8,24,720]{3,2,1,0:T(8,128)S(1)} %one_hour.2.q_ref, f32[4,8,720]{2,1,0:T(8,128)S(1)} %collective-permute-done.5.south_ref, f32[4,8,720]{2,1,0:T(8,128)S(1)} %collective-permute-done.6.north_ref, s32[24,720]{1,0:T(8,128)S(1)} %copy-done.2, ...), custom_call_target="tpu_custom_call" | custom-call | flops 11059200 | bytes 5594628 | tf_op jit(solution)/shard_map/one_hour/pallas_call | solution.py:164
  (19 shorter events, 0.4 us)
Async XLA Ops:
  0.0 31.8 %copy-start = (f32[4,8,24,720]{3,2,1,0:T(8,128)S(1)}, f32[4,8,24,720]{3,2,1,0:T(8,128)}, u32[]{:S(2)}) copy-start(f32[4,8,24,720]{3,2,1,0:T(8,128)} %q_ref.3) | copy-start | bytes 6635524
  0.0 1.3 %copy-start.1 = (bf16[1,3,8,24,720]{4,3,2,1,0:T(8,128)(2,1)S(1)}, bf16[1,3,8,24,720]{4,3,2,1,0:T(8,128)(2,1)}, u32[]{:S(2)}) copy-start(bf16[1,3,8,24,720]{4,3,2,1,0:T(8,128)(2,1)} %field_ref.1) | copy-start | bytes 2488324
  1.3 38.6 %copy-start.3 = (s32[2]{0:T(128)S(1)}, s32[2]{0:T(128)}, u32[]{:S(2)}) copy-start(s32[2]{0:T(128)} %param.6) | copy-start | bytes 28
  1.5 13.4 %collective-permute-start.3 = (bf16[16,112,128]{2,1,0:T(8,128)(2,1)S(1)}, bf16[16,112,128]{2,1,0:T(8,128)(2,1)}, u32[]{:S(2)}, u32[]{:S(2)}) collective-permute-start(bf16[16,112,128]{2,1,0:T(8,128)(2,1)S(1)} %get-tuple-element.10), channel_id=1, source_target_pairs={{0,256},{16,272},{32,288},{48,304},{64,320},{80,336},{96,352},{112... | collective-permute-start | bytes 1376264 | tf_op jit(solution)/shard_map/ppermute | solution.py:205
  4.6 10.3 %collective-permute-start.2 = (bf16[16,112,128]{2,1,0:T(8,128)(2,1)S(1)}, bf16[16,112,128]{2,1,0:T(8,128)(2,1)}, u32[]{:S(2)}, u32[]{:S(2)}) collective-permute-start(bf16[16,112,128]{2,1,0:T(8,128)(2,1)S(1)} %get-tuple-element.9), channel_id=1, source_target_pairs={{240,224},{496,480},{241,225},{497,481},{242,226},{498,482},{243,2... | collective-permute-start | bytes 1376264 | tf_op jit(solution)/shard_map/ppermute | solution.py:206
  16.7 76.8 %copy-start.2 = (s32[24,720]{1,0:T(8,128)S(1)}, s32[24,720]{1,0:T(8,128)}, u32[]{:S(2)}) copy-start(s32[24,720]{1,0:T(8,128)} %mask_ref.5) | copy-start | bytes 207364
  16.7 34.7 %all-to-all-start = ((bf16[16,112,128]{2,1,0:T(8,128)(2,1)}), bf16[16,112,128]{2,1,0:T(8,128)(2,1)S(1)}, u32[]{:S(2)}, u32[]{:S(2)}) async-start(bf16[16,112,128]{2,1,0:T(8,128)(2,1)} %select_select_fusion), calls=%async_computation | async-start | bytes 917504 | tf_op jit(solution)/shard_map/all_to_all | solution.py:214
  32.0 12.2 %collective-permute-start = (f32[4,8,720]{2,1,0:T(8,128)S(1)}, f32[4,8,720]{2,1,0:T(8,128)S(1)}, u32[]{:S(2)}, u32[]{:S(2)}) collective-permute-start(f32[4,8,720]{2,1,0:T(8,128)S(1)} %bitcast.19), channel_id=1, source_target_pairs={{0,1},{1,2},{2,3},{3,4},{4,5},{5,6},{6,7},{7,8},{8,9},{9,10},{10,1... | collective-permute-start | bytes 276488 | tf_op jit(solution)/shard_map/ppermute | solution.py:198
  38.0 9.7 %collective-permute-start.1 = (f32[4,8,720]{2,1,0:T(8,128)S(1)}, f32[4,8,720]{2,1,0:T(8,128)S(1)}, u32[]{:S(2)}, u32[]{:S(2)}) collective-permute-start(f32[4,8,720]{2,1,0:T(8,128)S(1)} %bitcast.20), channel_id=1, source_target_pairs={{1,0},{2,1},{3,2},{4,3},{5,4},{6,5},{7,6},{8,7},{9,8},{10,9},{11,1... | collective-permute-start | bytes 276488 | tf_op jit(solution)/shard_map/ppermute | solution.py:198
  84.1 9.5 %collective-permute-start.4 = (bf16[16,112,128]{2,1,0:T(8,128)(2,1)S(1)}, bf16[16,112,128]{2,1,0:T(8,128)(2,1)S(1)}, u32[]{:S(2)}, u32[]{:S(2)}) collective-permute-start(bf16[16,112,128]{2,1,0:T(8,128)(2,1)S(1)} %get-tuple-element.16.own_ref), channel_id=1, source_target_pairs={{0,256},{16,272},{32,288},{48,304},{64,320},{80,336},{96,352},{112... | collective-permute-start | bytes 1376264 | tf_op jit(solution)/shard_map/ppermute | solution.py:219
  86.2 27.8 %collective-permute-start.7 = (bf16[16,112,128]{2,1,0:T(8,128)(2,1)S(1)}, bf16[16,112,128]{2,1,0:T(8,128)(2,1)S(1)}, u32[]{:S(2)}, u32[]{:S(2)}) collective-permute-start(bf16[16,112,128]{2,1,0:T(8,128)(2,1)S(1)} %get-tuple-element.15.own_ref), channel_id=1, source_target_pairs={{0,256},{16,272},{32,288},{48,304},{64,320},{80,336},{96,352},{112... | collective-permute-start | bytes 1376264 | tf_op jit(solution)/shard_map/ppermute | solution.py:219
  94.1 19.9 %collective-permute-start.5 = (f32[4,8,720]{2,1,0:T(8,128)S(1)}, f32[4,8,720]{2,1,0:T(8,128)S(1)}, u32[]{:S(2)}, u32[]{:S(2)}) collective-permute-start(f32[4,8,720]{2,1,0:T(8,128)S(1)} %get-tuple-element.11), channel_id=1, source_target_pairs={{0,1},{1,2},{2,3},{3,4},{4,5},{5,6},{6,7},{7,8},{8,9},{9,10},{10,1... | collective-permute-start | bytes 276488 | tf_op jit(solution)/shard_map/ppermute | solution.py:198
  109.3 9.5 %collective-permute-start.6 = (f32[4,8,720]{2,1,0:T(8,128)S(1)}, f32[4,8,720]{2,1,0:T(8,128)S(1)}, u32[]{:S(2)}, u32[]{:S(2)}) collective-permute-start(f32[4,8,720]{2,1,0:T(8,128)S(1)} %get-tuple-element.12), channel_id=1, source_target_pairs={{1,0},{2,1},{3,2},{4,3},{5,4},{6,5},{7,6},{8,7},{9,8},{10,9},{11,1... | collective-permute-start | bytes 276488 | tf_op jit(solution)/shard_map/ppermute | solution.py:198

commit v6 on v5

--- a/solution.py
+++ b/solution.py
@@ -35,11 +35,11 @@
     return parts
 
 
-def pack_kernel(column_ref, field_ref, keep_ref, send_ref):
+def pack_kernel(place_ref, field_ref, keep_ref, send_ref):
     _, levs, rows, lon = field_ref.shape[1:]
     for own in range(COLUMNS):
 
-        @pl.when(column_ref[0] == own)
+        @pl.when(place_ref[0] == own)
         def _():
             for level in range(levs):
                 for half in range(2):
@@ -51,7 +51,7 @@
                         ]
 
 
-def pack(column, trajectory):
+def pack(place, trajectory):
     half = jax.ShapeDtypeStruct((RING, PIECE, LANES), trajectory.dtype)
     vmem = pl.BlockSpec(memory_space=pltpu.VMEM)
     return pl.pallas_call(
@@ -61,7 +61,7 @@
         out_specs=(vmem, vmem),
         compiler_params=pltpu.CompilerParams(vmem_limit_bytes=VMEM_LIMIT),
         name="pack",
-    )(column, trajectory)
+    )(place, trajectory)
 
 
 def lanes_next(x):
@@ -90,17 +90,22 @@
     return (wc * c + we * lanes_next(c) + ww * lanes_prev(c)) + (wn * n + ws * s + wl * (u + b))
 
 
+def neighbours(place_ref, near, far):
+    odd = place_ref[1] == 1
+    return jnp.where(odd, near, far), jnp.where(odd, far, near)
+
+
 def rows_kernel(
-    column_ref, q_ref, south_ref, north_ref, mask_ref, own_ref, other_ref, first_ref, last_ref, field_ref
+    place_ref, q_ref, near_ref, far_ref, mask_ref, own_ref, other_ref, to_near_ref, to_far_ref, field_ref
 ):
     vecs, levs, rows, lon = q_ref.shape
     lev = lax.broadcasted_iota(jnp.int32, (levs, lon), 0)
-    own_column = column_ref[0]
+    own_column, odd = place_ref[0], place_ref[1]
 
     def row_of(v, r):
         return jnp.concatenate([q_ref[v, z, r : r + 1] for z in range(levs)], axis=0)
 
-    for out_ref, r, step in ((first_ref, 0, 1), (last_ref, rows - 1, -1)):
+    for r, step in ((0, 1), (rows - 1, -1)):
         for own in range(COLUMNS):
 
             @pl.when(own_column == own)
@@ -116,21 +121,31 @@
                                 field_ref[k, z : z + 1, tile * LANES : (tile + 1) * LANES] = eight[i : i + 1]
 
         weight = weights(*(field_ref[k, :, :lon] for k in range(FIELDS)), mask_ref[r : r + 1].astype(jnp.float32))
+        to_near = odd == (1 if r == 0 else 0)
         for v in range(vecs):
+            south, north = neighbours(place_ref, near_ref[v], far_ref[v])
             c, inner = row_of(v, r), row_of(v, r + step)
-            n, s = (inner, south_ref[v]) if r == 0 else (north_ref[v], inner)
+            n, s = (inner, south) if r == 0 else (north, inner)
             u = jnp.where(lev == 0, c, pltpu.roll(c, 1, 0))
             b = jnp.where(lev == levs - 1, c, pltpu.roll(c, levs - 1, 0))
-            out_ref[v] = advance(c, n, s, u, b, weight)
+            new = advance(c, n, s, u, b, weight)
+
+            @pl.when(to_near)
+            def _():
+                to_near_ref[v] = new
+
+            @pl.when(jnp.logical_not(to_near))
+            def _():
+                to_far_ref[v] = new
 
 
 def hour_kernel(
-    column_ref, q_ref, south_ref, north_ref, mask_ref, own_ref, other_ref, out_ref, field_ref
+    place_ref, q_ref, near_ref, far_ref, mask_ref, own_ref, other_ref, out_ref, field_ref
 ):
     vecs, levs, rows, lon = q_ref.shape
     row = lax.broadcasted_iota(jnp.int32, (rows, lon), 0)
     mask = mask_ref[...].astype(jnp.float32)
-    own_column = column_ref[0]
+    own_column = place_ref[0]
 
     def level_step(level, carry):
         for own in range(COLUMNS):
@@ -149,8 +164,9 @@
         low = jnp.minimum(level + 1, levs - 1)
         for v in range(vecs):
             c = q_ref[v, level]
-            n = jnp.where(row == rows - 1, north_ref[v, pl.ds(level, 1)], pltpu.roll(c, rows - 1, 0))
-            s = jnp.where(row == 0, south_ref[v, pl.ds(level, 1)], pltpu.roll(c, 1, 0))
+            south, north = neighbours(place_ref, near_ref[v, pl.ds(level, 1)], far_ref[v, pl.ds(level, 1)])
+            n = jnp.where(row == rows - 1, north, pltpu.roll(c, rows - 1, 0))
+            s = jnp.where(row == 0, south, pltpu.roll(c, 1, 0))
             out_ref[v, level] = advance(c, n, s, q_ref[v, up], q_ref[v, low], weight)
         return carry
 
@@ -189,19 +205,22 @@
 def shards(perturb, trajectory, hour_slot, sea_mask):
     lat = lax.axis_size("lat")
     column = lax.axis_index("vec") // RING
-    northward = [(i, i + 1) for i in range(lat - 1)]
-    southward = [(i + 1, i) for i in range(lat - 1)]
+    odd = lax.axis_index("lat") % 2
+    on_chip = [(i, i ^ 1) for i in range(lat)]
+    between = [pair for i in range(1, lat - 1, 2) for pair in ((i, i + 1), (i + 1, i))]
     rings = [[c * RING + z for z in range(RING)] for c in range(COLUMNS)]
     swap = [(i, (i + RING) % (COLUMNS * RING)) for i in range(COLUMNS * RING)]
 
-    def halos(first, last):
-        return lax.ppermute(last, "lat", northward), lax.ppermute(first, "lat", southward)
-
-    which = column.astype(jnp.int32)[None]
-    halo = halos(perturb[:, :, 0], perturb[:, :, -1])
+    def halos(to_near, to_far):
+        far = lax.ppermute(to_far, "lat", between)
+        return lax.ppermute(to_near, "lat", on_chip), far
+
+    place_here = jnp.stack([column, odd]).astype(jnp.int32)
+    first, last = perturb[:, :, 0], perturb[:, :, -1]
+    halo = halos(jnp.where(odd == 1, first, last), jnp.where(odd == 1, last, first))
 
     end, last_hour = RING - 1, COLUMNS * RING - 1
-    keep, send = pack(which, trajectory)
+    keep, send = pack(place_here, trajectory)
     crossed = lax.ppermute(send, "vec", swap)
     moved = lax.ppermute(keep, "vec", [(c * RING + end, c * RING + end - 1) for c in range(COLUMNS)])
     asked = hour_slot[0] + hour_slot[1] - last_hour
@@ -218,9 +237,9 @@
     own = [gathered[:, h] for h in range(2)]
     other = [lax.ppermute(half, "vec", swap) for half in own]
 
-    args = (which, perturb, *halo, sea_mask, own[0], other[0])
+    args = (place_here, perturb, *halo, sea_mask, own[0], other[0])
     halo = halos(*edge_rows(*args))
-    return one_hour(which, one_hour(*args), *halo, sea_mask, own[1], other[1])
+    return one_hour(place_here, one_hour(*args), *halo, sea_mask, own[1], other[1])
 
 
 def solution(mesh):

time: 124 us -> 123 us (level)
  waiting for transfers between devices: 20.4 us -> 17.1 us
  Pallas kernels: 7.66 us -> 10.3 us
    ppermute x4, waiting for transfers between devices: 7.95 us -> 2.3 us  [the longest x2 2.3 us: halos(): far = lax.ppermute(to_far, 'lat', between)]
    all_to_all x1, waiting for transfers between devices: 1.99 us -> 4.74 us  [shards(): lax.all_to_all(offered, 'vec', 0, 0, axis_index_groups=rings, tiled=True)]
    pallas_call x3, Pallas kernels: 7.51 us -> 9.57 us  [on_band(): pl.pallas_call(kernel, out_shape=outs, in_specs=[pl.BlockSpec(memory_spac...]
  transfers between devices with their start and end apart: 9 -> 9, of which waited for: 5 -> 4; matrix products, arithmetic and copies ran while one was open for 3% -> 3% of each run, Pallas kernels for 3% -> 4%
where the time goes in v6:
time: 123 us; the launch traced here: 122 us
  starting transfers between devices  50.4 us (41%)
  blocking collectives  32.5 us (26%)
  waiting for transfers between devices  17.1 us (14%)
  Pallas kernels  10.3 us (8%)
  between operations  6.54 us (5%)
  local copies, waits for them, and re-layouts  4.53 us (4%)
    all_gather x1, blocking collectives, shards(): gathered = lax.all_gather(picked, 'vec', axis=0, axis_index_groups=rings)  32.5 us
    all_to_all x1, starting transfers between devices, shards(): lax.all_to_all(offered, 'vec', 0, 0, axis_index_groups=rings, tiled=True)  15 us
    ppermute x2, starting transfers between devices, halos(): return (lax.ppermute(to_near, 'lat', on_chip), far)  14.8 us
    ppermute x2, starting transfers between devices, halos(): far = lax.ppermute(to_far, 'lat', between)  9.94 us
    pallas_call x3, Pallas kernels, on_band(): pl.pallas_call(kernel, out_shape=outs, in_specs=[pl.BlockSpec(memory_spac...  9.57 us
    ppermute x1, waiting for transfers between devices, shards(): crossed = lax.ppermute(send, 'vec', swap)  6.17 us
    ppermute x2, starting transfers between devices, shards(): other = [lax.ppermute(half, 'vec', swap) for half in own]  6.05 us
    all_to_all x1, waiting for transfers between devices, shards(): lax.all_to_all(offered, 'vec', 0, 0, axis_index_groups=rings, tiled=True)  4.74 us
  transfers between devices with their start and end apart: 9, of which 4 were waited for; matrix products, arithmetic and copies ran while one was open for 3% of the time, Pallas kernels for 4%

profile of v6, /device:TPU:25, one launch (start us, length us, event | category | flops | bytes accessed | tf_op | source)
XLA Modules:
  0.0 122.4 jit_solution(3207425802851939724)
XLA Ops:
  0.1 1.3 %copy-done.1 = bf16[1,3,8,24,720]{4,3,2,1,0:T(8,128)(2,1)S(1)} copy-done((bf16[1,3,8,24,720]{4,3,2,1,0:T(8,128)(2,1)S(1)}, bf16[1,3,8,24,720]{4,3,2,1,0:T(8,128)(2,1)}, u32[]{:S(2)}) %copy-start.1) | copy-done | bytes 829464
  1.4 0.7 pack.1
  2.1 3.1 %collective-permute-start.3 = (bf16[16,112,128]{2,1,0:T(8,128)(2,1)S(1)}, bf16[16,112,128]{2,1,0:T(8,128)(2,1)}, u32[]{:S(2)}, u32[]{:S(2)}) collective-permute-start(bf16[16,112,128]{2,1,0:T(8,128)(2,1)S(1)} %get-tuple-element.10), channel_id=1, source_target_pairs={{0,256},{16,272},{32,288},{48,304},{64,320},{80,336},{96,352},{112... | collective-permute-start | bytes 1376264 | tf_op jit(solution)/shard_map/ppermute | solution.py:224
  5.2 1.4 %collective-permute-start.2 = (bf16[16,112,128]{2,1,0:T(8,128)(2,1)S(1)}, bf16[16,112,128]{2,1,0:T(8,128)(2,1)}, u32[]{:S(2)}, u32[]{:S(2)}) collective-permute-start(bf16[16,112,128]{2,1,0:T(8,128)(2,1)S(1)} %get-tuple-element.9), channel_id=1, source_target_pairs={{240,224},{496,480},{241,225},{497,481},{242,226},{498,482},{243,2... | collective-permute-start | bytes 1376264 | tf_op jit(solution)/shard_map/ppermute | solution.py:225
  6.7 1.3 %fusion.2 = (s32[1]{0:T(128)}, s32[1]{0:T(128)}) fusion(s32[2]{0:T(128)} %param.6), kind=kLoop, calls=%fused_computation.17 | loop fusion | bytes 16 | tf_op jit(solution)/shard_map/slice | solution.py:226
  9.3 6.2 %collective-permute-done.3 = bf16[16,112,128]{2,1,0:T(8,128)(2,1)} collective-permute-done((bf16[16,112,128]{2,1,0:T(8,128)(2,1)S(1)}, bf16[16,112,128]{2,1,0:T(8,128)(2,1)}, u32[]{:S(2)}, u32[]{:S(2)}) %collective-permute-start.3) | collective-permute-done | bytes 458784 | tf_op jit(solution)/shard_map/ppermute | solution.py:224
  15.5 0.8 select_select_fusion
  16.3 15.0 %all-to-all-start = ((bf16[16,112,128]{2,1,0:T(8,128)(2,1)}), bf16[16,112,128]{2,1,0:T(8,128)(2,1)S(1)}, u32[]{:S(2)}, u32[]{:S(2)}) async-start(bf16[16,112,128]{2,1,0:T(8,128)(2,1)} %select_select_fusion), calls=%async_computation | async-start | bytes 917504 | tf_op jit(solution)/shard_map/all_to_all | solution.py:233
  31.6 6.0 %collective-permute-start.1 = (f32[4,8,720]{2,1,0:T(8,128)S(1)}, f32[4,8,720]{2,1,0:T(8,128)S(1)}, u32[]{:S(2)}, u32[]{:S(2)}) collective-permute-start(f32[4,8,720]{2,1,0:T(8,128)S(1)} %get-tuple-element.19), channel_id=1, source_target_pairs={{1,2},{2,1},{3,4},{4,3},{5,6},{6,5},{7,8},{8,7},{9,10},{10,9},{11,... | collective-permute-start | bytes 276488 | tf_op jit(solution)/shard_map/ppermute | solution.py:215
  37.6 1.9 %collective-permute-start = (f32[4,8,720]{2,1,0:T(8,128)S(1)}, f32[4,8,720]{2,1,0:T(8,128)S(1)}, u32[]{:S(2)}, u32[]{:S(2)}) collective-permute-start(f32[4,8,720]{2,1,0:T(8,128)S(1)} %get-tuple-element.20), channel_id=1, source_target_pairs={{0,1},{1,0},{2,3},{3,2},{4,5},{5,4},{6,7},{7,6},{8,9},{9,8},{10,11... | collective-permute-start | bytes 276488 | tf_op jit(solution)/shard_map/ppermute | solution.py:216
  39.6 0.6 fusion.1
  44.0 0.5 slice.41
  44.5 0.5 slice.40
  46.3 4.7 %all-to-all-done = bf16[16,112,128]{2,1,0:T(8,128)(2,1)S(1)} async-done(((bf16[16,112,128]{2,1,0:T(8,128)(2,1)}), bf16[16,112,128]{2,1,0:T(8,128)(2,1)S(1)}, u32[]{:S(2)}, u32[]{:S(2)}) %all-to-all-start) | async-done | bytes 458784 | tf_op jit(solution)/shard_map/all_to_all | solution.py:233
  51.1 32.5 %all_gather.4 = bf16[16,2,112,128]{3,2,0,1:T(8,128)(2,1)S(1)} all-gather(bf16[1,2,112,128]{3,2,0,1:T(8,128)(2,1)S(1)} %maximum_add_fusion), channel_id=1, replica_groups={{0,16,32,48,64,80,96,112,128,144,160,176,192,208,224,240},{256,272,288,..., dimensions={0}, use_global_device_ids=true | all-gather | bytes 974848 | tf_op jit(solution)/shard_map/all_gather | solution.py:236
  83.7 4.1 %collective-permute-start.4 = (bf16[16,112,128]{2,1,0:T(8,128)(2,1)S(1)}, bf16[16,112,128]{2,1,0:T(8,128)(2,1)S(1)}, u32[]{:S(2)}, u32[]{:S(2)}) collective-permute-start(bf16[16,112,128]{2,1,0:T(8,128)(2,1)S(1)} %get-tuple-element.16.own_ref), channel_id=1, source_target_pairs={{0,256},{16,272},{32,288},{48,304},{64,320},{80,336},{96,352},{112... | collective-permute-start | bytes 1376264 | tf_op jit(solution)/shard_map/ppermute | solution.py:238
  87.8 1.9 %collective-permute-start.7 = (bf16[16,112,128]{2,1,0:T(8,128)(2,1)S(1)}, bf16[16,112,128]{2,1,0:T(8,128)(2,1)S(1)}, u32[]{:S(2)}, u32[]{:S(2)}) collective-permute-start(bf16[16,112,128]{2,1,0:T(8,128)(2,1)S(1)} %get-tuple-element.15.own_ref), channel_id=1, source_target_pairs={{0,256},{16,272},{32,288},{48,304},{64,320},{80,336},{96,352},{112... | collective-permute-start | bytes 1376264 | tf_op jit(solution)/shard_map/ppermute | solution.py:238
  89.7 3.9 %collective-permute-done.4.other_ref = bf16[16,112,128]{2,1,0:T(8,128)(2,1)S(1)} collective-permute-done((bf16[16,112,128]{2,1,0:T(8,128)(2,1)S(1)}, bf16[16,112,128]{2,1,0:T(8,128)(2,1)S(1)}, u32[]{:S(2)}, u32[]{:S(2)}) %collective-permute-start.4) | collective-permute-done | bytes 458784 | tf_op jit(solution)/shard_map/ppermute | solution.py:238
  93.7 1.4 %edge_rows.1 = (f32[4,8,720]{2,1,0:T(8,128)S(1)}, f32[4,8,720]{2,1,0:T(8,128)S(1)}) custom-call(s32[2]{0:T(128)S(1)} %pad_add_fusion.place_ref, f32[4,8,24,720]{3,2,1,0:T(8,128)S(1)} %copy-done, f32[4,8,720]{2,1,0:T(8,128)S(1)} %collective-permute-done.near_ref, f32[4,8,720]{2,1,0:T(8,128)S(1)} %collective-permute-done.1.far_ref, s32[24,720]{1,0:T(8,128)S(1)} %copy-done.2, ...), custom_call_target="tpu_custom_call" | custom-call | flops 691200 | bytes 3567112 | tf_op jit(solution)/shard_map/edge_rows/pallas_call | solution.py:180
  95.1 12.9 %collective-permute-start.5 = (f32[4,8,720]{2,1,0:T(8,128)S(1)}, f32[4,8,720]{2,1,0:T(8,128)S(1)}, u32[]{:S(2)}, u32[]{:S(2)}) collective-permute-start(f32[4,8,720]{2,1,0:T(8,128)S(1)} %get-tuple-element.11), channel_id=1, source_target_pairs={{0,1},{1,0},{2,3},{3,2},{4,5},{5,4},{6,7},{7,6},{8,9},{9,8},{10,11... | collective-permute-start | bytes 276488 | tf_op jit(solution)/shard_map/ppermute | solution.py:216
  108.0 3.9 %collective-permute-start.6 = (f32[4,8,720]{2,1,0:T(8,128)S(1)}, f32[4,8,720]{2,1,0:T(8,128)S(1)}, u32[]{:S(2)}, u32[]{:S(2)}) collective-permute-start(f32[4,8,720]{2,1,0:T(8,128)S(1)} %get-tuple-element.12), channel_id=1, source_target_pairs={{1,2},{2,1},{3,4},{4,3},{5,6},{6,5},{7,8},{8,7},{9,10},{10,9},{11,... | collective-permute-start | bytes 276488 | tf_op jit(solution)/shard_map/ppermute | solution.py:215
  112.0 3.3 %one_hour.2.q_ref = f32[4,8,24,720]{3,2,1,0:T(8,128)S(1)} custom-call(s32[2]{0:T(128)S(1)} %pad_add_fusion.place_ref, f32[4,8,24,720]{3,2,1,0:T(8,128)S(1)} %copy-done, f32[4,8,720]{2,1,0:T(8,128)S(1)} %collective-permute-done.near_ref, f32[4,8,720]{2,1,0:T(8,128)S(1)} %collective-permute-done.1.far_ref, s32[24,720]{1,0:T(8,128)S(1)} %copy-done.2, ...), custom_call_target="tpu_custom_call" | custom-call | flops 11059200 | bytes 5594632 | tf_op jit(solution)/shard_map/one_hour/pallas_call | solution.py:180
  115.3 2.3 %collective-permute-done.6.far_ref = f32[4,8,720]{2,1,0:T(8,128)S(1)} collective-permute-done((f32[4,8,720]{2,1,0:T(8,128)S(1)}, f32[4,8,720]{2,1,0:T(8,128)S(1)}, u32[]{:S(2)}, u32[]{:S(2)}) %collective-permute-start.6) | collective-permute-done | bytes 92192 | tf_op jit(solution)/shard_map/ppermute | solution.py:215
  117.6 4.8 %one_hour.3 = f32[4,8,24,720]{3,2,1,0:T(8,128)} custom-call(s32[2]{0:T(128)S(1)} %pad_add_fusion.place_ref, f32[4,8,24,720]{3,2,1,0:T(8,128)S(1)} %one_hour.2.q_ref, f32[4,8,720]{2,1,0:T(8,128)S(1)} %collective-permute-done.5.near_ref, f32[4,8,720]{2,1,0:T(8,128)S(1)} %collective-permute-done.6.far_ref, s32[24,720]{1,0:T(8,128)S(1)} %copy-done.2, ...), custom_call_target="tpu_custom_call" | custom-call | flops 11059200 | bytes 5594632 | tf_op jit(solution)/shard_map/one_hour/pallas_call | solution.py:180
  (19 shorter events, 0.3 us)
Async XLA Ops:
  0.0 31.4 %copy-start = (f32[4,8,24,720]{3,2,1,0:T(8,128)S(1)}, f32[4,8,24,720]{3,2,1,0:T(8,128)}, u32[]{:S(2)}) copy-start(f32[4,8,24,720]{3,2,1,0:T(8,128)} %q_ref.3) | copy-start | bytes 6635524
  0.1 1.3 %copy-start.1 = (bf16[1,3,8,24,720]{4,3,2,1,0:T(8,128)(2,1)S(1)}, bf16[1,3,8,24,720]{4,3,2,1,0:T(8,128)(2,1)}, u32[]{:S(2)}) copy-start(bf16[1,3,8,24,720]{4,3,2,1,0:T(8,128)(2,1)} %field_ref.1) | copy-start | bytes 2488324
  1.4 38.1 %copy-start.3 = (s32[2]{0:T(128)S(1)}, s32[2]{0:T(128)}, u32[]{:S(2)}) copy-start(s32[2]{0:T(128)} %param.6) | copy-start | bytes 28
  2.1 13.4 %collective-permute-start.3 = (bf16[16,112,128]{2,1,0:T(8,128)(2,1)S(1)}, bf16[16,112,128]{2,1,0:T(8,128)(2,1)}, u32[]{:S(2)}, u32[]{:S(2)}) collective-permute-start(bf16[16,112,128]{2,1,0:T(8,128)(2,1)S(1)} %get-tuple-element.10), channel_id=1, source_target_pairs={{0,256},{16,272},{32,288},{48,304},{64,320},{80,336},{96,352},{112... | collective-permute-start | bytes 1376264 | tf_op jit(solution)/shard_map/ppermute | solution.py:224
  5.2 10.3 %collective-permute-start.2 = (bf16[16,112,128]{2,1,0:T(8,128)(2,1)S(1)}, bf16[16,112,128]{2,1,0:T(8,128)(2,1)}, u32[]{:S(2)}, u32[]{:S(2)}) collective-permute-start(bf16[16,112,128]{2,1,0:T(8,128)(2,1)S(1)} %get-tuple-element.9), channel_id=1, source_target_pairs={{240,224},{496,480},{241,225},{497,481},{242,226},{498,482},{243,2... | collective-permute-start | bytes 1376264 | tf_op jit(solution)/shard_map/ppermute | solution.py:225
  16.3 77.3 %copy-start.2 = (s32[24,720]{1,0:T(8,128)S(1)}, s32[24,720]{1,0:T(8,128)}, u32[]{:S(2)}) copy-start(s32[24,720]{1,0:T(8,128)} %mask_ref.5) | copy-start | bytes 207364
  16.3 34.7 %all-to-all-start = ((bf16[16,112,128]{2,1,0:T(8,128)(2,1)}), bf16[16,112,128]{2,1,0:T(8,128)(2,1)S(1)}, u32[]{:S(2)}, u32[]{:S(2)}) async-start(bf16[16,112,128]{2,1,0:T(8,128)(2,1)} %select_select_fusion), calls=%async_computation | async-start | bytes 917504 | tf_op jit(solution)/shard_map/all_to_all | solution.py:233
  31.6 12.4 %collective-permute-start.1 = (f32[4,8,720]{2,1,0:T(8,128)S(1)}, f32[4,8,720]{2,1,0:T(8,128)S(1)}, u32[]{:S(2)}, u32[]{:S(2)}) collective-permute-start(f32[4,8,720]{2,1,0:T(8,128)S(1)} %get-tuple-element.19), channel_id=1, source_target_pairs={{1,2},{2,1},{3,4},{4,3},{5,6},{6,5},{7,8},{8,7},{9,10},{10,9},{11,... | collective-permute-start | bytes 276488 | tf_op jit(solution)/shard_map/ppermute | solution.py:215
  37.6 6.9 %collective-permute-start = (f32[4,8,720]{2,1,0:T(8,128)S(1)}, f32[4,8,720]{2,1,0:T(8,128)S(1)}, u32[]{:S(2)}, u32[]{:S(2)}) collective-permute-start(f32[4,8,720]{2,1,0:T(8,128)S(1)} %get-tuple-element.20), channel_id=1, source_target_pairs={{0,1},{1,0},{2,3},{3,2},{4,5},{5,4},{6,7},{7,6},{8,9},{9,8},{10,11... | collective-permute-start | bytes 276488 | tf_op jit(solution)/shard_map/ppermute | solution.py:216
  83.7 10.0 %collective-permute-start.4 = (bf16[16,112,128]{2,1,0:T(8,128)(2,1)S(1)}, bf16[16,112,128]{2,1,0:T(8,128)(2,1)S(1)}, u32[]{:S(2)}, u32[]{:S(2)}) collective-permute-start(bf16[16,112,128]{2,1,0:T(8,128)(2,1)S(1)} %get-tuple-element.16.own_ref), channel_id=1, source_target_pairs={{0,256},{16,272},{32,288},{48,304},{64,320},{80,336},{96,352},{112... | collective-permute-start | bytes 1376264 | tf_op jit(solution)/shard_map/ppermute | solution.py:238
  87.8 27.5 %collective-permute-start.7 = (bf16[16,112,128]{2,1,0:T(8,128)(2,1)S(1)}, bf16[16,112,128]{2,1,0:T(8,128)(2,1)S(1)}, u32[]{:S(2)}, u32[]{:S(2)}) collective-permute-start(bf16[16,112,128]{2,1,0:T(8,128)(2,1)S(1)} %get-tuple-element.15.own_ref), channel_id=1, source_target_pairs={{0,256},{16,272},{32,288},{48,304},{64,320},{80,336},{96,352},{112... | collective-permute-start | bytes 1376264 | tf_op jit(solution)/shard_map/ppermute | solution.py:238
  95.1 20.2 %collective-permute-start.5 = (f32[4,8,720]{2,1,0:T(8,128)S(1)}, f32[4,8,720]{2,1,0:T(8,128)S(1)}, u32[]{:S(2)}, u32[]{:S(2)}) collective-permute-start(f32[4,8,720]{2,1,0:T(8,128)S(1)} %get-tuple-element.11), channel_id=1, source_target_pairs={{0,1},{1,0},{2,3},{3,2},{4,5},{5,4},{6,7},{7,6},{8,9},{9,8},{10,11... | collective-permute-start | bytes 276488 | tf_op jit(solution)/shard_map/ppermute | solution.py:216
  108.0 9.5 %collective-permute-start.6 = (f32[4,8,720]{2,1,0:T(8,128)S(1)}, f32[4,8,720]{2,1,0:T(8,128)S(1)}, u32[]{:S(2)}, u32[]{:S(2)}) collective-permute-start(f32[4,8,720]{2,1,0:T(8,128)S(1)} %get-tuple-element.12), channel_id=1, source_target_pairs={{1,2},{2,1},{3,4},{4,3},{5,6},{6,5},{7,8},{8,7},{9,10},{10,9},{11,... | collective-permute-start | bytes 276488 | tf_op jit(solution)/shard_map/ppermute | solution.py:215

commit v7 on v6

--- a/solution.py
+++ b/solution.py
@@ -90,17 +90,26 @@
     return (wc * c + we * lanes_next(c) + ww * lanes_prev(c)) + (wn * n + ws * s + wl * (u + b))
 
 
-def neighbours(place_ref, near, far):
-    odd = place_ref[1] == 1
-    return jnp.where(odd, near, far), jnp.where(odd, far, near)
+def set_halos(place_ref, near_ref, far_ref, south_ref, north_ref):
+    @pl.when(place_ref[1] == 1)
+    def _():
+        south_ref[...] = near_ref[...]
+        north_ref[...] = far_ref[...]
+
+    @pl.when(place_ref[1] == 0)
+    def _():
+        south_ref[...] = far_ref[...]
+        north_ref[...] = near_ref[...]
 
 
 def rows_kernel(
-    place_ref, q_ref, near_ref, far_ref, mask_ref, own_ref, other_ref, to_near_ref, to_far_ref, field_ref
+    place_ref, q_ref, far_ref, near_ref, mask_ref, own_ref, other_ref,
+    to_far_ref, to_near_ref, field_ref, south_ref, north_ref,
 ):
     vecs, levs, rows, lon = q_ref.shape
     lev = lax.broadcasted_iota(jnp.int32, (levs, lon), 0)
     own_column, odd = place_ref[0], place_ref[1]
+    set_halos(place_ref, near_ref, far_ref, south_ref, north_ref)
 
     def row_of(v, r):
         return jnp.concatenate([q_ref[v, z, r : r + 1] for z in range(levs)], axis=0)
@@ -121,31 +130,34 @@
                                 field_ref[k, z : z + 1, tile * LANES : (tile + 1) * LANES] = eight[i : i + 1]
 
         weight = weights(*(field_ref[k, :, :lon] for k in range(FIELDS)), mask_ref[r : r + 1].astype(jnp.float32))
-        to_near = odd == (1 if r == 0 else 0)
+        new = []
         for v in range(vecs):
-            south, north = neighbours(place_ref, near_ref[v], far_ref[v])
             c, inner = row_of(v, r), row_of(v, r + step)
-            n, s = (inner, south) if r == 0 else (north, inner)
+            n, s = (inner, south_ref[v]) if r == 0 else (north_ref[v], inner)
             u = jnp.where(lev == 0, c, pltpu.roll(c, 1, 0))
             b = jnp.where(lev == levs - 1, c, pltpu.roll(c, levs - 1, 0))
-            new = advance(c, n, s, u, b, weight)
-
-            @pl.when(to_near)
-            def _():
-                to_near_ref[v] = new
-
-            @pl.when(jnp.logical_not(to_near))
-            def _():
-                to_far_ref[v] = new
+            new.append(advance(c, n, s, u, b, weight))
+
+        @pl.when(odd == (1 if r == 0 else 0))
+        def _():
+            for v in range(vecs):
+                to_near_ref[v] = new[v]
+
+        @pl.when(odd == (0 if r == 0 else 1))
+        def _():
+            for v in range(vecs):
+                to_far_ref[v] = new[v]
 
 
 def hour_kernel(
-    place_ref, q_ref, near_ref, far_ref, mask_ref, own_ref, other_ref, out_ref, field_ref
+    place_ref, q_ref, far_ref, near_ref, mask_ref, own_ref, other_ref,
+    out_ref, field_ref, south_ref, north_ref,
 ):
     vecs, levs, rows, lon = q_ref.shape
     row = lax.broadcasted_iota(jnp.int32, (rows, lon), 0)
     mask = mask_ref[...].astype(jnp.float32)
     own_column = place_ref[0]
+    set_halos(place_ref, near_ref, far_ref, south_ref, north_ref)
 
     def level_step(level, carry):
         for own in range(COLUMNS):
@@ -164,9 +176,8 @@
         low = jnp.minimum(level + 1, levs - 1)
         for v in range(vecs):
             c = q_ref[v, level]
-            south, north = neighbours(place_ref, near_ref[v, pl.ds(level, 1)], far_ref[v, pl.ds(level, 1)])
-            n = jnp.where(row == rows - 1, north, pltpu.roll(c, rows - 1, 0))
-            s = jnp.where(row == 0, south, pltpu.roll(c, 1, 0))
+            n = jnp.where(row == rows - 1, north_ref[v, pl.ds(level, 1)], pltpu.roll(c, rows - 1, 0))
+            s = jnp.where(row == 0, south_ref[v, pl.ds(level, 1)], pltpu.roll(c, 1, 0))
             out_ref[v, level] = advance(c, n, s, q_ref[v, up], q_ref[v, low], weight)
         return carry
 
@@ -182,7 +193,11 @@
         out_shape=outs,
         in_specs=[pl.BlockSpec(memory_space=pltpu.SMEM)] + [vmem] * (len(args) - 1),
         out_specs=tuple(vmem for _ in outs),
-        scratch_shapes=[pltpu.VMEM((FIELDS, field_rows, -(-lon // LANES) * LANES), jnp.float32)],
+        scratch_shapes=[
+            pltpu.VMEM((FIELDS, field_rows, -(-lon // LANES) * LANES), jnp.float32),
+            pltpu.VMEM(args[2].shape, jnp.float32),
+            pltpu.VMEM(args[2].shape, jnp.float32),
+        ],
         compiler_params=pltpu.CompilerParams(vmem_limit_bytes=VMEM_LIMIT),
         cost_estimate=pl.CostEstimate(flops=flops, bytes_accessed=bytes_accessed, transcendentals=0),
         name=name,
@@ -211,13 +226,13 @@
     rings = [[c * RING + z for z in range(RING)] for c in range(COLUMNS)]
     swap = [(i, (i + RING) % (COLUMNS * RING)) for i in range(COLUMNS * RING)]
 
-    def halos(to_near, to_far):
+    def halos(to_far, to_near):
         far = lax.ppermute(to_far, "lat", between)
-        return lax.ppermute(to_near, "lat", on_chip), far
+        return far, lax.ppermute(to_near, "lat", on_chip)
 
     place_here = jnp.stack([column, odd]).astype(jnp.int32)
     first, last = perturb[:, :, 0], perturb[:, :, -1]
-    halo = halos(jnp.where(odd == 1, first, last), jnp.where(odd == 1, last, first))
+    halo = halos(jnp.where(odd == 1, last, first), jnp.where(odd == 1, first, last))
 
     end, last_hour = RING - 1, COLUMNS * RING - 1
     keep, send = pack(place_here, trajectory)
@@ -235,7 +250,8 @@
     picked = picked + (sum(h[0, 0, 0] for h in halo) * 0).astype(picked.dtype)
     gathered = lax.all_gather(picked, "vec", axis=0, axis_index_groups=rings)
     own = [gathered[:, h] for h in range(2)]
-    other = [lax.ppermute(half, "vec", swap) for half in own]
+    other = [lax.ppermute(own[0], "vec", swap)]
+    other.append(lax.ppermute(own[1] + other[0][0, 0, 0] * 0, "vec", swap))
 
     args = (place_here, perturb, *halo, sea_mask, own[0], other[0])
     halo = halos(*edge_rows(*args))

time: 123 us -> 130 us (1.057)
  starting transfers between devices: 50.4 us -> 57.1 us
    ppermute x2, starting transfers between devices: 9.94 us -> 24.2 us  [halos(): far = lax.ppermute(to_far, 'lat', between)]
    ppermute x4, starting transfers between devices: 20.9 us -> 13.4 us  [the longest x2 5.66 us: halos(): return (far, lax.ppermute(to_near, 'lat', on_chip))]
    ppermute x4, waiting for transfers between devices: 3.93 us -> 5.86 us  [the longest x1 5.85 us: shards(): other = [lax.ppermute(own[0], 'vec', swap)]]
    ppermute x2, waiting for transfers between devices: 2.3 us -> 0.66 us  [halos(): far = lax.ppermute(to_far, 'lat', between)]
  transfers between devices with their start and end apart: 9 -> 9, of which waited for: 4 -> 4; matrix products, arithmetic and copies ran while one was open for 3% -> 2% of each run, Pallas kernels for 4% -> 3%
where the time goes in v7:
time: 130 us
  starting transfers between devices  57.1 us (44%)
  blocking collectives  32.5 us (25%)
  waiting for transfers between devices  16.8 us (13%)
  Pallas kernels  9.96 us (8%)
  between operations  7.23 us (6%)
  local copies, waits for them, and re-layouts  5.05 us (4%)
    all_gather x1, blocking collectives, shards(): gathered = lax.all_gather(picked, 'vec', axis=0, axis_index_groups=rings)  32.5 us
    ppermute x2, starting transfers between devices, halos(): far = lax.ppermute(to_far, 'lat', between)  24.2 us
    all_to_all x1, starting transfers between devices, shards(): lax.all_to_all(offered, 'vec', 0, 0, axis_index_groups=rings, tiled=True)  14.9 us
    pallas_call x3, Pallas kernels, on_band(): pl.pallas_call(kernel, out_shape=outs, in_specs=[pl.BlockSpec(memory_spac...  9.26 us
    ppermute x1, waiting for transfers between devices, shards(): crossed = lax.ppermute(send, 'vec', swap)  6.17 us
    ppermute x1, waiting for transfers between devices, shards(): other = [lax.ppermute(own[0], 'vec', swap)]  5.85 us
    ppermute x2, starting transfers between devices, halos(): return (far, lax.ppermute(to_near, 'lat', on_chip))  5.66 us
    ppermute x1, starting transfers between devices, shards(): other = [lax.ppermute(own[0], 'vec', swap)]  4.13 us
  transfers between devices with their start and end apart: 9, of which 4 were waited for; matrix products, arithmetic and copies ran while one was open for 2% of the time, Pallas kernels for 3%

profile of v7, /device:TPU:25, one launch (start us, length us, event | category | flops | bytes accessed | tf_op | source)
XLA Modules:
  0.0 129.6 jit_solution(15127551746769298287)
XLA Ops:
  0.1 1.3 %copy-done.1 = bf16[1,3,8,24,720]{4,3,2,1,0:T(8,128)(2,1)S(1)} copy-done((bf16[1,3,8,24,720]{4,3,2,1,0:T(8,128)(2,1)S(1)}, bf16[1,3,8,24,720]{4,3,2,1,0:T(8,128)(2,1)}, u32[]{:S(2)}) %copy-start.1) | copy-done | bytes 829464
  1.4 0.7 pack.1
  2.1 3.1 %collective-permute-start.3 = (bf16[16,112,128]{2,1,0:T(8,128)(2,1)S(1)}, bf16[16,112,128]{2,1,0:T(8,128)(2,1)}, u32[]{:S(2)}, u32[]{:S(2)}) collective-permute-start(bf16[16,112,128]{2,1,0:T(8,128)(2,1)S(1)} %get-tuple-element.10), channel_id=1, source_target_pairs={{0,256},{16,272},{32,288},{48,304},{64,320},{80,336},{96,352},{112... | collective-permute-start | bytes 1376264 | tf_op jit(solution)/shard_map/ppermute | solution.py:239
  5.2 1.4 %collective-permute-start.2 = (bf16[16,112,128]{2,1,0:T(8,128)(2,1)S(1)}, bf16[16,112,128]{2,1,0:T(8,128)(2,1)}, u32[]{:S(2)}, u32[]{:S(2)}) collective-permute-start(bf16[16,112,128]{2,1,0:T(8,128)(2,1)S(1)} %get-tuple-element.9), channel_id=1, source_target_pairs={{240,224},{496,480},{241,225},{497,481},{242,226},{498,482},{243,2... | collective-permute-start | bytes 1376264 | tf_op jit(solution)/shard_map/ppermute | solution.py:240
  6.7 1.3 %fusion.2 = (s32[1]{0:T(128)}, s32[1]{0:T(128)}) fusion(s32[2]{0:T(128)} %param.6), kind=kLoop, calls=%fused_computation.18 | loop fusion | bytes 16 | tf_op jit(solution)/shard_map/slice | solution.py:241
  9.3 6.2 %collective-permute-done.3 = bf16[16,112,128]{2,1,0:T(8,128)(2,1)} collective-permute-done((bf16[16,112,128]{2,1,0:T(8,128)(2,1)S(1)}, bf16[16,112,128]{2,1,0:T(8,128)(2,1)}, u32[]{:S(2)}, u32[]{:S(2)}) %collective-permute-start.3) | collective-permute-done | bytes 458784 | tf_op jit(solution)/shard_map/ppermute | solution.py:239
  15.5 0.8 select_select_fusion
  16.3 14.9 %all-to-all-start = ((bf16[16,112,128]{2,1,0:T(8,128)(2,1)}), bf16[16,112,128]{2,1,0:T(8,128)(2,1)S(1)}, u32[]{:S(2)}, u32[]{:S(2)}) async-start(bf16[16,112,128]{2,1,0:T(8,128)(2,1)} %select_select_fusion), calls=%async_computation | async-start | bytes 917504 | tf_op jit(solution)/shard_map/all_to_all | solution.py:248
  31.5 3.7 %collective-permute-start.1 = (f32[4,8,720]{2,1,0:T(8,128)S(1)}, f32[4,8,720]{2,1,0:T(8,128)S(1)}, u32[]{:S(2)}, u32[]{:S(2)}) collective-permute-start(f32[4,8,720]{2,1,0:T(8,128)S(1)} %get-tuple-element.19), channel_id=1, source_target_pairs={{0,1},{1,0},{2,3},{3,2},{4,5},{5,4},{6,7},{7,6},{8,9},{9,8},{10,11... | collective-permute-start | bytes 276488 | tf_op jit(solution)/shard_map/ppermute | solution.py:231
  35.2 4.2 %collective-permute-start = (f32[4,8,720]{2,1,0:T(8,128)S(1)}, f32[4,8,720]{2,1,0:T(8,128)S(1)}, u32[]{:S(2)}, u32[]{:S(2)}) collective-permute-start(f32[4,8,720]{2,1,0:T(8,128)S(1)} %get-tuple-element.20), channel_id=1, source_target_pairs={{1,2},{2,1},{3,4},{4,3},{5,6},{6,5},{7,8},{8,7},{9,10},{10,9},{11,... | collective-permute-start | bytes 276488 | tf_op jit(solution)/shard_map/ppermute | solution.py:230
  39.4 0.6 fusion.1
  43.8 0.5 slice.45
  44.4 0.7 collective-permute-done.far_ref
  45.0 0.5 slice.44
  46.8 4.1 %all-to-all-done = bf16[16,112,128]{2,1,0:T(8,128)(2,1)S(1)} async-done(((bf16[16,112,128]{2,1,0:T(8,128)(2,1)}), bf16[16,112,128]{2,1,0:T(8,128)(2,1)S(1)}, u32[]{:S(2)}, u32[]{:S(2)}) %all-to-all-start) | async-done | bytes 458784 | tf_op jit(solution)/shard_map/all_to_all | solution.py:248
  50.9 32.5 %all_gather.4 = bf16[16,2,112,128]{3,2,0,1:T(8,128)(2,1)S(1)} all-gather(bf16[1,2,112,128]{3,2,0,1:T(8,128)(2,1)S(1)} %maximum_add_fusion), channel_id=1, replica_groups={{0,16,32,48,64,80,96,112,128,144,160,176,192,208,224,240},{256,272,288,..., dimensions={0}, use_global_device_ids=true | all-gather | bytes 974848 | tf_op jit(solution)/shard_map/all_gather | solution.py:251
  83.5 4.1 %collective-permute-start.4 = (bf16[16,112,128]{2,1,0:T(8,128)(2,1)S(1)}, bf16[16,112,128]{2,1,0:T(8,128)(2,1)S(1)}, u32[]{:S(2)}, u32[]{:S(2)}) collective-permute-start(bf16[16,112,128]{2,1,0:T(8,128)(2,1)S(1)} %get-tuple-element.16.own_ref), channel_id=1, source_target_pairs={{0,256},{16,272},{32,288},{48,304},{64,320},{80,336},{96,352},{112... | collective-permute-start | bytes 1376264 | tf_op jit(solution)/shard_map/ppermute | solution.py:253
  87.7 5.9 %collective-permute-done.4.other_ref = bf16[16,112,128]{2,1,0:T(8,128)(2,1)S(1)} collective-permute-done((bf16[16,112,128]{2,1,0:T(8,128)(2,1)S(1)}, bf16[16,112,128]{2,1,0:T(8,128)(2,1)S(1)}, u32[]{:S(2)}, u32[]{:S(2)}) %collective-permute-start.4) | collective-permute-done | bytes 458784 | tf_op jit(solution)/shard_map/ppermute | solution.py:253
  94.7 3.7 %collective-permute-start.7 = (bf16[16,112,128]{2,1,0:T(8,128)(2,1)S(1)}, bf16[16,112,128]{2,1,0:T(8,128)(2,1)S(1)}, u32[]{:S(2)}, u32[]{:S(2)}) collective-permute-start(bf16[16,112,128]{2,1,0:T(8,128)(2,1)S(1)} %broadcast_add_fusion), channel_id=1, source_target_pairs={{0,256},{16,272},{32,288},{48,304},{64,320},{80,336},{96,352},{112... | collective-permute-start | bytes 1376264 | tf_op jit(solution)/shard_map/ppermute | solution.py:254
  98.4 1.1 edge_rows.1
  99.5 20.0 %collective-permute-start.5 = (f32[4,8,720]{2,1,0:T(8,128)S(1)}, f32[4,8,720]{2,1,0:T(8,128)S(1)}, u32[]{:S(2)}, u32[]{:S(2)}) collective-permute-start(f32[4,8,720]{2,1,0:T(8,128)S(1)} %get-tuple-element.11), channel_id=1, source_target_pairs={{1,2},{2,1},{3,4},{4,3},{5,6},{6,5},{7,8},{8,7},{9,10},{10,9},{11,... | collective-permute-start | bytes 276488 | tf_op jit(solution)/shard_map/ppermute | solution.py:230
  119.5 1.9 %collective-permute-start.6 = (f32[4,8,720]{2,1,0:T(8,128)S(1)}, f32[4,8,720]{2,1,0:T(8,128)S(1)}, u32[]{:S(2)}, u32[]{:S(2)}) collective-permute-start(f32[4,8,720]{2,1,0:T(8,128)S(1)} %get-tuple-element.12), channel_id=1, source_target_pairs={{0,1},{1,0},{2,3},{3,2},{4,5},{5,4},{6,7},{7,6},{8,9},{9,8},{10,11... | collective-permute-start | bytes 276488 | tf_op jit(solution)/shard_map/ppermute | solution.py:231
  121.4 3.3 %one_hour.2.q_ref = f32[4,8,24,720]{3,2,1,0:T(8,128)S(1)} custom-call(s32[2]{0:T(128)S(1)} %pad_add_fusion.place_ref, f32[4,8,24,720]{3,2,1,0:T(8,128)S(1)} %copy-done, f32[4,8,720]{2,1,0:T(8,128)S(1)} %collective-permute-done.far_ref, f32[4,8,720]{2,1,0:T(8,128)S(1)} %collective-permute-done.1.near_ref, s32[24,720]{1,0:T(8,128)S(1)} %copy-done.2, ...), custom_call_target="tpu_custom_call" | custom-call | flops 11059200 | bytes 5594632 | tf_op jit(solution)/shard_map/one_hour/pallas_call | solution.py:191
  124.8 4.9 %one_hour.3 = f32[4,8,24,720]{3,2,1,0:T(8,128)} custom-call(s32[2]{0:T(128)S(1)} %pad_add_fusion.place_ref, f32[4,8,24,720]{3,2,1,0:T(8,128)S(1)} %one_hour.2.q_ref, f32[4,8,720]{2,1,0:T(8,128)S(1)} %collective-permute-done.5.far_ref, f32[4,8,720]{2,1,0:T(8,128)S(1)} %collective-permute-done.6.near_ref, s32[24,720]{1,0:T(8,128)S(1)} %copy-done.2, ...), custom_call_target="tpu_custom_call" | custom-call | flops 11059200 | bytes 5594632 | tf_op jit(solution)/shard_map/one_hour/pallas_call | solution.py:191
  (21 shorter events, 0.9 us)
Async XLA Ops:
  0.0 31.3 %copy-start = (f32[4,8,24,720]{3,2,1,0:T(8,128)S(1)}, f32[4,8,24,720]{3,2,1,0:T(8,128)}, u32[]{:S(2)}) copy-start(f32[4,8,24,720]{3,2,1,0:T(8,128)} %q_ref.3) | copy-start | bytes 6635524
  0.1 1.3 %copy-start.1 = (bf16[1,3,8,24,720]{4,3,2,1,0:T(8,128)(2,1)S(1)}, bf16[1,3,8,24,720]{4,3,2,1,0:T(8,128)(2,1)}, u32[]{:S(2)}) copy-start(bf16[1,3,8,24,720]{4,3,2,1,0:T(8,128)(2,1)} %field_ref.1) | copy-start | bytes 2488324
  1.4 38.0 %copy-start.3 = (s32[2]{0:T(128)S(1)}, s32[2]{0:T(128)}, u32[]{:S(2)}) copy-start(s32[2]{0:T(128)} %param.6) | copy-start | bytes 28
  2.1 13.4 %collective-permute-start.3 = (bf16[16,112,128]{2,1,0:T(8,128)(2,1)S(1)}, bf16[16,112,128]{2,1,0:T(8,128)(2,1)}, u32[]{:S(2)}, u32[]{:S(2)}) collective-permute-start(bf16[16,112,128]{2,1,0:T(8,128)(2,1)S(1)} %get-tuple-element.10), channel_id=1, source_target_pairs={{0,256},{16,272},{32,288},{48,304},{64,320},{80,336},{96,352},{112... | collective-permute-start | bytes 1376264 | tf_op jit(solution)/shard_map/ppermute | solution.py:239
  5.2 10.3 %collective-permute-start.2 = (bf16[16,112,128]{2,1,0:T(8,128)(2,1)S(1)}, bf16[16,112,128]{2,1,0:T(8,128)(2,1)}, u32[]{:S(2)}, u32[]{:S(2)}) collective-permute-start(bf16[16,112,128]{2,1,0:T(8,128)(2,1)S(1)} %get-tuple-element.9), channel_id=1, source_target_pairs={{240,224},{496,480},{241,225},{497,481},{242,226},{498,482},{243,2... | collective-permute-start | bytes 1376264 | tf_op jit(solution)/shard_map/ppermute | solution.py:240
  16.3 34.6 %all-to-all-start = ((bf16[16,112,128]{2,1,0:T(8,128)(2,1)}), bf16[16,112,128]{2,1,0:T(8,128)(2,1)S(1)}, u32[]{:S(2)}, u32[]{:S(2)}) async-start(bf16[16,112,128]{2,1,0:T(8,128)(2,1)} %select_select_fusion), calls=%async_computation | async-start | bytes 917504 | tf_op jit(solution)/shard_map/all_to_all | solution.py:248
  31.3 67.1 %copy-start.2 = (s32[24,720]{1,0:T(8,128)S(1)}, s32[24,720]{1,0:T(8,128)}, u32[]{:S(2)}) copy-start(s32[24,720]{1,0:T(8,128)} %mask_ref.5) | copy-start | bytes 207364
  31.5 12.4 %collective-permute-start.1 = (f32[4,8,720]{2,1,0:T(8,128)S(1)}, f32[4,8,720]{2,1,0:T(8,128)S(1)}, u32[]{:S(2)}, u32[]{:S(2)}) collective-permute-start(f32[4,8,720]{2,1,0:T(8,128)S(1)} %get-tuple-element.19), channel_id=1, source_target_pairs={{0,1},{1,0},{2,3},{3,2},{4,5},{5,4},{6,7},{7,6},{8,9},{9,8},{10,11... | collective-permute-start | bytes 276488 | tf_op jit(solution)/shard_map/ppermute | solution.py:231
  35.2 9.8 %collective-permute-start = (f32[4,8,720]{2,1,0:T(8,128)S(1)}, f32[4,8,720]{2,1,0:T(8,128)S(1)}, u32[]{:S(2)}, u32[]{:S(2)}) collective-permute-start(f32[4,8,720]{2,1,0:T(8,128)S(1)} %get-tuple-element.20), channel_id=1, source_target_pairs={{1,2},{2,1},{3,4},{4,3},{5,6},{6,5},{7,8},{8,7},{9,10},{10,9},{11,... | collective-permute-start | bytes 276488 | tf_op jit(solution)/shard_map/ppermute | solution.py:230
  83.5 10.0 %collective-permute-start.4 = (bf16[16,112,128]{2,1,0:T(8,128)(2,1)S(1)}, bf16[16,112,128]{2,1,0:T(8,128)(2,1)S(1)}, u32[]{:S(2)}, u32[]{:S(2)}) collective-permute-start(bf16[16,112,128]{2,1,0:T(8,128)(2,1)S(1)} %get-tuple-element.16.own_ref), channel_id=1, source_target_pairs={{0,256},{16,272},{32,288},{48,304},{64,320},{80,336},{96,352},{112... | collective-permute-start | bytes 1376264 | tf_op jit(solution)/shard_map/ppermute | solution.py:253
  94.7 30.0 %collective-permute-start.7 = (bf16[16,112,128]{2,1,0:T(8,128)(2,1)S(1)}, bf16[16,112,128]{2,1,0:T(8,128)(2,1)S(1)}, u32[]{:S(2)}, u32[]{:S(2)}) collective-permute-start(bf16[16,112,128]{2,1,0:T(8,128)(2,1)S(1)} %broadcast_add_fusion), channel_id=1, source_target_pairs={{0,256},{16,272},{32,288},{48,304},{64,320},{80,336},{96,352},{112... | collective-permute-start | bytes 1376264 | tf_op jit(solution)/shard_map/ppermute | solution.py:254
  99.5 25.2 %collective-permute-start.5 = (f32[4,8,720]{2,1,0:T(8,128)S(1)}, f32[4,8,720]{2,1,0:T(8,128)S(1)}, u32[]{:S(2)}, u32[]{:S(2)}) collective-permute-start(f32[4,8,720]{2,1,0:T(8,128)S(1)} %get-tuple-element.11), channel_id=1, source_target_pairs={{1,2},{2,1},{3,4},{4,3},{5,6},{6,5},{7,8},{8,7},{9,10},{10,9},{11,... | collective-permute-start | bytes 276488 | tf_op jit(solution)/shard_map/ppermute | solution.py:230
  119.5 5.3 %collective-permute-start.6 = (f32[4,8,720]{2,1,0:T(8,128)S(1)}, f32[4,8,720]{2,1,0:T(8,128)S(1)}, u32[]{:S(2)}, u32[]{:S(2)}) collective-permute-start(f32[4,8,720]{2,1,0:T(8,128)S(1)} %get-tuple-element.12), channel_id=1, source_target_pairs={{0,1},{1,0},{2,3},{3,2},{4,5},{5,4},{6,7},{7,6},{8,9},{9,8},{10,11... | collective-permute-start | bytes 276488 | tf_op jit(solution)/shard_map/ppermute | solution.py:231

commit v8 on v7

--- a/solution.py
+++ b/solution.py
@@ -250,8 +250,7 @@
     picked = picked + (sum(h[0, 0, 0] for h in halo) * 0).astype(picked.dtype)
     gathered = lax.all_gather(picked, "vec", axis=0, axis_index_groups=rings)
     own = [gathered[:, h] for h in range(2)]
-    other = [lax.ppermute(own[0], "vec", swap)]
-    other.append(lax.ppermute(own[1] + other[0][0, 0, 0] * 0, "vec", swap))
+    other = [lax.ppermute(half, "vec", swap) for half in own]
 
     args = (place_here, perturb, *halo, sea_mask, own[0], other[0])
     halo = halos(*edge_rows(*args))

time: 130 us -> 121 us (0.931)
  starting transfers between devices: 57.1 us -> 50.4 us
  waiting for transfers between devices: 16.8 us -> 14.9 us
    ppermute x2, starting transfers between devices: 24.2 us -> 19.1 us  [halos(): far = lax.ppermute(to_far, 'lat', between)]
    ppermute x2, waiting for transfers between devices: 5.86 us -> 3.93 us  [shards(): other = [lax.ppermute(half, 'vec', swap) for half in own]]
    ppermute x2, starting transfers between devices: 7.79 us -> 6.05 us  [shards(): other = [lax.ppermute(half, 'vec', swap) for half in own]]
  transfers between devices with their start and end apart: 9 -> 9, of which waited for: 4 -> 4; matrix products, arithmetic and copies ran while one was open for 2% -> 3% of each run, Pallas kernels for 3% -> 4%
where the time goes in v8:
time: 121 us; the launch traced here: 120 us
  starting transfers between devices  50.4 us (42%)
  blocking collectives  32.5 us (27%)
  waiting for transfers between devices  14.9 us (12%)
  Pallas kernels  9.96 us (8%)
  between operations  6.54 us (5%)
  local copies, waits for them, and re-layouts  4.53 us (4%)
    all_gather x1, blocking collectives, shards(): gathered = lax.all_gather(picked, 'vec', axis=0, axis_index_groups=rings)  32.5 us
    ppermute x2, starting transfers between devices, halos(): far = lax.ppermute(to_far, 'lat', between)  19.1 us
    all_to_all x1, starting transfers between devices, shards(): lax.all_to_all(offered, 'vec', 0, 0, axis_index_groups=rings, tiled=True)  15 us
    pallas_call x3, Pallas kernels, on_band(): pl.pallas_call(kernel, out_shape=outs, in_specs=[pl.BlockSpec(memory_spac...  9.26 us
    ppermute x1, waiting for transfers between devices, shards(): crossed = lax.ppermute(send, 'vec', swap)  6.17 us
    ppermute x2, starting transfers between devices, shards(): other = [lax.ppermute(half, 'vec', swap) for half in own]  6.05 us
    ppermute x2, starting transfers between devices, halos(): return (far, lax.ppermute(to_near, 'lat', on_chip))  5.66 us
    all_to_all x1, waiting for transfers between devices, shards(): lax.all_to_all(offered, 'vec', 0, 0, axis_index_groups=rings, tiled=True)  4.09 us
  transfers between devices with their start and end apart: 9, of which 4 were waited for; matrix products, arithmetic and copies ran while one was open for 3% of the time, Pallas kernels for 4%

profile of v8, /device:TPU:25, one launch (start us, length us, event | category | flops | bytes accessed | tf_op | source)
XLA Modules:
  0.0 119.8 jit_solution(3557923168238552080)
XLA Ops:
  0.1 1.3 %copy-done.1 = bf16[1,3,8,24,720]{4,3,2,1,0:T(8,128)(2,1)S(1)} copy-done((bf16[1,3,8,24,720]{4,3,2,1,0:T(8,128)(2,1)S(1)}, bf16[1,3,8,24,720]{4,3,2,1,0:T(8,128)(2,1)}, u32[]{:S(2)}) %copy-start.1) | copy-done | bytes 829464
  1.4 0.7 pack.1
  2.1 3.1 %collective-permute-start.3 = (bf16[16,112,128]{2,1,0:T(8,128)(2,1)S(1)}, bf16[16,112,128]{2,1,0:T(8,128)(2,1)}, u32[]{:S(2)}, u32[]{:S(2)}) collective-permute-start(bf16[16,112,128]{2,1,0:T(8,128)(2,1)S(1)} %get-tuple-element.10), channel_id=1, source_target_pairs={{0,256},{16,272},{32,288},{48,304},{64,320},{80,336},{96,352},{112... | collective-permute-start | bytes 1376264 | tf_op jit(solution)/shard_map/ppermute | solution.py:239
  5.2 1.4 %collective-permute-start.2 = (bf16[16,112,128]{2,1,0:T(8,128)(2,1)S(1)}, bf16[16,112,128]{2,1,0:T(8,128)(2,1)}, u32[]{:S(2)}, u32[]{:S(2)}) collective-permute-start(bf16[16,112,128]{2,1,0:T(8,128)(2,1)S(1)} %get-tuple-element.9), channel_id=1, source_target_pairs={{240,224},{496,480},{241,225},{497,481},{242,226},{498,482},{243,2... | collective-permute-start | bytes 1376264 | tf_op jit(solution)/shard_map/ppermute | solution.py:240
  6.7 1.3 %fusion.2 = (s32[1]{0:T(128)}, s32[1]{0:T(128)}) fusion(s32[2]{0:T(128)} %param.6), kind=kLoop, calls=%fused_computation.17 | loop fusion | bytes 16 | tf_op jit(solution)/shard_map/slice | solution.py:241
  9.3 6.2 %collective-permute-done.3 = bf16[16,112,128]{2,1,0:T(8,128)(2,1)} collective-permute-done((bf16[16,112,128]{2,1,0:T(8,128)(2,1)S(1)}, bf16[16,112,128]{2,1,0:T(8,128)(2,1)}, u32[]{:S(2)}, u32[]{:S(2)}) %collective-permute-start.3) | collective-permute-done | bytes 458784 | tf_op jit(solution)/shard_map/ppermute | solution.py:239
  15.5 0.8 select_select_fusion
  16.3 15.0 %all-to-all-start = ((bf16[16,112,128]{2,1,0:T(8,128)(2,1)}), bf16[16,112,128]{2,1,0:T(8,128)(2,1)S(1)}, u32[]{:S(2)}, u32[]{:S(2)}) async-start(bf16[16,112,128]{2,1,0:T(8,128)(2,1)} %select_select_fusion), calls=%async_computation | async-start | bytes 917504 | tf_op jit(solution)/shard_map/all_to_all | solution.py:248
  31.6 3.7 %collective-permute-start.1 = (f32[4,8,720]{2,1,0:T(8,128)S(1)}, f32[4,8,720]{2,1,0:T(8,128)S(1)}, u32[]{:S(2)}, u32[]{:S(2)}) collective-permute-start(f32[4,8,720]{2,1,0:T(8,128)S(1)} %get-tuple-element.19), channel_id=1, source_target_pairs={{0,1},{1,0},{2,3},{3,2},{4,5},{5,4},{6,7},{7,6},{8,9},{9,8},{10,11... | collective-permute-start | bytes 276488 | tf_op jit(solution)/shard_map/ppermute | solution.py:231
  35.3 4.2 %collective-permute-start = (f32[4,8,720]{2,1,0:T(8,128)S(1)}, f32[4,8,720]{2,1,0:T(8,128)S(1)}, u32[]{:S(2)}, u32[]{:S(2)}) collective-permute-start(f32[4,8,720]{2,1,0:T(8,128)S(1)} %get-tuple-element.20), channel_id=1, source_target_pairs={{1,2},{2,1},{3,4},{4,3},{5,6},{6,5},{7,8},{8,7},{9,10},{10,9},{11,... | collective-permute-start | bytes 276488 | tf_op jit(solution)/shard_map/ppermute | solution.py:230
  39.6 0.6 fusion.1
  44.0 0.5 slice.41
  44.5 0.7 collective-permute-done.far_ref
  45.2 0.5 slice.40
  47.0 4.1 %all-to-all-done = bf16[16,112,128]{2,1,0:T(8,128)(2,1)S(1)} async-done(((bf16[16,112,128]{2,1,0:T(8,128)(2,1)}), bf16[16,112,128]{2,1,0:T(8,128)(2,1)S(1)}, u32[]{:S(2)}, u32[]{:S(2)}) %all-to-all-start) | async-done | bytes 458784 | tf_op jit(solution)/shard_map/all_to_all | solution.py:248
  51.1 32.5 %all_gather.4 = bf16[16,2,112,128]{3,2,0,1:T(8,128)(2,1)S(1)} all-gather(bf16[1,2,112,128]{3,2,0,1:T(8,128)(2,1)S(1)} %maximum_add_fusion), channel_id=1, replica_groups={{0,16,32,48,64,80,96,112,128,144,160,176,192,208,224,240},{256,272,288,..., dimensions={0}, use_global_device_ids=true | all-gather | bytes 974848 | tf_op jit(solution)/shard_map/all_gather | solution.py:251
  83.7 4.1 %collective-permute-start.4 = (bf16[16,112,128]{2,1,0:T(8,128)(2,1)S(1)}, bf16[16,112,128]{2,1,0:T(8,128)(2,1)S(1)}, u32[]{:S(2)}, u32[]{:S(2)}) collective-permute-start(bf16[16,112,128]{2,1,0:T(8,128)(2,1)S(1)} %get-tuple-element.16.own_ref), channel_id=1, source_target_pairs={{0,256},{16,272},{32,288},{48,304},{64,320},{80,336},{96,352},{112... | collective-permute-start | bytes 1376264 | tf_op jit(solution)/shard_map/ppermute | solution.py:253
  87.8 1.9 %collective-permute-start.7 = (bf16[16,112,128]{2,1,0:T(8,128)(2,1)S(1)}, bf16[16,112,128]{2,1,0:T(8,128)(2,1)S(1)}, u32[]{:S(2)}, u32[]{:S(2)}) collective-permute-start(bf16[16,112,128]{2,1,0:T(8,128)(2,1)S(1)} %get-tuple-element.15.own_ref), channel_id=1, source_target_pairs={{0,256},{16,272},{32,288},{48,304},{64,320},{80,336},{96,352},{112... | collective-permute-start | bytes 1376264 | tf_op jit(solution)/shard_map/ppermute | solution.py:253
  89.7 3.9 %collective-permute-done.4.other_ref = bf16[16,112,128]{2,1,0:T(8,128)(2,1)S(1)} collective-permute-done((bf16[16,112,128]{2,1,0:T(8,128)(2,1)S(1)}, bf16[16,112,128]{2,1,0:T(8,128)(2,1)S(1)}, u32[]{:S(2)}, u32[]{:S(2)}) %collective-permute-start.4) | collective-permute-done | bytes 458784 | tf_op jit(solution)/shard_map/ppermute | solution.py:253
  93.7 1.1 edge_rows.1
  94.7 14.9 %collective-permute-start.5 = (f32[4,8,720]{2,1,0:T(8,128)S(1)}, f32[4,8,720]{2,1,0:T(8,128)S(1)}, u32[]{:S(2)}, u32[]{:S(2)}) collective-permute-start(f32[4,8,720]{2,1,0:T(8,128)S(1)} %get-tuple-element.11), channel_id=1, source_target_pairs={{1,2},{2,1},{3,4},{4,3},{5,6},{6,5},{7,8},{8,7},{9,10},{10,9},{11,... | collective-permute-start | bytes 276488 | tf_op jit(solution)/shard_map/ppermute | solution.py:230
  109.7 1.9 %collective-permute-start.6 = (f32[4,8,720]{2,1,0:T(8,128)S(1)}, f32[4,8,720]{2,1,0:T(8,128)S(1)}, u32[]{:S(2)}, u32[]{:S(2)}) collective-permute-start(f32[4,8,720]{2,1,0:T(8,128)S(1)} %get-tuple-element.12), channel_id=1, source_target_pairs={{0,1},{1,0},{2,3},{3,2},{4,5},{5,4},{6,7},{7,6},{8,9},{9,8},{10,11... | collective-permute-start | bytes 276488 | tf_op jit(solution)/shard_map/ppermute | solution.py:231
  111.6 3.3 %one_hour.2.q_ref = f32[4,8,24,720]{3,2,1,0:T(8,128)S(1)} custom-call(s32[2]{0:T(128)S(1)} %pad_add_fusion.place_ref, f32[4,8,24,720]{3,2,1,0:T(8,128)S(1)} %copy-done, f32[4,8,720]{2,1,0:T(8,128)S(1)} %collective-permute-done.far_ref, f32[4,8,720]{2,1,0:T(8,128)S(1)} %collective-permute-done.1.near_ref, s32[24,720]{1,0:T(8,128)S(1)} %copy-done.2, ...), custom_call_target="tpu_custom_call" | custom-call | flops 11059200 | bytes 5594632 | tf_op jit(solution)/shard_map/one_hour/pallas_call | solution.py:191
  115.0 4.9 %one_hour.3 = f32[4,8,24,720]{3,2,1,0:T(8,128)} custom-call(s32[2]{0:T(128)S(1)} %pad_add_fusion.place_ref, f32[4,8,24,720]{3,2,1,0:T(8,128)S(1)} %one_hour.2.q_ref, f32[4,8,720]{2,1,0:T(8,128)S(1)} %collective-permute-done.5.far_ref, f32[4,8,720]{2,1,0:T(8,128)S(1)} %collective-permute-done.6.near_ref, s32[24,720]{1,0:T(8,128)S(1)} %copy-done.2, ...), custom_call_target="tpu_custom_call" | custom-call | flops 11059200 | bytes 5594632 | tf_op jit(solution)/shard_map/one_hour/pallas_call | solution.py:191
  (19 shorter events, 0.3 us)
Async XLA Ops:
  0.0 31.4 %copy-start = (f32[4,8,24,720]{3,2,1,0:T(8,128)S(1)}, f32[4,8,24,720]{3,2,1,0:T(8,128)}, u32[]{:S(2)}) copy-start(f32[4,8,24,720]{3,2,1,0:T(8,128)} %q_ref.3) | copy-start | bytes 6635524
  0.1 1.3 %copy-start.1 = (bf16[1,3,8,24,720]{4,3,2,1,0:T(8,128)(2,1)S(1)}, bf16[1,3,8,24,720]{4,3,2,1,0:T(8,128)(2,1)}, u32[]{:S(2)}) copy-start(bf16[1,3,8,24,720]{4,3,2,1,0:T(8,128)(2,1)} %field_ref.1) | copy-start | bytes 2488324
  1.4 38.1 %copy-start.3 = (s32[2]{0:T(128)S(1)}, s32[2]{0:T(128)}, u32[]{:S(2)}) copy-start(s32[2]{0:T(128)} %param.6) | copy-start | bytes 28
  2.1 13.4 %collective-permute-start.3 = (bf16[16,112,128]{2,1,0:T(8,128)(2,1)S(1)}, bf16[16,112,128]{2,1,0:T(8,128)(2,1)}, u32[]{:S(2)}, u32[]{:S(2)}) collective-permute-start(bf16[16,112,128]{2,1,0:T(8,128)(2,1)S(1)} %get-tuple-element.10), channel_id=1, source_target_pairs={{0,256},{16,272},{32,288},{48,304},{64,320},{80,336},{96,352},{112... | collective-permute-start | bytes 1376264 | tf_op jit(solution)/shard_map/ppermute | solution.py:239
  5.2 10.3 %collective-permute-start.2 = (bf16[16,112,128]{2,1,0:T(8,128)(2,1)S(1)}, bf16[16,112,128]{2,1,0:T(8,128)(2,1)}, u32[]{:S(2)}, u32[]{:S(2)}) collective-permute-start(bf16[16,112,128]{2,1,0:T(8,128)(2,1)S(1)} %get-tuple-element.9), channel_id=1, source_target_pairs={{240,224},{496,480},{241,225},{497,481},{242,226},{498,482},{243,2... | collective-permute-start | bytes 1376264 | tf_op jit(solution)/shard_map/ppermute | solution.py:240
  16.3 77.3 %copy-start.2 = (s32[24,720]{1,0:T(8,128)S(1)}, s32[24,720]{1,0:T(8,128)}, u32[]{:S(2)}) copy-start(s32[24,720]{1,0:T(8,128)} %mask_ref.5) | copy-start | bytes 207364
  16.3 34.7 %all-to-all-start = ((bf16[16,112,128]{2,1,0:T(8,128)(2,1)}), bf16[16,112,128]{2,1,0:T(8,128)(2,1)S(1)}, u32[]{:S(2)}, u32[]{:S(2)}) async-start(bf16[16,112,128]{2,1,0:T(8,128)(2,1)} %select_select_fusion), calls=%async_computation | async-start | bytes 917504 | tf_op jit(solution)/shard_map/all_to_all | solution.py:248
  31.6 12.4 %collective-permute-start.1 = (f32[4,8,720]{2,1,0:T(8,128)S(1)}, f32[4,8,720]{2,1,0:T(8,128)S(1)}, u32[]{:S(2)}, u32[]{:S(2)}) collective-permute-start(f32[4,8,720]{2,1,0:T(8,128)S(1)} %get-tuple-element.19), channel_id=1, source_target_pairs={{0,1},{1,0},{2,3},{3,2},{4,5},{5,4},{6,7},{7,6},{8,9},{9,8},{10,11... | collective-permute-start | bytes 276488 | tf_op jit(solution)/shard_map/ppermute | solution.py:231
  35.3 9.8 %collective-permute-start = (f32[4,8,720]{2,1,0:T(8,128)S(1)}, f32[4,8,720]{2,1,0:T(8,128)S(1)}, u32[]{:S(2)}, u32[]{:S(2)}) collective-permute-start(f32[4,8,720]{2,1,0:T(8,128)S(1)} %get-tuple-element.20), channel_id=1, source_target_pairs={{1,2},{2,1},{3,4},{4,3},{5,6},{6,5},{7,8},{8,7},{9,10},{10,9},{11,... | collective-permute-start | bytes 276488 | tf_op jit(solution)/shard_map/ppermute | solution.py:230
  83.7 10.0 %collective-permute-start.4 = (bf16[16,112,128]{2,1,0:T(8,128)(2,1)S(1)}, bf16[16,112,128]{2,1,0:T(8,128)(2,1)S(1)}, u32[]{:S(2)}, u32[]{:S(2)}) collective-permute-start(bf16[16,112,128]{2,1,0:T(8,128)(2,1)S(1)} %get-tuple-element.16.own_ref), channel_id=1, source_target_pairs={{0,256},{16,272},{32,288},{48,304},{64,320},{80,336},{96,352},{112... | collective-permute-start | bytes 1376264 | tf_op jit(solution)/shard_map/ppermute | solution.py:253
  87.8 27.1 %collective-permute-start.7 = (bf16[16,112,128]{2,1,0:T(8,128)(2,1)S(1)}, bf16[16,112,128]{2,1,0:T(8,128)(2,1)S(1)}, u32[]{:S(2)}, u32[]{:S(2)}) collective-permute-start(bf16[16,112,128]{2,1,0:T(8,128)(2,1)S(1)} %get-tuple-element.15.own_ref), channel_id=1, source_target_pairs={{0,256},{16,272},{32,288},{48,304},{64,320},{80,336},{96,352},{112... | collective-permute-start | bytes 1376264 | tf_op jit(solution)/shard_map/ppermute | solution.py:253
  94.7 20.2 %collective-permute-start.5 = (f32[4,8,720]{2,1,0:T(8,128)S(1)}, f32[4,8,720]{2,1,0:T(8,128)S(1)}, u32[]{:S(2)}, u32[]{:S(2)}) collective-permute-start(f32[4,8,720]{2,1,0:T(8,128)S(1)} %get-tuple-element.11), channel_id=1, source_target_pairs={{1,2},{2,1},{3,4},{4,3},{5,6},{6,5},{7,8},{8,7},{9,10},{10,9},{11,... | collective-permute-start | bytes 276488 | tf_op jit(solution)/shard_map/ppermute | solution.py:230
  109.7 5.3 %collective-permute-start.6 = (f32[4,8,720]{2,1,0:T(8,128)S(1)}, f32[4,8,720]{2,1,0:T(8,128)S(1)}, u32[]{:S(2)}, u32[]{:S(2)}) collective-permute-start(f32[4,8,720]{2,1,0:T(8,128)S(1)} %get-tuple-element.12), channel_id=1, source_target_pairs={{0,1},{1,0},{2,3},{3,2},{4,5},{5,4},{6,7},{7,6},{8,9},{9,8},{10,11... | collective-permute-start | bytes 276488 | tf_op jit(solution)/shard_map/ppermute | solution.py:231

commit v9 on v8

--- a/solution.py
+++ b/solution.py
@@ -12,6 +12,14 @@
 CUT = 40
 PIECE = 112
 VMEM_LIMIT = 48 * 1024 * 1024
+
+
+def this_column():
+    return lax.axis_index("vec") // RING
+
+
+def odd_band():
+    return lax.axis_index("lat") % 2
 
 
 def tile_parts(rows, half):
@@ -35,11 +43,11 @@
     return parts
 
 
-def pack_kernel(place_ref, field_ref, keep_ref, send_ref):
+def pack_kernel(field_ref, keep_ref, send_ref):
     _, levs, rows, lon = field_ref.shape[1:]
     for own in range(COLUMNS):
 
-        @pl.when(place_ref[0] == own)
+        @pl.when(this_column() == own)
         def _():
             for level in range(levs):
                 for half in range(2):
@@ -51,17 +59,17 @@
                         ]
 
 
-def pack(place, trajectory):
+def pack(trajectory):
     half = jax.ShapeDtypeStruct((RING, PIECE, LANES), trajectory.dtype)
     vmem = pl.BlockSpec(memory_space=pltpu.VMEM)
     return pl.pallas_call(
         pack_kernel,
         out_shape=(half, half),
-        in_specs=[pl.BlockSpec(memory_space=pltpu.SMEM), vmem],
+        in_specs=[vmem],
         out_specs=(vmem, vmem),
         compiler_params=pltpu.CompilerParams(vmem_limit_bytes=VMEM_LIMIT),
         name="pack",
-    )(place, trajectory)
+    )(trajectory)
 
 
 def lanes_next(x):
@@ -90,26 +98,26 @@
     return (wc * c + we * lanes_next(c) + ww * lanes_prev(c)) + (wn * n + ws * s + wl * (u + b))
 
 
-def set_halos(place_ref, near_ref, far_ref, south_ref, north_ref):
-    @pl.when(place_ref[1] == 1)
+def set_halos(near_ref, far_ref, south_ref, north_ref):
+    @pl.when(odd_band() == 1)
     def _():
         south_ref[...] = near_ref[...]
         north_ref[...] = far_ref[...]
 
-    @pl.when(place_ref[1] == 0)
+    @pl.when(odd_band() == 0)
     def _():
         south_ref[...] = far_ref[...]
         north_ref[...] = near_ref[...]
 
 
 def rows_kernel(
-    place_ref, q_ref, far_ref, near_ref, mask_ref, own_ref, other_ref,
+    q_ref, far_ref, near_ref, mask_ref, own_ref, other_ref,
     to_far_ref, to_near_ref, field_ref, south_ref, north_ref,
 ):
     vecs, levs, rows, lon = q_ref.shape
     lev = lax.broadcasted_iota(jnp.int32, (levs, lon), 0)
-    own_column, odd = place_ref[0], place_ref[1]
-    set_halos(place_ref, near_ref, far_ref, south_ref, north_ref)
+    own_column, odd = this_column(), odd_band()
+    set_halos(near_ref, far_ref, south_ref, north_ref)
 
     def row_of(v, r):
         return jnp.concatenate([q_ref[v, z, r : r + 1] for z in range(levs)], axis=0)
@@ -150,16 +158,20 @@
 
 
 def hour_kernel(
-    place_ref, q_ref, far_ref, near_ref, mask_ref, own_ref, other_ref,
-    out_ref, field_ref, south_ref, north_ref,
+    q_ref, far_ref, near_ref, mask_ref, own_ref, other_ref,
+    out_ref, field_ref, south_ref, north_ref, new_ref=None, sent=None,
 ):
     vecs, levs, rows, lon = q_ref.shape
     row = lax.broadcasted_iota(jnp.int32, (rows, lon), 0)
     mask = mask_ref[...].astype(jnp.float32)
-    own_column = place_ref[0]
-    set_halos(place_ref, near_ref, far_ref, south_ref, north_ref)
-
-    def level_step(level, carry):
+    own_column = this_column()
+    set_halos(near_ref, far_ref, south_ref, north_ref)
+    to_ref = out_ref if new_ref is None else new_ref
+
+    def sending(level):
+        return pltpu.make_async_copy(new_ref.at[:, level], out_ref.at[:, level], sent.at[level])
+
+    for level in range(levs):
         for own in range(COLUMNS):
 
             @pl.when(own_column == own)
@@ -172,31 +184,34 @@
                         ].astype(jnp.float32)
 
         weight = weights(*(field_ref[k, :, :lon] for k in range(FIELDS)), mask)
-        up = jnp.maximum(level - 1, 0)
-        low = jnp.minimum(level + 1, levs - 1)
+        up, low = max(level - 1, 0), min(level + 1, levs - 1)
         for v in range(vecs):
             c = q_ref[v, level]
-            n = jnp.where(row == rows - 1, north_ref[v, pl.ds(level, 1)], pltpu.roll(c, rows - 1, 0))
-            s = jnp.where(row == 0, south_ref[v, pl.ds(level, 1)], pltpu.roll(c, 1, 0))
-            out_ref[v, level] = advance(c, n, s, q_ref[v, up], q_ref[v, low], weight)
-        return carry
-
-    lax.fori_loop(0, levs, level_step, 0)
-
-
-def on_band(kernel, name, outs, field_rows, flops, args):
+            n = jnp.where(row == rows - 1, north_ref[v, level : level + 1], pltpu.roll(c, rows - 1, 0))
+            s = jnp.where(row == 0, south_ref[v, level : level + 1], pltpu.roll(c, 1, 0))
+            to_ref[v, level] = advance(c, n, s, q_ref[v, up], q_ref[v, low], weight)
+        if new_ref is not None:
+            sending(level).start()
+
+    if new_ref is not None:
+        for level in range(levs):
+            sending(level).wait()
+
+
+def on_band(kernel, name, outs, out_space, field_rows, flops, args, scratch=()):
     vmem = pl.BlockSpec(memory_space=pltpu.VMEM)
-    lon = args[1].shape[-1]
+    lon = args[0].shape[-1]
     bytes_accessed = sum(a.size * a.dtype.itemsize for a in (*args, *outs))
     return pl.pallas_call(
         kernel,
         out_shape=outs,
-        in_specs=[pl.BlockSpec(memory_space=pltpu.SMEM)] + [vmem] * (len(args) - 1),
-        out_specs=tuple(vmem for _ in outs),
+        in_specs=[vmem] * len(args),
+        out_specs=tuple(pl.BlockSpec(memory_space=out_space) for _ in outs),
         scratch_shapes=[
             pltpu.VMEM((FIELDS, field_rows, -(-lon // LANES) * LANES), jnp.float32),
-            pltpu.VMEM(args[2].shape, jnp.float32),
-            pltpu.VMEM(args[2].shape, jnp.float32),
+            pltpu.VMEM(args[1].shape, jnp.float32),
+            pltpu.VMEM(args[1].shape, jnp.float32),
+            *scratch,
         ],
         compiler_params=pltpu.CompilerParams(vmem_limit_bytes=VMEM_LIMIT),
         cost_estimate=pl.CostEstimate(flops=flops, bytes_accessed=bytes_accessed, transcendentals=0),
@@ -205,22 +220,28 @@
 
 
 def edge_rows(*args):
-    vecs, levs, _, lon = args[1].shape
+    vecs, levs, _, lon = args[0].shape
     edge = jax.ShapeDtypeStruct((vecs, levs, lon), jnp.float32)
-    return on_band(rows_kernel, "edge_rows", (edge, edge), levs, 30 * edge.size, args)
+    return on_band(rows_kernel, "edge_rows", (edge, edge), pltpu.VMEM, levs, 30 * edge.size, args)
 
 
 def one_hour(*args):
-    q = args[1]
-    return on_band(
-        hour_kernel, "one_hour", (jax.ShapeDtypeStruct(q.shape, q.dtype),), q.shape[2], 20 * q.size, args
-    )[0]
+    q = args[0]
+    out = jax.ShapeDtypeStruct(q.shape, q.dtype)
+    return on_band(hour_kernel, "one_hour", (out,), pltpu.VMEM, q.shape[2], 20 * q.size, args)[0]
+
+
+def last_hour(*args):
+    q = args[0]
+    out = jax.ShapeDtypeStruct(q.shape, q.dtype)
+    scratch = (pltpu.VMEM(q.shape, q.dtype), pltpu.SemaphoreType.DMA((q.shape[1],)))
+    return on_band(hour_kernel, "last_hour", (out,), pl.ANY, q.shape[2], 20 * q.size, args, scratch)[0]
 
 
 def shards(perturb, trajectory, hour_slot, sea_mask):
     lat = lax.axis_size("lat")
-    column = lax.axis_index("vec") // RING
-    odd = lax.axis_index("lat") % 2
+    column = this_column()
+    odd = odd_band()
     on_chip = [(i, i ^ 1) for i in range(lat)]
     between = [pair for i in range(1, lat - 1, 2) for pair in ((i, i + 1), (i + 1, i))]
     rings = [[c * RING + z for z in range(RING)] for c in range(COLUMNS)]
@@ -230,15 +251,14 @@
         far = lax.ppermute(to_far, "lat", between)
         return far, lax.ppermute(to_near, "lat", on_chip)
 
-    place_here = jnp.stack([column, odd]).astype(jnp.int32)
     first, last = perturb[:, :, 0], perturb[:, :, -1]
     halo = halos(jnp.where(odd == 1, last, first), jnp.where(odd == 1, first, last))
 
-    end, last_hour = RING - 1, COLUMNS * RING - 1
-    keep, send = pack(place_here, trajectory)
+    end, last_slot = RING - 1, COLUMNS * RING - 1
+    keep, send = pack(trajectory)
     crossed = lax.ppermute(send, "vec", swap)
     moved = lax.ppermute(keep, "vec", [(c * RING + end, c * RING + end - 1) for c in range(COLUMNS)])
-    asked = hour_slot[0] + hour_slot[1] - last_hour
+    asked = hour_slot[0] + hour_slot[1] - last_slot
     both = asked == end
     z = lax.axis_index("vec") % RING
     own_there = jnp.where(z == end, (column == 1) & ~both, asked // RING == column)
@@ -252,9 +272,9 @@
     own = [gathered[:, h] for h in range(2)]
     other = [lax.ppermute(half, "vec", swap) for half in own]
 
-    args = (place_here, perturb, *halo, sea_mask, own[0], other[0])
+    args = (perturb, *halo, sea_mask, own[0], other[0])
     halo = halos(*edge_rows(*args))
-    return one_hour(place_here, one_hour(*args), *halo, sea_mask, own[1], other[1])
+    return last_hour(one_hour(*args), *halo, sea_mask, own[1], other[1])
 
 
 def solution(mesh):

time: 121 us -> 118 us (0.975)
  Pallas kernels: 9.96 us -> 6.7 us
    pallas_call x4, Pallas kernels: 9.96 us -> 6.7 us  [the longest x3 6.54 us: on_band(): pl.pallas_call(kernel, out_shape=outs, in_specs=[vmem] * len(args), out_s...]
  transfers between devices with their start and end apart: 9 -> 9, of which waited for: 4 -> 4; matrix products, arithmetic and copies ran while one was open for 3% -> 3% of each run, Pallas kernels for 4% -> 3%
where the time goes in v9:
time: 118 us; the launch traced here: 116 us
  starting transfers between devices  50.4 us (43%)
  blocking collectives  32.5 us (28%)
  waiting for transfers between devices  14.9 us (13%)
  Pallas kernels  6.7 us (6%)
  between operations  6.5 us (6%)
  local copies, waits for them, and re-layouts  4.53 us (4%)
    all_gather x1, blocking collectives, shards(): gathered = lax.all_gather(picked, 'vec', axis=0, axis_index_groups=rings)  32.5 us
    ppermute x2, starting transfers between devices, halos(): far = lax.ppermute(to_far, 'lat', between)  19.1 us
    all_to_all x1, starting transfers between devices, shards(): lax.all_to_all(offered, 'vec', 0, 0, axis_index_groups=rings, tiled=True)  15 us
    pallas_call x3, Pallas kernels, on_band(): pl.pallas_call(kernel, out_shape=outs, in_specs=[vmem] * len(args), out_s...  6.54 us
    ppermute x1, waiting for transfers between devices, shards(): crossed = lax.ppermute(send, 'vec', swap)  6.22 us
    ppermute x2, starting transfers between devices, shards(): other = [lax.ppermute(half, 'vec', swap) for half in own]  6.05 us
    ppermute x2, starting transfers between devices, halos(): return (far, lax.ppermute(to_near, 'lat', on_chip))  5.66 us
    all_to_all x1, waiting for transfers between devices, shards(): lax.all_to_all(offered, 'vec', 0, 0, axis_index_groups=rings, tiled=True)  4.08 us
  transfers between devices with their start and end apart: 9, of which 4 were waited for; matrix products, arithmetic and copies ran while one was open for 3% of the time, Pallas kernels for 3%

profile of v9, /device:TPU:25, one launch (start us, length us, event | category | flops | bytes accessed | tf_op | source)
XLA Modules:
  0.0 116.5 jit_solution(10484378333015426272)
XLA Ops:
  0.0 1.3 %copy-done.1 = bf16[1,3,8,24,720]{4,3,2,1,0:T(8,128)(2,1)S(1)} copy-done((bf16[1,3,8,24,720]{4,3,2,1,0:T(8,128)(2,1)S(1)}, bf16[1,3,8,24,720]{4,3,2,1,0:T(8,128)(2,1)}, u32[]{:S(2)}) %copy-start.1) | copy-done | bytes 829464
  1.3 0.2 pack.1
  1.5 3.1 %collective-permute-start.3 = (bf16[16,112,128]{2,1,0:T(8,128)(2,1)S(1)}, bf16[16,112,128]{2,1,0:T(8,128)(2,1)}, u32[]{:S(2)}, u32[]{:S(2)}) collective-permute-start(bf16[16,112,128]{2,1,0:T(8,128)(2,1)S(1)} %get-tuple-element.10), channel_id=1, source_target_pairs={{0,256},{16,272},{32,288},{48,304},{64,320},{80,336},{96,352},{112... | collective-permute-start | bytes 1376264 | tf_op jit(solution)/shard_map/ppermute | solution.py:259
  4.6 1.4 %collective-permute-start.2 = (bf16[16,112,128]{2,1,0:T(8,128)(2,1)S(1)}, bf16[16,112,128]{2,1,0:T(8,128)(2,1)}, u32[]{:S(2)}, u32[]{:S(2)}) collective-permute-start(bf16[16,112,128]{2,1,0:T(8,128)(2,1)S(1)} %get-tuple-element.9), channel_id=1, source_target_pairs={{240,224},{496,480},{241,225},{497,481},{242,226},{498,482},{243,2... | collective-permute-start | bytes 1376264 | tf_op jit(solution)/shard_map/ppermute | solution.py:260
  6.0 1.3 %fusion.2 = (s32[1]{0:T(128)}, s32[1]{0:T(128)}) fusion(s32[2]{0:T(128)} %param.6), kind=kLoop, calls=%fused_computation.16 | loop fusion | bytes 16 | tf_op jit(solution)/shard_map/slice | solution.py:261
  8.6 6.2 %collective-permute-done.3 = bf16[16,112,128]{2,1,0:T(8,128)(2,1)} collective-permute-done((bf16[16,112,128]{2,1,0:T(8,128)(2,1)S(1)}, bf16[16,112,128]{2,1,0:T(8,128)(2,1)}, u32[]{:S(2)}, u32[]{:S(2)}) %collective-permute-start.3) | collective-permute-done | bytes 458784 | tf_op jit(solution)/shard_map/ppermute | solution.py:259
  14.9 0.8 select_select_fusion
  15.7 15.0 %all-to-all-start = ((bf16[16,112,128]{2,1,0:T(8,128)(2,1)}), bf16[16,112,128]{2,1,0:T(8,128)(2,1)S(1)}, u32[]{:S(2)}, u32[]{:S(2)}) async-start(bf16[16,112,128]{2,1,0:T(8,128)(2,1)} %select_select_fusion), calls=%async_computation | async-start | bytes 917504 | tf_op jit(solution)/shard_map/all_to_all | solution.py:268
  31.0 3.7 %collective-permute-start.1 = (f32[4,8,720]{2,1,0:T(8,128)S(1)}, f32[4,8,720]{2,1,0:T(8,128)S(1)}, u32[]{:S(2)}, u32[]{:S(2)}) collective-permute-start(f32[4,8,720]{2,1,0:T(8,128)S(1)} %get-tuple-element.19), channel_id=1, source_target_pairs={{0,1},{1,0},{2,3},{3,2},{4,5},{5,4},{6,7},{7,6},{8,9},{9,8},{10,11... | collective-permute-start | bytes 276488 | tf_op jit(solution)/shard_map/ppermute | solution.py:252
  34.7 4.2 %collective-permute-start = (f32[4,8,720]{2,1,0:T(8,128)S(1)}, f32[4,8,720]{2,1,0:T(8,128)S(1)}, u32[]{:S(2)}, u32[]{:S(2)}) collective-permute-start(f32[4,8,720]{2,1,0:T(8,128)S(1)} %get-tuple-element.20), channel_id=1, source_target_pairs={{1,2},{2,1},{3,4},{4,3},{5,6},{6,5},{7,8},{8,7},{9,10},{10,9},{11,... | collective-permute-start | bytes 276488 | tf_op jit(solution)/shard_map/ppermute | solution.py:251
  39.0 0.6 fusion.1
  43.3 0.5 slice.41
  43.9 0.7 collective-permute-done.far_ref
  44.6 0.5 slice.40
  46.3 4.1 %all-to-all-done = bf16[16,112,128]{2,1,0:T(8,128)(2,1)S(1)} async-done(((bf16[16,112,128]{2,1,0:T(8,128)(2,1)}), bf16[16,112,128]{2,1,0:T(8,128)(2,1)S(1)}, u32[]{:S(2)}, u32[]{:S(2)}) %all-to-all-start) | async-done | bytes 458784 | tf_op jit(solution)/shard_map/all_to_all | solution.py:268
  50.4 32.5 %all_gather.4 = bf16[16,2,112,128]{3,2,0,1:T(8,128)(2,1)S(1)} all-gather(bf16[1,2,112,128]{3,2,0,1:T(8,128)(2,1)S(1)} %maximum_add_fusion), channel_id=1, replica_groups={{0,16,32,48,64,80,96,112,128,144,160,176,192,208,224,240},{256,272,288,..., dimensions={0}, use_global_device_ids=true | all-gather | bytes 974848 | tf_op jit(solution)/shard_map/all_gather | solution.py:271
  83.0 4.1 %collective-permute-start.4 = (bf16[16,112,128]{2,1,0:T(8,128)(2,1)S(1)}, bf16[16,112,128]{2,1,0:T(8,128)(2,1)S(1)}, u32[]{:S(2)}, u32[]{:S(2)}) collective-permute-start(bf16[16,112,128]{2,1,0:T(8,128)(2,1)S(1)} %get-tuple-element.16.own_ref), channel_id=1, source_target_pairs={{0,256},{16,272},{32,288},{48,304},{64,320},{80,336},{96,352},{112... | collective-permute-start | bytes 1376264 | tf_op jit(solution)/shard_map/ppermute | solution.py:273
  87.2 1.9 %collective-permute-start.7 = (bf16[16,112,128]{2,1,0:T(8,128)(2,1)S(1)}, bf16[16,112,128]{2,1,0:T(8,128)(2,1)S(1)}, u32[]{:S(2)}, u32[]{:S(2)}) collective-permute-start(bf16[16,112,128]{2,1,0:T(8,128)(2,1)S(1)} %get-tuple-element.15.own_ref), channel_id=1, source_target_pairs={{0,256},{16,272},{32,288},{48,304},{64,320},{80,336},{96,352},{112... | collective-permute-start | bytes 1376264 | tf_op jit(solution)/shard_map/ppermute | solution.py:273
  89.1 3.9 %collective-permute-done.4.other_ref = bf16[16,112,128]{2,1,0:T(8,128)(2,1)S(1)} collective-permute-done((bf16[16,112,128]{2,1,0:T(8,128)(2,1)S(1)}, bf16[16,112,128]{2,1,0:T(8,128)(2,1)S(1)}, u32[]{:S(2)}, u32[]{:S(2)}) %collective-permute-start.4) | collective-permute-done | bytes 458784 | tf_op jit(solution)/shard_map/ppermute | solution.py:273
  93.0 0.5 edge_rows.1
  93.6 14.9 %collective-permute-start.5 = (f32[4,8,720]{2,1,0:T(8,128)S(1)}, f32[4,8,720]{2,1,0:T(8,128)S(1)}, u32[]{:S(2)}, u32[]{:S(2)}) collective-permute-start(f32[4,8,720]{2,1,0:T(8,128)S(1)} %get-tuple-element.11), channel_id=1, source_target_pairs={{1,2},{2,1},{3,4},{4,3},{5,6},{6,5},{7,8},{8,7},{9,10},{10,9},{11,... | collective-permute-start | bytes 276488 | tf_op jit(solution)/shard_map/ppermute | solution.py:251
  108.5 1.9 %collective-permute-start.6 = (f32[4,8,720]{2,1,0:T(8,128)S(1)}, f32[4,8,720]{2,1,0:T(8,128)S(1)}, u32[]{:S(2)}, u32[]{:S(2)}) collective-permute-start(f32[4,8,720]{2,1,0:T(8,128)S(1)} %get-tuple-element.12), channel_id=1, source_target_pairs={{0,1},{1,0},{2,3},{3,2},{4,5},{5,4},{6,7},{7,6},{8,9},{9,8},{10,11... | collective-permute-start | bytes 276488 | tf_op jit(solution)/shard_map/ppermute | solution.py:252
  110.4 2.5 %one_hour.1.q_ref = f32[4,8,24,720]{3,2,1,0:T(8,128)S(1)} custom-call(f32[4,8,24,720]{3,2,1,0:T(8,128)S(1)} %copy-done, f32[4,8,720]{2,1,0:T(8,128)S(1)} %collective-permute-done.far_ref, f32[4,8,720]{2,1,0:T(8,128)S(1)} %collective-permute-done.1.near_ref, s32[24,720]{1,0:T(8,128)S(1)} %copy-done.2, bf16[16,112,128]{2,1,0:T(8,128)(2,1)S(1)} %get-tuple-element.16.own_ref, ...), custom_call_target="tpu_custom_call" | custom-call | flops 11059200 | bytes 5594624 | tf_op jit(solution)/shard_map/one_hour/pallas_call | solution.py:205
  112.9 3.6 %last_hour.1 = f32[4,8,24,720]{3,2,1,0:T(8,128)} custom-call(f32[4,8,24,720]{3,2,1,0:T(8,128)S(1)} %one_hour.1.q_ref, f32[4,8,720]{2,1,0:T(8,128)S(1)} %collective-permute-done.5.far_ref, f32[4,8,720]{2,1,0:T(8,128)S(1)} %collective-permute-done.6.near_ref, s32[24,720]{1,0:T(8,128)S(1)} %copy-done.2, bf16[16,112,128]{2,1,0:T(8,128)(2,1)S(1)} %get-tuple-element.15.own_ref, ...), custom_call_target="tpu_custom_call" | custom-call | flops 11059200 | bytes 5594624 | tf_op jit(solution)/shard_map/last_hour/pallas_call | solution.py:205
  (18 shorter events, 0.3 us)
Async XLA Ops:
  0.0 30.8 %copy-start = (f32[4,8,24,720]{3,2,1,0:T(8,128)S(1)}, f32[4,8,24,720]{3,2,1,0:T(8,128)}, u32[]{:S(2)}) copy-start(f32[4,8,24,720]{3,2,1,0:T(8,128)} %q_ref.3) | copy-start | bytes 6635524
  0.0 1.3 %copy-start.1 = (bf16[1,3,8,24,720]{4,3,2,1,0:T(8,128)(2,1)S(1)}, bf16[1,3,8,24,720]{4,3,2,1,0:T(8,128)(2,1)}, u32[]{:S(2)}) copy-start(bf16[1,3,8,24,720]{4,3,2,1,0:T(8,128)(2,1)} %field_ref.1) | copy-start | bytes 2488324
  1.3 37.6 %copy-start.3 = (s32[2]{0:T(128)S(1)}, s32[2]{0:T(128)}, u32[]{:S(2)}) copy-start(s32[2]{0:T(128)} %param.6) | copy-start | bytes 28
  1.5 13.4 %collective-permute-start.3 = (bf16[16,112,128]{2,1,0:T(8,128)(2,1)S(1)}, bf16[16,112,128]{2,1,0:T(8,128)(2,1)}, u32[]{:S(2)}, u32[]{:S(2)}) collective-permute-start(bf16[16,112,128]{2,1,0:T(8,128)(2,1)S(1)} %get-tuple-element.10), channel_id=1, source_target_pairs={{0,256},{16,272},{32,288},{48,304},{64,320},{80,336},{96,352},{112... | collective-permute-start | bytes 1376264 | tf_op jit(solution)/shard_map/ppermute | solution.py:259
  4.6 10.3 %collective-permute-start.2 = (bf16[16,112,128]{2,1,0:T(8,128)(2,1)S(1)}, bf16[16,112,128]{2,1,0:T(8,128)(2,1)}, u32[]{:S(2)}, u32[]{:S(2)}) collective-permute-start(bf16[16,112,128]{2,1,0:T(8,128)(2,1)S(1)} %get-tuple-element.9), channel_id=1, source_target_pairs={{240,224},{496,480},{241,225},{497,481},{242,226},{498,482},{243,2... | collective-permute-start | bytes 1376264 | tf_op jit(solution)/shard_map/ppermute | solution.py:260
  15.7 77.3 %copy-start.2 = (s32[24,720]{1,0:T(8,128)S(1)}, s32[24,720]{1,0:T(8,128)}, u32[]{:S(2)}) copy-start(s32[24,720]{1,0:T(8,128)} %mask_ref.5) | copy-start | bytes 207364
  15.7 34.7 %all-to-all-start = ((bf16[16,112,128]{2,1,0:T(8,128)(2,1)}), bf16[16,112,128]{2,1,0:T(8,128)(2,1)S(1)}, u32[]{:S(2)}, u32[]{:S(2)}) async-start(bf16[16,112,128]{2,1,0:T(8,128)(2,1)} %select_select_fusion), calls=%async_computation | async-start | bytes 917504 | tf_op jit(solution)/shard_map/all_to_all | solution.py:268
  31.0 12.4 %collective-permute-start.1 = (f32[4,8,720]{2,1,0:T(8,128)S(1)}, f32[4,8,720]{2,1,0:T(8,128)S(1)}, u32[]{:S(2)}, u32[]{:S(2)}) collective-permute-start(f32[4,8,720]{2,1,0:T(8,128)S(1)} %get-tuple-element.19), channel_id=1, source_target_pairs={{0,1},{1,0},{2,3},{3,2},{4,5},{5,4},{6,7},{7,6},{8,9},{9,8},{10,11... | collective-permute-start | bytes 276488 | tf_op jit(solution)/shard_map/ppermute | solution.py:252
  34.7 9.8 %collective-permute-start = (f32[4,8,720]{2,1,0:T(8,128)S(1)}, f32[4,8,720]{2,1,0:T(8,128)S(1)}, u32[]{:S(2)}, u32[]{:S(2)}) collective-permute-start(f32[4,8,720]{2,1,0:T(8,128)S(1)} %get-tuple-element.20), channel_id=1, source_target_pairs={{1,2},{2,1},{3,4},{4,3},{5,6},{6,5},{7,8},{8,7},{9,10},{10,9},{11,... | collective-permute-start | bytes 276488 | tf_op jit(solution)/shard_map/ppermute | solution.py:251
  83.0 10.0 %collective-permute-start.4 = (bf16[16,112,128]{2,1,0:T(8,128)(2,1)S(1)}, bf16[16,112,128]{2,1,0:T(8,128)(2,1)S(1)}, u32[]{:S(2)}, u32[]{:S(2)}) collective-permute-start(bf16[16,112,128]{2,1,0:T(8,128)(2,1)S(1)} %get-tuple-element.16.own_ref), channel_id=1, source_target_pairs={{0,256},{16,272},{32,288},{48,304},{64,320},{80,336},{96,352},{112... | collective-permute-start | bytes 1376264 | tf_op jit(solution)/shard_map/ppermute | solution.py:273
  87.2 25.7 %collective-permute-start.7 = (bf16[16,112,128]{2,1,0:T(8,128)(2,1)S(1)}, bf16[16,112,128]{2,1,0:T(8,128)(2,1)S(1)}, u32[]{:S(2)}, u32[]{:S(2)}) collective-permute-start(bf16[16,112,128]{2,1,0:T(8,128)(2,1)S(1)} %get-tuple-element.15.own_ref), channel_id=1, source_target_pairs={{0,256},{16,272},{32,288},{48,304},{64,320},{80,336},{96,352},{112... | collective-permute-start | bytes 1376264 | tf_op jit(solution)/shard_map/ppermute | solution.py:273
  93.6 19.3 %collective-permute-start.5 = (f32[4,8,720]{2,1,0:T(8,128)S(1)}, f32[4,8,720]{2,1,0:T(8,128)S(1)}, u32[]{:S(2)}, u32[]{:S(2)}) collective-permute-start(f32[4,8,720]{2,1,0:T(8,128)S(1)} %get-tuple-element.11), channel_id=1, source_target_pairs={{1,2},{2,1},{3,4},{4,3},{5,6},{6,5},{7,8},{8,7},{9,10},{10,9},{11,... | collective-permute-start | bytes 276488 | tf_op jit(solution)/shard_map/ppermute | solution.py:251
  108.5 4.4 %collective-permute-start.6 = (f32[4,8,720]{2,1,0:T(8,128)S(1)}, f32[4,8,720]{2,1,0:T(8,128)S(1)}, u32[]{:S(2)}, u32[]{:S(2)}) collective-permute-start(f32[4,8,720]{2,1,0:T(8,128)S(1)} %get-tuple-element.12), channel_id=1, source_target_pairs={{0,1},{1,0},{2,3},{3,2},{4,5},{5,4},{6,7},{7,6},{8,9},{9,8},{10,11... | collective-permute-start | bytes 276488 | tf_op jit(solution)/shard_map/ppermute | solution.py:252

commit v10 on v9

--- a/solution.py
+++ b/solution.py
@@ -9,8 +9,9 @@
 RING = 16
 LANES = 128
 FIELDS = 3
-CUT = 40
-PIECE = 112
+FULL = 5
+TALL = 40
+PIECE = 104
 VMEM_LIMIT = 48 * 1024 * 1024
 
 
@@ -22,24 +23,29 @@
     return lax.axis_index("lat") % 2
 
 
-def tile_parts(rows, half):
+def level_parts(rows):
     total = FIELDS * rows
-    base = 3 * half
-    return (
-        (base, 0, total, 0, 0),
-        (base + 1, 0, CUT, 0, total),
-        (base + 1, CUT, total, 1, 0),
-        (base + 2, 0, total, 1, total - CUT),
-    )
+    parts = [(t * LANES, LANES, 0, total, t * total, 0) for t in range(FULL)]
+    lane, at = FULL * LANES, FULL * total
+    parts.append((lane, 64, 0, TALL, at, 0))
+    parts.append((lane, 64, TALL, total, at, 64))
+    lane, at = lane + 64, at + TALL
+    for start in range(0, total, 8):
+        down, across = divmod(start // 8, 8)
+        parts.append((lane, 16, start, start + 8, at + 8 * down, 16 * across))
+    return parts
 
 
 def field_parts(rows, half):
     parts = []
-    for tile, start, stop, column, at in tile_parts(rows, half):
+    for lane, lanes, start, stop, at, at_lane in level_parts(rows):
         for k in range(FIELDS):
-            lo, hi = max(start, k * rows), min(stop, (k + 1) * rows)
-            if lo < hi:
-                parts.append((k, tile, lo - k * rows, hi - k * rows, column, at + lo - start))
+            for column in range(COLUMNS):
+                top = (half * COLUMNS + column) * PIECE
+                lo = max(start, k * rows, start + top - at)
+                hi = min(stop, (k + 1) * rows, start + top + PIECE - at)
+                if lo < hi:
+                    parts.append((k, lane, lanes, lo - k * rows, hi - k * rows, column, at + lo - start - top, at_lane))
     return parts
 
 
@@ -51,11 +57,10 @@
         def _():
             for level in range(levs):
                 for half in range(2):
-                    for k, tile, lo, hi, column, at in field_parts(rows, half):
+                    for k, lane, lanes, lo, hi, column, at, at_lane in field_parts(rows, half):
                         piece_ref = keep_ref if column == own else send_ref
-                        left, right = tile * LANES, min((tile + 1) * LANES, lon)
-                        piece_ref[level * 2 + half, at : at + hi - lo, : right - left] = field_ref[
-                            0, k, level, lo:hi, left:right
+                        piece_ref[level * 2 + half, at : at + hi - lo, at_lane : at_lane + lanes] = field_ref[
+                            0, k, level, lo:hi, lane : lane + lanes
                         ]
 
 
@@ -128,14 +133,16 @@
             @pl.when(own_column == own)
             def _():
                 for half in range(2):
-                    for k, tile, lo, hi, column, at in field_parts(rows, half):
+                    for k, lane, lanes, lo, hi, column, at, at_lane in field_parts(rows, half):
                         if lo <= r < hi:
                             piece_ref = own_ref if column == own else other_ref
                             base = at + (r - lo) // 8 * 8
                             for z in range(levs):
                                 eight = piece_ref[z * 2 + half, base : base + 8].astype(jnp.float32)
                                 i = (r - lo) % 8
-                                field_ref[k, z : z + 1, tile * LANES : (tile + 1) * LANES] = eight[i : i + 1]
+                                field_ref[k, z : z + 1, lane : lane + lanes] = eight[
+                                    i : i + 1, at_lane : at_lane + lanes
+                                ]
 
         weight = weights(*(field_ref[k, :, :lon] for k in range(FIELDS)), mask_ref[r : r + 1].astype(jnp.float32))
         new = []
@@ -177,11 +184,10 @@
             @pl.when(own_column == own)
             def _():
                 for half in range(2):
-                    for k, tile, lo, hi, column, at in field_parts(rows, half):
+                    for k, lane, lanes, lo, hi, column, at, at_lane in field_parts(rows, half):
                         piece_ref = own_ref if column == own else other_ref
-                        field_ref[k, lo:hi, tile * LANES : (tile + 1) * LANES] = piece_ref[
-                            level * 2 + half, at : at + hi - lo
-                        ].astype(jnp.float32)
+                        part = piece_ref[level * 2 + half, at : at + hi - lo].astype(jnp.float32)
+                        field_ref[k, lo:hi, lane : lane + lanes] = part[:, at_lane : at_lane + lanes]
 
         weight = weights(*(field_ref[k, :, :lon] for k in range(FIELDS)), mask)
         up, low = max(level - 1, 0), min(level + 1, levs - 1)

time: 118 us -> 115 us (0.975)
  waiting for transfers between devices: 14.9 us -> 12.4 us
    all_to_all x1, waiting for transfers between devices: 4.08 us -> 2.67 us  [shards(): lax.all_to_all(offered, 'vec', 0, 0, axis_index_groups=rings, tiled=True)]
where the time goes in v10:
time: 115 us; the launch traced here: 113 us
  starting transfers between devices  49.3 us (43%)
  blocking collectives  32 us (28%)
  waiting for transfers between devices  12.4 us (11%)
  Pallas kernels  7.83 us (7%)
  between operations  6.54 us (6%)
  local copies, waits for them, and re-layouts  4.53 us (4%)
    all_gather x1, blocking collectives, shards(): gathered = lax.all_gather(picked, 'vec', axis=0, axis_index_groups=rings)  32 us
    ppermute x2, starting transfers between devices, halos(): far = lax.ppermute(to_far, 'lat', between)  18 us
    all_to_all x1, starting transfers between devices, shards(): lax.all_to_all(offered, 'vec', 0, 0, axis_index_groups=rings, tiled=True)  15 us
    pallas_call x3, Pallas kernels, on_band(): pl.pallas_call(kernel, out_shape=outs, in_specs=[vmem] * len(args), out_s...  7.63 us
    ppermute x2, starting transfers between devices, shards(): other = [lax.ppermute(half, 'vec', swap) for half in own]  6.04 us
    ppermute x2, starting transfers between devices, halos(): return (far, lax.ppermute(to_near, 'lat', on_chip))  5.66 us
    ppermute x1, waiting for transfers between devices, shards(): crossed = lax.ppermute(send, 'vec', swap)  5.5 us
    ppermute x2, waiting for transfers between devices, shards(): other = [lax.ppermute(half, 'vec', swap) for half in own]  3.58 us
  transfers between devices with their start and end apart: 9, of which 4 were waited for; matrix products, arithmetic and copies ran while one was open for 3% of the time, Pallas kernels for 3%

profile of v10, /device:TPU:25, one launch (start us, length us, event | category | flops | bytes accessed | tf_op | source)
XLA Modules:
  0.0 113.4 jit_solution(9914650668841675695)
XLA Ops:
  0.0 1.3 %copy-done.1 = bf16[1,3,8,24,720]{4,3,2,1,0:T(8,128)(2,1)S(1)} copy-done((bf16[1,3,8,24,720]{4,3,2,1,0:T(8,128)(2,1)S(1)}, bf16[1,3,8,24,720]{4,3,2,1,0:T(8,128)(2,1)}, u32[]{:S(2)}) %copy-start.1) | copy-done | bytes 829464
  1.3 0.2 pack.1
  1.5 3.1 %collective-permute-start.3 = (bf16[16,104,128]{2,1,0:T(8,128)(2,1)S(1)}, bf16[16,104,128]{2,1,0:T(8,128)(2,1)}, u32[]{:S(2)}, u32[]{:S(2)}) collective-permute-start(bf16[16,104,128]{2,1,0:T(8,128)(2,1)S(1)} %get-tuple-element.10), channel_id=1, source_target_pairs={{0,256},{16,272},{32,288},{48,304},{64,320},{80,336},{96,352},{112... | collective-permute-start | bytes 1277960 | tf_op jit(solution)/shard_map/ppermute | solution.py:265
  4.6 1.4 %collective-permute-start.2 = (bf16[16,104,128]{2,1,0:T(8,128)(2,1)S(1)}, bf16[16,104,128]{2,1,0:T(8,128)(2,1)}, u32[]{:S(2)}, u32[]{:S(2)}) collective-permute-start(bf16[16,104,128]{2,1,0:T(8,128)(2,1)S(1)} %get-tuple-element.9), channel_id=1, source_target_pairs={{240,224},{496,480},{241,225},{497,481},{242,226},{498,482},{243,2... | collective-permute-start | bytes 1277960 | tf_op jit(solution)/shard_map/ppermute | solution.py:266
  6.1 1.3 %fusion.2 = (s32[1]{0:T(128)}, s32[1]{0:T(128)}) fusion(s32[2]{0:T(128)} %param.6), kind=kLoop, calls=%fused_computation.16 | loop fusion | bytes 16 | tf_op jit(solution)/shard_map/slice | solution.py:267
  8.7 5.5 %collective-permute-done.3 = bf16[16,104,128]{2,1,0:T(8,128)(2,1)} collective-permute-done((bf16[16,104,128]{2,1,0:T(8,128)(2,1)S(1)}, bf16[16,104,128]{2,1,0:T(8,128)(2,1)}, u32[]{:S(2)}, u32[]{:S(2)}) %collective-permute-start.3) | collective-permute-done | bytes 426016 | tf_op jit(solution)/shard_map/ppermute | solution.py:265
  14.2 0.8 select_select_fusion
  15.0 15.0 %all-to-all-start = ((bf16[16,104,128]{2,1,0:T(8,128)(2,1)}), bf16[16,104,128]{2,1,0:T(8,128)(2,1)S(1)}, u32[]{:S(2)}, u32[]{:S(2)}) async-start(bf16[16,104,128]{2,1,0:T(8,128)(2,1)} %select_select_fusion), calls=%async_computation | async-start | bytes 851968 | tf_op jit(solution)/shard_map/all_to_all | solution.py:274
  30.3 3.7 %collective-permute-start.1 = (f32[4,8,720]{2,1,0:T(8,128)S(1)}, f32[4,8,720]{2,1,0:T(8,128)S(1)}, u32[]{:S(2)}, u32[]{:S(2)}) collective-permute-start(f32[4,8,720]{2,1,0:T(8,128)S(1)} %get-tuple-element.19), channel_id=1, source_target_pairs={{0,1},{1,0},{2,3},{3,2},{4,5},{5,4},{6,7},{7,6},{8,9},{9,8},{10,11... | collective-permute-start | bytes 276488 | tf_op jit(solution)/shard_map/ppermute | solution.py:258
  34.0 4.2 %collective-permute-start = (f32[4,8,720]{2,1,0:T(8,128)S(1)}, f32[4,8,720]{2,1,0:T(8,128)S(1)}, u32[]{:S(2)}, u32[]{:S(2)}) collective-permute-start(f32[4,8,720]{2,1,0:T(8,128)S(1)} %get-tuple-element.20), channel_id=1, source_target_pairs={{1,2},{2,1},{3,4},{4,3},{5,6},{6,5},{7,8},{8,7},{9,10},{10,9},{11,... | collective-permute-start | bytes 276488 | tf_op jit(solution)/shard_map/ppermute | solution.py:257
  38.3 0.6 fusion.1
  42.7 0.5 slice.41
  43.2 0.7 collective-permute-done.far_ref
  43.9 0.5 slice.40
  45.7 2.7 %all-to-all-done = bf16[16,104,128]{2,1,0:T(8,128)(2,1)S(1)} async-done(((bf16[16,104,128]{2,1,0:T(8,128)(2,1)}), bf16[16,104,128]{2,1,0:T(8,128)(2,1)S(1)}, u32[]{:S(2)}, u32[]{:S(2)}) %all-to-all-start) | async-done | bytes 426016 | tf_op jit(solution)/shard_map/all_to_all | solution.py:274
  48.3 32.0 %all_gather.4 = bf16[16,2,104,128]{3,2,0,1:T(8,128)(2,1)S(1)} all-gather(bf16[1,2,104,128]{3,2,0,1:T(8,128)(2,1)S(1)} %maximum_add_fusion), channel_id=1, replica_groups={{0,16,32,48,64,80,96,112,128,144,160,176,192,208,224,240},{256,272,288,..., dimensions={0}, use_global_device_ids=true | all-gather | bytes 905216 | tf_op jit(solution)/shard_map/all_gather | solution.py:277
  80.4 4.1 %collective-permute-start.4 = (bf16[16,104,128]{2,1,0:T(8,128)(2,1)S(1)}, bf16[16,104,128]{2,1,0:T(8,128)(2,1)S(1)}, u32[]{:S(2)}, u32[]{:S(2)}) collective-permute-start(bf16[16,104,128]{2,1,0:T(8,128)(2,1)S(1)} %get-tuple-element.16.own_ref), channel_id=1, source_target_pairs={{0,256},{16,272},{32,288},{48,304},{64,320},{80,336},{96,352},{112... | collective-permute-start | bytes 1277960 | tf_op jit(solution)/shard_map/ppermute | solution.py:279
  84.5 1.9 %collective-permute-start.7 = (bf16[16,104,128]{2,1,0:T(8,128)(2,1)S(1)}, bf16[16,104,128]{2,1,0:T(8,128)(2,1)S(1)}, u32[]{:S(2)}, u32[]{:S(2)}) collective-permute-start(bf16[16,104,128]{2,1,0:T(8,128)(2,1)S(1)} %get-tuple-element.15.own_ref), channel_id=1, source_target_pairs={{0,256},{16,272},{32,288},{48,304},{64,320},{80,336},{96,352},{112... | collective-permute-start | bytes 1277960 | tf_op jit(solution)/shard_map/ppermute | solution.py:279
  86.4 3.6 %collective-permute-done.4.other_ref = bf16[16,104,128]{2,1,0:T(8,128)(2,1)S(1)} collective-permute-done((bf16[16,104,128]{2,1,0:T(8,128)(2,1)S(1)}, bf16[16,104,128]{2,1,0:T(8,128)(2,1)S(1)}, u32[]{:S(2)}, u32[]{:S(2)}) %collective-permute-start.4) | collective-permute-done | bytes 426016 | tf_op jit(solution)/shard_map/ppermute | solution.py:279
  90.0 0.6 edge_rows.1
  90.6 13.8 %collective-permute-start.5 = (f32[4,8,720]{2,1,0:T(8,128)S(1)}, f32[4,8,720]{2,1,0:T(8,128)S(1)}, u32[]{:S(2)}, u32[]{:S(2)}) collective-permute-start(f32[4,8,720]{2,1,0:T(8,128)S(1)} %get-tuple-element.11), channel_id=1, source_target_pairs={{1,2},{2,1},{3,4},{4,3},{5,6},{6,5},{7,8},{8,7},{9,10},{10,9},{11,... | collective-permute-start | bytes 276488 | tf_op jit(solution)/shard_map/ppermute | solution.py:257
  104.4 1.9 %collective-permute-start.6 = (f32[4,8,720]{2,1,0:T(8,128)S(1)}, f32[4,8,720]{2,1,0:T(8,128)S(1)}, u32[]{:S(2)}, u32[]{:S(2)}) collective-permute-start(f32[4,8,720]{2,1,0:T(8,128)S(1)} %get-tuple-element.12), channel_id=1, source_target_pairs={{0,1},{1,0},{2,3},{3,2},{4,5},{5,4},{6,7},{7,6},{8,9},{9,8},{10,11... | collective-permute-start | bytes 276488 | tf_op jit(solution)/shard_map/ppermute | solution.py:258
  106.3 3.0 %one_hour.1.q_ref = f32[4,8,24,720]{3,2,1,0:T(8,128)S(1)} custom-call(f32[4,8,24,720]{3,2,1,0:T(8,128)S(1)} %copy-done, f32[4,8,720]{2,1,0:T(8,128)S(1)} %collective-permute-done.far_ref, f32[4,8,720]{2,1,0:T(8,128)S(1)} %collective-permute-done.1.near_ref, s32[24,720]{1,0:T(8,128)S(1)} %copy-done.2, bf16[16,104,128]{2,1,0:T(8,128)(2,1)S(1)} %get-tuple-element.16.own_ref, ...), custom_call_target="tpu_custom_call" | custom-call | flops 11059200 | bytes 5529088 | tf_op jit(solution)/shard_map/one_hour/pallas_call | solution.py:211
  109.3 4.1 %last_hour.1 = f32[4,8,24,720]{3,2,1,0:T(8,128)} custom-call(f32[4,8,24,720]{3,2,1,0:T(8,128)S(1)} %one_hour.1.q_ref, f32[4,8,720]{2,1,0:T(8,128)S(1)} %collective-permute-done.5.far_ref, f32[4,8,720]{2,1,0:T(8,128)S(1)} %collective-permute-done.6.near_ref, s32[24,720]{1,0:T(8,128)S(1)} %copy-done.2, bf16[16,104,128]{2,1,0:T(8,128)(2,1)S(1)} %get-tuple-element.15.own_ref, ...), custom_call_target="tpu_custom_call" | custom-call | flops 11059200 | bytes 5529088 | tf_op jit(solution)/shard_map/last_hour/pallas_call | solution.py:211
  (18 shorter events, 0.3 us)
Async XLA Ops:
  0.0 30.1 %copy-start = (f32[4,8,24,720]{3,2,1,0:T(8,128)S(1)}, f32[4,8,24,720]{3,2,1,0:T(8,128)}, u32[]{:S(2)}) copy-start(f32[4,8,24,720]{3,2,1,0:T(8,128)} %q_ref.3) | copy-start | bytes 6635524
  0.0 1.3 %copy-start.1 = (bf16[1,3,8,24,720]{4,3,2,1,0:T(8,128)(2,1)S(1)}, bf16[1,3,8,24,720]{4,3,2,1,0:T(8,128)(2,1)}, u32[]{:S(2)}) copy-start(bf16[1,3,8,24,720]{4,3,2,1,0:T(8,128)(2,1)} %field_ref.1) | copy-start | bytes 2488324
  1.3 36.9 %copy-start.3 = (s32[2]{0:T(128)S(1)}, s32[2]{0:T(128)}, u32[]{:S(2)}) copy-start(s32[2]{0:T(128)} %param.6) | copy-start | bytes 28
  1.5 12.7 %collective-permute-start.3 = (bf16[16,104,128]{2,1,0:T(8,128)(2,1)S(1)}, bf16[16,104,128]{2,1,0:T(8,128)(2,1)}, u32[]{:S(2)}, u32[]{:S(2)}) collective-permute-start(bf16[16,104,128]{2,1,0:T(8,128)(2,1)S(1)} %get-tuple-element.10), channel_id=1, source_target_pairs={{0,256},{16,272},{32,288},{48,304},{64,320},{80,336},{96,352},{112... | collective-permute-start | bytes 1277960 | tf_op jit(solution)/shard_map/ppermute | solution.py:265
  4.6 9.6 %collective-permute-start.2 = (bf16[16,104,128]{2,1,0:T(8,128)(2,1)S(1)}, bf16[16,104,128]{2,1,0:T(8,128)(2,1)}, u32[]{:S(2)}, u32[]{:S(2)}) collective-permute-start(bf16[16,104,128]{2,1,0:T(8,128)(2,1)S(1)} %get-tuple-element.9), channel_id=1, source_target_pairs={{240,224},{496,480},{241,225},{497,481},{242,226},{498,482},{243,2... | collective-permute-start | bytes 1277960 | tf_op jit(solution)/shard_map/ppermute | solution.py:266
  15.0 75.0 %copy-start.2 = (s32[24,720]{1,0:T(8,128)S(1)}, s32[24,720]{1,0:T(8,128)}, u32[]{:S(2)}) copy-start(s32[24,720]{1,0:T(8,128)} %mask_ref.5) | copy-start | bytes 207364
  15.0 33.3 %all-to-all-start = ((bf16[16,104,128]{2,1,0:T(8,128)(2,1)}), bf16[16,104,128]{2,1,0:T(8,128)(2,1)S(1)}, u32[]{:S(2)}, u32[]{:S(2)}) async-start(bf16[16,104,128]{2,1,0:T(8,128)(2,1)} %select_select_fusion), calls=%async_computation | async-start | bytes 851968 | tf_op jit(solution)/shard_map/all_to_all | solution.py:274
  30.3 12.4 %collective-permute-start.1 = (f32[4,8,720]{2,1,0:T(8,128)S(1)}, f32[4,8,720]{2,1,0:T(8,128)S(1)}, u32[]{:S(2)}, u32[]{:S(2)}) collective-permute-start(f32[4,8,720]{2,1,0:T(8,128)S(1)} %get-tuple-element.19), channel_id=1, source_target_pairs={{0,1},{1,0},{2,3},{3,2},{4,5},{5,4},{6,7},{7,6},{8,9},{9,8},{10,11... | collective-permute-start | bytes 276488 | tf_op jit(solution)/shard_map/ppermute | solution.py:258
  34.0 9.8 %collective-permute-start = (f32[4,8,720]{2,1,0:T(8,128)S(1)}, f32[4,8,720]{2,1,0:T(8,128)S(1)}, u32[]{:S(2)}, u32[]{:S(2)}) collective-permute-start(f32[4,8,720]{2,1,0:T(8,128)S(1)} %get-tuple-element.20), channel_id=1, source_target_pairs={{1,2},{2,1},{3,4},{4,3},{5,6},{6,5},{7,8},{8,7},{9,10},{10,9},{11,... | collective-permute-start | bytes 276488 | tf_op jit(solution)/shard_map/ppermute | solution.py:257
  80.4 9.6 %collective-permute-start.4 = (bf16[16,104,128]{2,1,0:T(8,128)(2,1)S(1)}, bf16[16,104,128]{2,1,0:T(8,128)(2,1)S(1)}, u32[]{:S(2)}, u32[]{:S(2)}) collective-permute-start(bf16[16,104,128]{2,1,0:T(8,128)(2,1)S(1)} %get-tuple-element.16.own_ref), channel_id=1, source_target_pairs={{0,256},{16,272},{32,288},{48,304},{64,320},{80,336},{96,352},{112... | collective-permute-start | bytes 1277960 | tf_op jit(solution)/shard_map/ppermute | solution.py:279
  84.5 24.8 %collective-permute-start.7 = (bf16[16,104,128]{2,1,0:T(8,128)(2,1)S(1)}, bf16[16,104,128]{2,1,0:T(8,128)(2,1)S(1)}, u32[]{:S(2)}, u32[]{:S(2)}) collective-permute-start(bf16[16,104,128]{2,1,0:T(8,128)(2,1)S(1)} %get-tuple-element.15.own_ref), channel_id=1, source_target_pairs={{0,256},{16,272},{32,288},{48,304},{64,320},{80,336},{96,352},{112... | collective-permute-start | bytes 1277960 | tf_op jit(solution)/shard_map/ppermute | solution.py:279
  90.6 18.7 %collective-permute-start.5 = (f32[4,8,720]{2,1,0:T(8,128)S(1)}, f32[4,8,720]{2,1,0:T(8,128)S(1)}, u32[]{:S(2)}, u32[]{:S(2)}) collective-permute-start(f32[4,8,720]{2,1,0:T(8,128)S(1)} %get-tuple-element.11), channel_id=1, source_target_pairs={{1,2},{2,1},{3,4},{4,3},{5,6},{6,5},{7,8},{8,7},{9,10},{10,9},{11,... | collective-permute-start | bytes 276488 | tf_op jit(solution)/shard_map/ppermute | solution.py:257
  104.4 4.9 %collective-permute-start.6 = (f32[4,8,720]{2,1,0:T(8,128)S(1)}, f32[4,8,720]{2,1,0:T(8,128)S(1)}, u32[]{:S(2)}, u32[]{:S(2)}) collective-permute-start(f32[4,8,720]{2,1,0:T(8,128)S(1)} %get-tuple-element.12), channel_id=1, source_target_pairs={{0,1},{1,0},{2,3},{3,2},{4,5},{5,4},{6,7},{7,6},{8,9},{9,8},{10,11... | collective-permute-start | bytes 276488 | tf_op jit(solution)/shard_map/ppermute | solution.py:258

commit v11 on v10

--- a/solution.py
+++ b/solution.py
@@ -1,3 +1,5 @@
+import functools
+
 import jax
 import jax.numpy as jnp
 from jax import lax
@@ -115,6 +117,42 @@
         north_ref[...] = near_ref[...]
 
 
+def pick_kernel(rows, own_ref, rows_ref, half_ref):
+    levs = rows_ref.shape[2]
+    half_ref[...] = own_ref[...]
+    for own in range(COLUMNS):
+
+        @pl.when(this_column() == own)
+        def _():
+            for i, r in enumerate((0, rows - 1)):
+                for half in range(2):
+                    for k, lane, lanes, lo, hi, column, at, at_lane in field_parts(rows, half):
+                        if column == own and lo <= r < hi:
+                            base, down = at + (r - lo) // 8 * 8, (r - lo) % 8
+                            picked = [
+                                own_ref[z * 2 + half, base : base + 8].astype(jnp.float32)[down : down + 1]
+                                for z in range(levs)
+                            ]
+                            rows_ref[i, k, :, lane : lane + lanes] = jnp.concatenate(picked, axis=0)[
+                                :, at_lane : at_lane + lanes
+                            ].astype(rows_ref.dtype)
+
+
+def pick(own, levs, rows):
+    vmem = pl.BlockSpec(memory_space=pltpu.VMEM)
+    return pl.pallas_call(
+        functools.partial(pick_kernel, rows),
+        out_shape=(
+            jax.ShapeDtypeStruct((2, FIELDS, levs, (FULL + 1) * LANES), own.dtype),
+            jax.ShapeDtypeStruct(own.shape, own.dtype),
+        ),
+        in_specs=[vmem],
+        out_specs=(vmem, vmem),
+        compiler_params=pltpu.CompilerParams(vmem_limit_bytes=VMEM_LIMIT),
+        name="pick",
+    )(own)
+
+
 def rows_kernel(
     q_ref, far_ref, near_ref, mask_ref, own_ref, other_ref,
     to_far_ref, to_near_ref, field_ref, south_ref, north_ref,
@@ -127,22 +165,18 @@
     def row_of(v, r):
         return jnp.concatenate([q_ref[v, z, r : r + 1] for z in range(levs)], axis=0)
 
-    for r, step in ((0, 1), (rows - 1, -1)):
+    for i, r, step in ((0, 0, 1), (1, rows - 1, -1)):
         for own in range(COLUMNS):
 
             @pl.when(own_column == own)
             def _():
                 for half in range(2):
-                    for k, lane, lanes, lo, hi, column, at, at_lane in field_parts(rows, half):
+                    for k, lane, lanes, lo, hi, column, _, _ in field_parts(rows, half):
                         if lo <= r < hi:
-                            piece_ref = own_ref if column == own else other_ref
-                            base = at + (r - lo) // 8 * 8
-                            for z in range(levs):
-                                eight = piece_ref[z * 2 + half, base : base + 8].astype(jnp.float32)
-                                i = (r - lo) % 8
-                                field_ref[k, z : z + 1, lane : lane + lanes] = eight[
-                                    i : i + 1, at_lane : at_lane + lanes
-                                ]
+                            picked_ref = own_ref if column == own else other_ref
+                            field_ref[k, :, lane : lane + lanes] = picked_ref[i, k, :, lane : lane + lanes].astype(
+                                jnp.float32
+                            )
 
         weight = weights(*(field_ref[k, :, :lon] for k in range(FIELDS)), mask_ref[r : r + 1].astype(jnp.float32))
         new = []
@@ -178,17 +212,7 @@
     def sending(level):
         return pltpu.make_async_copy(new_ref.at[:, level], out_ref.at[:, level], sent.at[level])
 
-    for level in range(levs):
-        for own in range(COLUMNS):
-
-            @pl.when(own_column == own)
-            def _():
-                for half in range(2):
-                    for k, lane, lanes, lo, hi, column, at, at_lane in field_parts(rows, half):
-                        piece_ref = own_ref if column == own else other_ref
-                        part = piece_ref[level * 2 + half, at : at + hi - lo].astype(jnp.float32)
-                        field_ref[k, lo:hi, lane : lane + lanes] = part[:, at_lane : at_lane + lanes]
-
+    def step(level):
         weight = weights(*(field_ref[k, :, :lon] for k in range(FIELDS)), mask)
         up, low = max(level - 1, 0), min(level + 1, levs - 1)
         for v in range(vecs):
@@ -198,6 +222,18 @@
             to_ref[v, level] = advance(c, n, s, q_ref[v, up], q_ref[v, low], weight)
         if new_ref is not None:
             sending(level).start()
+
+    for own in range(COLUMNS):
+
+        @pl.when(own_column == own)
+        def _():
+            for level in range(levs):
+                for half in range(2):
+                    for k, lane, lanes, lo, hi, column, at, at_lane in field_parts(rows, half):
+                        piece_ref = own_ref if column == own else other_ref
+                        part = piece_ref[level * 2 + half, at : at + hi - lo].astype(jnp.float32)
+                        field_ref[k, lo:hi, lane : lane + lanes] = part[:, at_lane : at_lane + lanes]
+                step(level)
 
     if new_ref is not None:
         for level in range(levs):
@@ -276,11 +312,14 @@
     picked = picked + (sum(h[0, 0, 0] for h in halo) * 0).astype(picked.dtype)
     gathered = lax.all_gather(picked, "vec", axis=0, axis_index_groups=rings)
     own = [gathered[:, h] for h in range(2)]
-    other = [lax.ppermute(half, "vec", swap) for half in own]
-
-    args = (perturb, *halo, sea_mask, own[0], other[0])
-    halo = halos(*edge_rows(*args))
-    return last_hour(one_hour(*args), *halo, sea_mask, own[1], other[1])
+    own_rows, half = pick(own[0], perturb.shape[1], perturb.shape[2])
+    other_rows = lax.ppermute(own_rows, "vec", swap)
+    late = jnp.where(column == 0, other_rows[0, 0, 0, 2 * LANES], other_rows[0, 0, 0, 0]) * 0
+    other = [lax.ppermute(half, "vec", swap), lax.ppermute(own[1] + late, "vec", swap)]
+
+    next_halo = halos(*edge_rows(perturb, *halo, sea_mask, own_rows, other_rows))
+    q = one_hour(perturb, *halo, sea_mask, own[0], other[0])
+    return last_hour(q, *next_halo, sea_mask, own[1], other[1])
 
 
 def solution(mesh):

time: 115 us -> 120 us (1.043)
  waiting for transfers between devices: 12.4 us -> 8.72 us
  starting transfers between devices: 49.3 us -> 51.9 us
  local copies, waits for them, and re-layouts: 4.53 us -> 6.78 us
  other arithmetic: 0.86 us -> 2.91 us
  between operations: 6.54 us -> 7.92 us
    ppermute x2 -> x3, waiting for transfers between devices: 3.58 us -> 0.01 us  [the longest x1 0.01 us: shards(): other_rows = lax.ppermute(own_rows, 'vec', swap)]
    ppermute x2 -> x3, starting transfers between devices: 6.04 us -> 7.74 us  [the longest x1 3.1 us: shards(): lax.ppermute(half, 'vec', swap)]
    unnamed x8 -> x12, local copies, waits for them, and re-layouts: 1.33 us -> 2.93 us
  transfers between devices with their start and end apart: 9 -> 10, of which waited for: 4 -> 3; matrix products, arithmetic and copies ran while one was open for 3% -> 4% of each run, Pallas kernels for 3% -> 4%
where the time goes in v11:
time: 120 us; the launch traced here: 119 us
  starting transfers between devices  51.9 us (43%)
  blocking collectives  32 us (27%)
  waiting for transfers between devices  8.72 us (7%)
  Pallas kernels  8.65 us (7%)
  between operations  7.92 us (7%)
  local copies, waits for them, and re-layouts  6.78 us (6%)
  other arithmetic  2.91 us (2%)
    all_gather x1, blocking collectives, shards(): gathered = lax.all_gather(picked, 'vec', axis=0, axis_index_groups=rings)  32 us
    ppermute x2, starting transfers between devices, halos(): far = lax.ppermute(to_far, 'lat', between)  19.1 us
    all_to_all x1, starting transfers between devices, shards(): lax.all_to_all(offered, 'vec', 0, 0, axis_index_groups=rings, tiled=True)  14.9 us
    pallas_call x3, Pallas kernels, on_band(): pl.pallas_call(kernel, out_shape=outs, in_specs=[vmem] * len(args), out_s...  7.75 us
    ppermute x2, starting transfers between devices, halos(): return (far, lax.ppermute(to_near, 'lat', on_chip))  5.66 us
    ppermute x1, waiting for transfers between devices, shards(): crossed = lax.ppermute(send, 'vec', swap)  5.4 us
    ppermute x1, starting transfers between devices, shards(): crossed = lax.ppermute(send, 'vec', swap)  3.12 us
    ppermute x1, starting transfers between devices, shards(): lax.ppermute(half, 'vec', swap)  3.1 us
  transfers between devices with their start and end apart: 10, of which 3 were waited for; matrix products, arithmetic and copies ran while one was open for 4% of the time, Pallas kernels for 4%

profile of v11, /device:TPU:25, one launch (start us, length us, event | category | flops | bytes accessed | tf_op | source)
XLA Modules:
  0.0 118.8 jit_solution(15335750331068248150)
XLA Ops:
  0.0 1.3 %copy-done.1 = bf16[1,3,8,24,720]{4,3,2,1,0:T(8,128)(2,1)S(1)} copy-done((bf16[1,3,8,24,720]{4,3,2,1,0:T(8,128)(2,1)S(1)}, bf16[1,3,8,24,720]{4,3,2,1,0:T(8,128)(2,1)}, u32[]{:S(2)}) %copy-start.1) | copy-done | bytes 829464
  1.5 3.1 %collective-permute-start.3 = (bf16[16,104,128]{2,1,0:T(8,128)(2,1)S(1)}, bf16[16,104,128]{2,1,0:T(8,128)(2,1)}, u32[]{:S(2)}, u32[]{:S(2)}) collective-permute-start(bf16[16,104,128]{2,1,0:T(8,128)(2,1)S(1)} %get-tuple-element.12), channel_id=1, source_target_pairs={{0,256},{16,272},{32,288},{48,304},{64,320},{80,336},{96,352},{112... | collective-permute-start | bytes 1277960 | tf_op jit(solution)/shard_map/ppermute | solution.py:301
  4.6 1.4 %collective-permute-start.2 = (bf16[16,104,128]{2,1,0:T(8,128)(2,1)S(1)}, bf16[16,104,128]{2,1,0:T(8,128)(2,1)}, u32[]{:S(2)}, u32[]{:S(2)}) collective-permute-start(bf16[16,104,128]{2,1,0:T(8,128)(2,1)S(1)} %get-tuple-element.11), channel_id=1, source_target_pairs={{240,224},{496,480},{241,225},{497,481},{242,226},{498,482},{243,2... | collective-permute-start | bytes 1277960 | tf_op jit(solution)/shard_map/ppermute | solution.py:302
  6.1 1.3 %fusion.3 = (s32[1]{0:T(128)}, s32[1]{0:T(128)}) fusion(s32[2]{0:T(128)} %param.6), kind=kLoop, calls=%fused_computation.18 | loop fusion | bytes 16 | tf_op jit(solution)/shard_map/slice | solution.py:303
  8.8 5.4 %collective-permute-done.3 = bf16[16,104,128]{2,1,0:T(8,128)(2,1)} collective-permute-done((bf16[16,104,128]{2,1,0:T(8,128)(2,1)S(1)}, bf16[16,104,128]{2,1,0:T(8,128)(2,1)}, u32[]{:S(2)}, u32[]{:S(2)}) %collective-permute-start.3) | collective-permute-done | bytes 426016 | tf_op jit(solution)/shard_map/ppermute | solution.py:301
  14.2 1.8 %select_select_fusion = bf16[16,104,128]{2,1,0:T(8,128)(2,1)} fusion(bf16[16,104,128]{2,1,0:T(8,128)(2,1)} %collective-permute-done.2, bf16[16,104,128]{2,1,0:T(8,128)(2,1)S(1)} %get-tuple-element.11, bf16[16,104,128]{2,1,0:T(8,128)(2,1)} %collective-permute-done.3, pred[]{:T(512)S(6)} %select_n.90, pred[]{:T(512)S(6)} %and.44), kind=kLoop, calls=%fused_computation.2 | loop fusion | flops 425984 | bytes 1703938 | tf_op jit(solution)/shard_map/jit(_where)/select_n | solution.py:307
  16.0 14.9 %all-to-all-start = ((bf16[16,104,128]{2,1,0:T(8,128)(2,1)}), bf16[16,104,128]{2,1,0:T(8,128)(2,1)S(1)}, u32[]{:S(2)}, u32[]{:S(2)}) async-start(bf16[16,104,128]{2,1,0:T(8,128)(2,1)} %select_select_fusion), calls=%async_computation | async-start | bytes 851968 | tf_op jit(solution)/shard_map/all_to_all | solution.py:310
  31.2 3.7 %collective-permute-start.1 = (f32[4,8,720]{2,1,0:T(8,128)S(1)}, f32[4,8,720]{2,1,0:T(8,128)S(1)}, u32[]{:S(2)}, u32[]{:S(2)}) collective-permute-start(f32[4,8,720]{2,1,0:T(8,128)S(1)} %get-tuple-element.23), channel_id=1, source_target_pairs={{0,1},{1,0},{2,3},{3,2},{4,5},{5,4},{6,7},{7,6},{8,9},{9,8},{10,11... | collective-permute-start | bytes 276488 | tf_op jit(solution)/shard_map/ppermute | solution.py:294
  34.9 4.2 %collective-permute-start = (f32[4,8,720]{2,1,0:T(8,128)S(1)}, f32[4,8,720]{2,1,0:T(8,128)S(1)}, u32[]{:S(2)}, u32[]{:S(2)}) collective-permute-start(f32[4,8,720]{2,1,0:T(8,128)S(1)} %get-tuple-element.24), channel_id=1, source_target_pairs={{1,2},{2,1},{3,4},{4,3},{5,6},{6,5},{7,8},{8,7},{9,10},{10,9},{11,... | collective-permute-start | bytes 276488 | tf_op jit(solution)/shard_map/ppermute | solution.py:293
  39.2 0.6 fusion.2
  46.5 2.7 %all-to-all-done = bf16[16,104,128]{2,1,0:T(8,128)(2,1)S(1)} async-done(((bf16[16,104,128]{2,1,0:T(8,128)(2,1)}), bf16[16,104,128]{2,1,0:T(8,128)(2,1)S(1)}, u32[]{:S(2)}, u32[]{:S(2)}) %all-to-all-start) | async-done | bytes 426016 | tf_op jit(solution)/shard_map/all_to_all | solution.py:310
  49.2 32.0 %all_gather.4 = bf16[16,2,104,128]{3,2,0,1:T(8,128)(2,1)S(1)} all-gather(bf16[1,2,104,128]{3,2,0,1:T(8,128)(2,1)S(1)} %maximum_add_fusion), channel_id=1, replica_groups={{0,16,32,48,64,80,96,112,128,144,160,176,192,208,224,240},{256,272,288,..., dimensions={0}, use_global_device_ids=true | all-gather | bytes 905216 | tf_op jit(solution)/shard_map/all_gather | solution.py:313
  81.2 0.8 copy-done.4
  82.1 0.7 pick.1
  82.8 0.8 copy-done.3
  83.5 2.2 %collective-permute-start.5 = (bf16[2,3,8,768]{3,2,1,0:T(8,128)(2,1)}, bf16[2,3,8,768]{3,2,1,0:T(8,128)(2,1)S(1)}, u32[]{:S(2)}, u32[]{:S(2)}) collective-permute-start(bf16[2,3,8,768]{3,2,1,0:T(8,128)(2,1)} %get-tuple-element.14.own_ref), channel_id=1, source_target_pairs={{0,256},{16,272},{32,288},{48,304},{64,320},{80,336},{96,352},{112... | collective-permute-start | bytes 221192 | tf_op jit(solution)/shard_map/ppermute | solution.py:316
  85.7 3.1 %collective-permute-start.4 = (bf16[16,104,128]{2,1,0:T(8,128)(2,1)}, bf16[16,104,128]{2,1,0:T(8,128)(2,1)}, u32[]{:S(2)}, u32[]{:S(2)}) collective-permute-start(bf16[16,104,128]{2,1,0:T(8,128)(2,1)} %copy-done.3), channel_id=1, source_target_pairs={{0,256},{16,272},{32,288},{48,304},{64,320},{80,336},{96,352},{112... | collective-permute-start | bytes 1277960 | tf_op jit(solution)/shard_map/ppermute | solution.py:318
  90.7 1.0 broadcast_add_fusion
  91.8 2.5 %collective-permute-start.8 = (bf16[16,104,128]{2,1,0:T(8,128)(2,1)S(1)}, bf16[16,104,128]{2,1,0:T(8,128)(2,1)S(1)}, u32[]{:S(2)}, u32[]{:S(2)}) collective-permute-start(bf16[16,104,128]{2,1,0:T(8,128)(2,1)S(1)} %broadcast_add_fusion), channel_id=1, source_target_pairs={{0,256},{16,272},{32,288},{48,304},{64,320},{80,336},{96,352},{112... | collective-permute-start | bytes 1277960 | tf_op jit(solution)/shard_map/ppermute | solution.py:318
  94.2 1.3 %edge_rows.1 = (f32[4,8,720]{2,1,0:T(8,128)S(1)}, f32[4,8,720]{2,1,0:T(8,128)S(1)}) custom-call(f32[4,8,24,720]{3,2,1,0:T(8,128)S(1)} %copy-done, f32[4,8,720]{2,1,0:T(8,128)S(1)} %collective-permute-done.far_ref, f32[4,8,720]{2,1,0:T(8,128)S(1)} %collective-permute-done.1.near_ref, s32[24,720]{1,0:T(8,128)S(1)} %copy-done.2, ...), custom_call_target="tpu_custom_call" | custom-call | flops 691200 | bytes 2797056 | tf_op jit(solution)/shard_map/edge_rows/pallas_call | solution.py:247
  95.6 14.9 %collective-permute-start.6 = (f32[4,8,720]{2,1,0:T(8,128)S(1)}, f32[4,8,720]{2,1,0:T(8,128)S(1)}, u32[]{:S(2)}, u32[]{:S(2)}) collective-permute-start(f32[4,8,720]{2,1,0:T(8,128)S(1)} %get-tuple-element.15), channel_id=1, source_target_pairs={{1,2},{2,1},{3,4},{4,3},{5,6},{6,5},{7,8},{8,7},{9,10},{10,9},{11,... | collective-permute-start | bytes 276488 | tf_op jit(solution)/shard_map/ppermute | solution.py:293
  110.5 1.9 %collective-permute-start.7 = (f32[4,8,720]{2,1,0:T(8,128)S(1)}, f32[4,8,720]{2,1,0:T(8,128)S(1)}, u32[]{:S(2)}, u32[]{:S(2)}) collective-permute-start(f32[4,8,720]{2,1,0:T(8,128)S(1)} %get-tuple-element.16), channel_id=1, source_target_pairs={{0,1},{1,0},{2,3},{3,2},{4,5},{5,4},{6,7},{7,6},{8,9},{9,8},{10,11... | collective-permute-start | bytes 276488 | tf_op jit(solution)/shard_map/ppermute | solution.py:294
  112.4 3.3 %one_hour.1.q_ref = f32[4,8,24,720]{3,2,1,0:T(8,128)S(1)} custom-call(f32[4,8,24,720]{3,2,1,0:T(8,128)S(1)} %copy-done, f32[4,8,720]{2,1,0:T(8,128)S(1)} %collective-permute-done.far_ref, f32[4,8,720]{2,1,0:T(8,128)S(1)} %collective-permute-done.1.near_ref, s32[24,720]{1,0:T(8,128)S(1)} %copy-done.2, bf16[16,104,128]{2,1,0:T(8,128)(2,1)S(1)} %get-tuple-element.20.own_ref, ...), custom_call_target="tpu_custom_call" | custom-call | flops 11059200 | bytes 5529088 | tf_op jit(solution)/shard_map/one_hour/pallas_call | solution.py:247
  115.7 3.1 %last_hour.1 = f32[4,8,24,720]{3,2,1,0:T(8,128)} custom-call(f32[4,8,24,720]{3,2,1,0:T(8,128)S(1)} %one_hour.1.q_ref, f32[4,8,720]{2,1,0:T(8,128)S(1)} %collective-permute-done.6.far_ref, f32[4,8,720]{2,1,0:T(8,128)S(1)} %collective-permute-done.7.near_ref, s32[24,720]{1,0:T(8,128)S(1)} %copy-done.2, bf16[16,104,128]{2,1,0:T(8,128)(2,1)S(1)} %get-tuple-element.19.own_ref, ...), custom_call_target="tpu_custom_call" | custom-call | flops 11059200 | bytes 5529088 | tf_op jit(solution)/shard_map/last_hour/pallas_call | solution.py:247
  (27 shorter events, 2.8 us)
Async XLA Ops:
  0.0 31.0 %copy-start = (f32[4,8,24,720]{3,2,1,0:T(8,128)S(1)}, f32[4,8,24,720]{3,2,1,0:T(8,128)}, u32[]{:S(2)}) copy-start(f32[4,8,24,720]{3,2,1,0:T(8,128)} %q_ref.3) | copy-start | bytes 6635524
  0.0 1.3 %copy-start.1 = (bf16[1,3,8,24,720]{4,3,2,1,0:T(8,128)(2,1)S(1)}, bf16[1,3,8,24,720]{4,3,2,1,0:T(8,128)(2,1)}, u32[]{:S(2)}) copy-start(bf16[1,3,8,24,720]{4,3,2,1,0:T(8,128)(2,1)} %field_ref.1) | copy-start | bytes 2488324
  1.3 37.8 %copy-start.5 = (s32[2]{0:T(128)S(1)}, s32[2]{0:T(128)}, u32[]{:S(2)}) copy-start(s32[2]{0:T(128)} %param.6) | copy-start | bytes 28
  1.5 12.7 %collective-permute-start.3 = (bf16[16,104,128]{2,1,0:T(8,128)(2,1)S(1)}, bf16[16,104,128]{2,1,0:T(8,128)(2,1)}, u32[]{:S(2)}, u32[]{:S(2)}) collective-permute-start(bf16[16,104,128]{2,1,0:T(8,128)(2,1)S(1)} %get-tuple-element.12), channel_id=1, source_target_pairs={{0,256},{16,272},{32,288},{48,304},{64,320},{80,336},{96,352},{112... | collective-permute-start | bytes 1277960 | tf_op jit(solution)/shard_map/ppermute | solution.py:301
  4.6 9.6 %collective-permute-start.2 = (bf16[16,104,128]{2,1,0:T(8,128)(2,1)S(1)}, bf16[16,104,128]{2,1,0:T(8,128)(2,1)}, u32[]{:S(2)}, u32[]{:S(2)}) collective-permute-start(bf16[16,104,128]{2,1,0:T(8,128)(2,1)S(1)} %get-tuple-element.11), channel_id=1, source_target_pairs={{240,224},{496,480},{241,225},{497,481},{242,226},{498,482},{243,2... | collective-permute-start | bytes 1277960 | tf_op jit(solution)/shard_map/ppermute | solution.py:302
  16.0 33.2 %all-to-all-start = ((bf16[16,104,128]{2,1,0:T(8,128)(2,1)}), bf16[16,104,128]{2,1,0:T(8,128)(2,1)S(1)}, u32[]{:S(2)}, u32[]{:S(2)}) async-start(bf16[16,104,128]{2,1,0:T(8,128)(2,1)} %select_select_fusion), calls=%async_computation | async-start | bytes 851968 | tf_op jit(solution)/shard_map/all_to_all | solution.py:310
  31.1 63.1 %copy-start.2 = (s32[24,720]{1,0:T(8,128)S(1)}, s32[24,720]{1,0:T(8,128)}, u32[]{:S(2)}) copy-start(s32[24,720]{1,0:T(8,128)} %mask_ref.5) | copy-start | bytes 207364
  31.2 12.4 %collective-permute-start.1 = (f32[4,8,720]{2,1,0:T(8,128)S(1)}, f32[4,8,720]{2,1,0:T(8,128)S(1)}, u32[]{:S(2)}, u32[]{:S(2)}) collective-permute-start(f32[4,8,720]{2,1,0:T(8,128)S(1)} %get-tuple-element.23), channel_id=1, source_target_pairs={{0,1},{1,0},{2,3},{3,2},{4,5},{5,4},{6,7},{7,6},{8,9},{9,8},{10,11... | collective-permute-start | bytes 276488 | tf_op jit(solution)/shard_map/ppermute | solution.py:294
  34.9 9.8 %collective-permute-start = (f32[4,8,720]{2,1,0:T(8,128)S(1)}, f32[4,8,720]{2,1,0:T(8,128)S(1)}, u32[]{:S(2)}, u32[]{:S(2)}) collective-permute-start(f32[4,8,720]{2,1,0:T(8,128)S(1)} %get-tuple-element.24), channel_id=1, source_target_pairs={{1,2},{2,1},{3,4},{4,3},{5,6},{6,5},{7,8},{8,7},{9,10},{10,9},{11,... | collective-permute-start | bytes 276488 | tf_op jit(solution)/shard_map/ppermute | solution.py:293
  81.2 0.9 copy-start.4
  82.8 0.8 copy-start.3
  83.5 5.3 %collective-permute-start.5 = (bf16[2,3,8,768]{3,2,1,0:T(8,128)(2,1)}, bf16[2,3,8,768]{3,2,1,0:T(8,128)(2,1)S(1)}, u32[]{:S(2)}, u32[]{:S(2)}) collective-permute-start(bf16[2,3,8,768]{3,2,1,0:T(8,128)(2,1)} %get-tuple-element.14.own_ref), channel_id=1, source_target_pairs={{0,256},{16,272},{32,288},{48,304},{64,320},{80,336},{96,352},{112... | collective-permute-start | bytes 221192 | tf_op jit(solution)/shard_map/ppermute | solution.py:316
  85.7 26.7 %collective-permute-start.4 = (bf16[16,104,128]{2,1,0:T(8,128)(2,1)}, bf16[16,104,128]{2,1,0:T(8,128)(2,1)}, u32[]{:S(2)}, u32[]{:S(2)}) collective-permute-start(bf16[16,104,128]{2,1,0:T(8,128)(2,1)} %copy-done.3), channel_id=1, source_target_pairs={{0,256},{16,272},{32,288},{48,304},{64,320},{80,336},{96,352},{112... | collective-permute-start | bytes 1277960 | tf_op jit(solution)/shard_map/ppermute | solution.py:318
  91.8 24.0 %collective-permute-start.8 = (bf16[16,104,128]{2,1,0:T(8,128)(2,1)S(1)}, bf16[16,104,128]{2,1,0:T(8,128)(2,1)S(1)}, u32[]{:S(2)}, u32[]{:S(2)}) collective-permute-start(bf16[16,104,128]{2,1,0:T(8,128)(2,1)S(1)} %broadcast_add_fusion), channel_id=1, source_target_pairs={{0,256},{16,272},{32,288},{48,304},{64,320},{80,336},{96,352},{112... | collective-permute-start | bytes 1277960 | tf_op jit(solution)/shard_map/ppermute | solution.py:318
  95.6 20.1 %collective-permute-start.6 = (f32[4,8,720]{2,1,0:T(8,128)S(1)}, f32[4,8,720]{2,1,0:T(8,128)S(1)}, u32[]{:S(2)}, u32[]{:S(2)}) collective-permute-start(f32[4,8,720]{2,1,0:T(8,128)S(1)} %get-tuple-element.15), channel_id=1, source_target_pairs={{1,2},{2,1},{3,4},{4,3},{5,6},{6,5},{7,8},{8,7},{9,10},{10,9},{11,... | collective-permute-start | bytes 276488 | tf_op jit(solution)/shard_map/ppermute | solution.py:293
  110.5 5.3 %collective-permute-start.7 = (f32[4,8,720]{2,1,0:T(8,128)S(1)}, f32[4,8,720]{2,1,0:T(8,128)S(1)}, u32[]{:S(2)}, u32[]{:S(2)}) collective-permute-start(f32[4,8,720]{2,1,0:T(8,128)S(1)} %get-tuple-element.16), channel_id=1, source_target_pairs={{0,1},{1,0},{2,3},{3,2},{4,5},{5,4},{6,7},{7,6},{8,9},{9,8},{10,11... | collective-permute-start | bytes 276488 | tf_op jit(solution)/shard_map/ppermute | solution.py:294

commit v12 on v10

--- a/solution.py
+++ b/solution.py
@@ -178,17 +178,7 @@
     def sending(level):
         return pltpu.make_async_copy(new_ref.at[:, level], out_ref.at[:, level], sent.at[level])
 
-    for level in range(levs):
-        for own in range(COLUMNS):
-
-            @pl.when(own_column == own)
-            def _():
-                for half in range(2):
-                    for k, lane, lanes, lo, hi, column, at, at_lane in field_parts(rows, half):
-                        piece_ref = own_ref if column == own else other_ref
-                        part = piece_ref[level * 2 + half, at : at + hi - lo].astype(jnp.float32)
-                        field_ref[k, lo:hi, lane : lane + lanes] = part[:, at_lane : at_lane + lanes]
-
+    def step(level):
         weight = weights(*(field_ref[k, :, :lon] for k in range(FIELDS)), mask)
         up, low = max(level - 1, 0), min(level + 1, levs - 1)
         for v in range(vecs):
@@ -198,6 +188,18 @@
             to_ref[v, level] = advance(c, n, s, q_ref[v, up], q_ref[v, low], weight)
         if new_ref is not None:
             sending(level).start()
+
+    for own in range(COLUMNS):
+
+        @pl.when(own_column == own)
+        def _():
+            for level in range(levs):
+                for half in range(2):
+                    for k, lane, lanes, lo, hi, column, at, at_lane in field_parts(rows, half):
+                        piece_ref = own_ref if column == own else other_ref
+                        part = piece_ref[level * 2 + half, at : at + hi - lo].astype(jnp.float32)
+                        field_ref[k, lo:hi, lane : lane + lanes] = part[:, at_lane : at_lane + lanes]
+                step(level)
 
     if new_ref is not None:
         for level in range(levs):

time: 115 us -> 114 us (level)
  Pallas kernels: 7.83 us -> 6.58 us
    pallas_call x3, Pallas kernels: 7.63 us -> 6.39 us  [on_band(): pl.pallas_call(kernel, out_shape=outs, in_specs=[vmem] * len(args), out_s...]
where the time goes in v12:
time: 114 us; the launch traced here: 113 us
  starting transfers between devices  49.1 us (43%)
  blocking collectives  32 us (28%)
  waiting for transfers between devices  12.4 us (11%)
  Pallas kernels  6.58 us (6%)
  between operations  6.54 us (6%)
  local copies, waits for them, and re-layouts  4.53 us (4%)
  other arithmetic  1.87 us (2%)
    all_gather x1, blocking collectives, shards(): gathered = lax.all_gather(picked, 'vec', axis=0, axis_index_groups=rings)  32 us
    ppermute x2, starting transfers between devices, halos(): far = lax.ppermute(to_far, 'lat', between)  18.6 us
    all_to_all x1, starting transfers between devices, shards(): lax.all_to_all(offered, 'vec', 0, 0, axis_index_groups=rings, tiled=True)  15 us
    pallas_call x3, Pallas kernels, on_band(): pl.pallas_call(kernel, out_shape=outs, in_specs=[vmem] * len(args), out_s...  6.39 us
    ppermute x2, starting transfers between devices, halos(): return (far, lax.ppermute(to_near, 'lat', on_chip))  5.66 us
    ppermute x1, waiting for transfers between devices, shards(): crossed = lax.ppermute(send, 'vec', swap)  5.5 us
    ppermute x2, starting transfers between devices, shards(): other = [lax.ppermute(half, 'vec', swap) for half in own]  5.28 us
    ppermute x2, waiting for transfers between devices, shards(): other = [lax.ppermute(half, 'vec', swap) for half in own]  3.58 us
  transfers between devices with their start and end apart: 9, of which 4 were waited for; matrix products, arithmetic and copies ran while one was open for 3% of the time, Pallas kernels for 3%

profile of v12, /device:TPU:25, one launch (start us, length us, event | category | flops | bytes accessed | tf_op | source)
XLA Modules:
  0.0 113.0 jit_solution(9503512033799433542)
XLA Ops:
  0.0 1.3 %copy-done.1 = bf16[1,3,8,24,720]{4,3,2,1,0:T(8,128)(2,1)S(1)} copy-done((bf16[1,3,8,24,720]{4,3,2,1,0:T(8,128)(2,1)S(1)}, bf16[1,3,8,24,720]{4,3,2,1,0:T(8,128)(2,1)}, u32[]{:S(2)}) %copy-start.1) | copy-done | bytes 829464
  1.3 0.2 pack.1
  1.5 3.1 %collective-permute-start.3 = (bf16[16,104,128]{2,1,0:T(8,128)(2,1)S(1)}, bf16[16,104,128]{2,1,0:T(8,128)(2,1)}, u32[]{:S(2)}, u32[]{:S(2)}) collective-permute-start(bf16[16,104,128]{2,1,0:T(8,128)(2,1)S(1)} %get-tuple-element.10), channel_id=1, source_target_pairs={{0,256},{16,272},{32,288},{48,304},{64,320},{80,336},{96,352},{112... | collective-permute-start | bytes 1277960 | tf_op jit(solution)/shard_map/ppermute | solution.py:267
  4.6 1.4 %collective-permute-start.2 = (bf16[16,104,128]{2,1,0:T(8,128)(2,1)S(1)}, bf16[16,104,128]{2,1,0:T(8,128)(2,1)}, u32[]{:S(2)}, u32[]{:S(2)}) collective-permute-start(bf16[16,104,128]{2,1,0:T(8,128)(2,1)S(1)} %get-tuple-element.9), channel_id=1, source_target_pairs={{240,224},{496,480},{241,225},{497,481},{242,226},{498,482},{243,2... | collective-permute-start | bytes 1277960 | tf_op jit(solution)/shard_map/ppermute | solution.py:268
  6.1 1.3 %fusion.2 = (s32[1]{0:T(128)}, s32[1]{0:T(128)}) fusion(s32[2]{0:T(128)} %param.6), kind=kLoop, calls=%fused_computation.16 | loop fusion | bytes 16 | tf_op jit(solution)/shard_map/slice | solution.py:269
  8.7 5.5 %collective-permute-done.3 = bf16[16,104,128]{2,1,0:T(8,128)(2,1)} collective-permute-done((bf16[16,104,128]{2,1,0:T(8,128)(2,1)S(1)}, bf16[16,104,128]{2,1,0:T(8,128)(2,1)}, u32[]{:S(2)}, u32[]{:S(2)}) %collective-permute-start.3) | collective-permute-done | bytes 426016 | tf_op jit(solution)/shard_map/ppermute | solution.py:267
  14.2 1.8 %select_select_fusion = bf16[16,104,128]{2,1,0:T(8,128)(2,1)} fusion(bf16[16,104,128]{2,1,0:T(8,128)(2,1)} %collective-permute-done.2, bf16[16,104,128]{2,1,0:T(8,128)(2,1)S(1)} %get-tuple-element.9, bf16[16,104,128]{2,1,0:T(8,128)(2,1)} %collective-permute-done.3, pred[]{:T(512)S(6)} %select_n.86, pred[]{:T(512)S(6)} %and.44), kind=kLoop, calls=%fused_computation.2 | loop fusion | flops 425984 | bytes 1703938 | tf_op jit(solution)/shard_map/jit(_where)/select_n | solution.py:273
  16.0 15.0 %all-to-all-start = ((bf16[16,104,128]{2,1,0:T(8,128)(2,1)}), bf16[16,104,128]{2,1,0:T(8,128)(2,1)S(1)}, u32[]{:S(2)}, u32[]{:S(2)}) async-start(bf16[16,104,128]{2,1,0:T(8,128)(2,1)} %select_select_fusion), calls=%async_computation | async-start | bytes 851968 | tf_op jit(solution)/shard_map/all_to_all | solution.py:276
  31.3 3.7 %collective-permute-start.1 = (f32[4,8,720]{2,1,0:T(8,128)S(1)}, f32[4,8,720]{2,1,0:T(8,128)S(1)}, u32[]{:S(2)}, u32[]{:S(2)}) collective-permute-start(f32[4,8,720]{2,1,0:T(8,128)S(1)} %get-tuple-element.19), channel_id=1, source_target_pairs={{0,1},{1,0},{2,3},{3,2},{4,5},{5,4},{6,7},{7,6},{8,9},{9,8},{10,11... | collective-permute-start | bytes 276488 | tf_op jit(solution)/shard_map/ppermute | solution.py:260
  35.0 4.2 %collective-permute-start = (f32[4,8,720]{2,1,0:T(8,128)S(1)}, f32[4,8,720]{2,1,0:T(8,128)S(1)}, u32[]{:S(2)}, u32[]{:S(2)}) collective-permute-start(f32[4,8,720]{2,1,0:T(8,128)S(1)} %get-tuple-element.20), channel_id=1, source_target_pairs={{1,2},{2,1},{3,4},{4,3},{5,6},{6,5},{7,8},{8,7},{9,10},{10,9},{11,... | collective-permute-start | bytes 276488 | tf_op jit(solution)/shard_map/ppermute | solution.py:259
  39.3 0.6 fusion.1
  43.7 0.5 slice.41
  44.2 0.7 collective-permute-done.far_ref
  44.9 0.5 slice.40
  46.7 2.7 %all-to-all-done = bf16[16,104,128]{2,1,0:T(8,128)(2,1)S(1)} async-done(((bf16[16,104,128]{2,1,0:T(8,128)(2,1)}), bf16[16,104,128]{2,1,0:T(8,128)(2,1)S(1)}, u32[]{:S(2)}, u32[]{:S(2)}) %all-to-all-start) | async-done | bytes 426016 | tf_op jit(solution)/shard_map/all_to_all | solution.py:276
  49.4 32.0 %all_gather.4 = bf16[16,2,104,128]{3,2,0,1:T(8,128)(2,1)S(1)} all-gather(bf16[1,2,104,128]{3,2,0,1:T(8,128)(2,1)S(1)} %maximum_add_fusion), channel_id=1, replica_groups={{0,16,32,48,64,80,96,112,128,144,160,176,192,208,224,240},{256,272,288,..., dimensions={0}, use_global_device_ids=true | all-gather | bytes 905216 | tf_op jit(solution)/shard_map/all_gather | solution.py:279
  81.4 2.1 %collective-permute-start.4 = (bf16[16,104,128]{2,1,0:T(8,128)(2,1)S(1)}, bf16[16,104,128]{2,1,0:T(8,128)(2,1)S(1)}, u32[]{:S(2)}, u32[]{:S(2)}) collective-permute-start(bf16[16,104,128]{2,1,0:T(8,128)(2,1)S(1)} %get-tuple-element.16.own_ref), channel_id=1, source_target_pairs={{0,256},{16,272},{32,288},{48,304},{64,320},{80,336},{96,352},{112... | collective-permute-start | bytes 1277960 | tf_op jit(solution)/shard_map/ppermute | solution.py:281
  83.5 3.2 %collective-permute-start.7 = (bf16[16,104,128]{2,1,0:T(8,128)(2,1)S(1)}, bf16[16,104,128]{2,1,0:T(8,128)(2,1)S(1)}, u32[]{:S(2)}, u32[]{:S(2)}) collective-permute-start(bf16[16,104,128]{2,1,0:T(8,128)(2,1)S(1)} %get-tuple-element.15.own_ref), channel_id=1, source_target_pairs={{0,256},{16,272},{32,288},{48,304},{64,320},{80,336},{96,352},{112... | collective-permute-start | bytes 1277960 | tf_op jit(solution)/shard_map/ppermute | solution.py:281
  86.7 3.6 %collective-permute-done.4.other_ref = bf16[16,104,128]{2,1,0:T(8,128)(2,1)S(1)} collective-permute-done((bf16[16,104,128]{2,1,0:T(8,128)(2,1)S(1)}, bf16[16,104,128]{2,1,0:T(8,128)(2,1)S(1)}, u32[]{:S(2)}, u32[]{:S(2)}) %collective-permute-start.4) | collective-permute-done | bytes 426016 | tf_op jit(solution)/shard_map/ppermute | solution.py:281
  90.2 0.6 edge_rows.1
  90.9 14.4 %collective-permute-start.5 = (f32[4,8,720]{2,1,0:T(8,128)S(1)}, f32[4,8,720]{2,1,0:T(8,128)S(1)}, u32[]{:S(2)}, u32[]{:S(2)}) collective-permute-start(f32[4,8,720]{2,1,0:T(8,128)S(1)} %get-tuple-element.11), channel_id=1, source_target_pairs={{1,2},{2,1},{3,4},{4,3},{5,6},{6,5},{7,8},{8,7},{9,10},{10,9},{11,... | collective-permute-start | bytes 276488 | tf_op jit(solution)/shard_map/ppermute | solution.py:259
  105.2 1.9 %collective-permute-start.6 = (f32[4,8,720]{2,1,0:T(8,128)S(1)}, f32[4,8,720]{2,1,0:T(8,128)S(1)}, u32[]{:S(2)}, u32[]{:S(2)}) collective-permute-start(f32[4,8,720]{2,1,0:T(8,128)S(1)} %get-tuple-element.12), channel_id=1, source_target_pairs={{0,1},{1,0},{2,3},{3,2},{4,5},{5,4},{6,7},{7,6},{8,9},{9,8},{10,11... | collective-permute-start | bytes 276488 | tf_op jit(solution)/shard_map/ppermute | solution.py:260
  107.2 2.3 %one_hour.1.q_ref = f32[4,8,24,720]{3,2,1,0:T(8,128)S(1)} custom-call(f32[4,8,24,720]{3,2,1,0:T(8,128)S(1)} %copy-done, f32[4,8,720]{2,1,0:T(8,128)S(1)} %collective-permute-done.far_ref, f32[4,8,720]{2,1,0:T(8,128)S(1)} %collective-permute-done.1.near_ref, s32[24,720]{1,0:T(8,128)S(1)} %copy-done.2, bf16[16,104,128]{2,1,0:T(8,128)(2,1)S(1)} %get-tuple-element.16.own_ref, ...), custom_call_target="tpu_custom_call" | custom-call | flops 11059200 | bytes 5529088 | tf_op jit(solution)/shard_map/one_hour/pallas_call | solution.py:213
  109.5 3.5 %last_hour.1 = f32[4,8,24,720]{3,2,1,0:T(8,128)} custom-call(f32[4,8,24,720]{3,2,1,0:T(8,128)S(1)} %one_hour.1.q_ref, f32[4,8,720]{2,1,0:T(8,128)S(1)} %collective-permute-done.5.far_ref, f32[4,8,720]{2,1,0:T(8,128)S(1)} %collective-permute-done.6.near_ref, s32[24,720]{1,0:T(8,128)S(1)} %copy-done.2, bf16[16,104,128]{2,1,0:T(8,128)(2,1)S(1)} %get-tuple-element.15.own_ref, ...), custom_call_target="tpu_custom_call" | custom-call | flops 11059200 | bytes 5529088 | tf_op jit(solution)/shard_map/last_hour/pallas_call | solution.py:213
  (18 shorter events, 0.3 us)
Async XLA Ops:
  0.0 31.1 %copy-start = (f32[4,8,24,720]{3,2,1,0:T(8,128)S(1)}, f32[4,8,24,720]{3,2,1,0:T(8,128)}, u32[]{:S(2)}) copy-start(f32[4,8,24,720]{3,2,1,0:T(8,128)} %q_ref.3) | copy-start | bytes 6635524
  0.0 1.3 %copy-start.1 = (bf16[1,3,8,24,720]{4,3,2,1,0:T(8,128)(2,1)S(1)}, bf16[1,3,8,24,720]{4,3,2,1,0:T(8,128)(2,1)}, u32[]{:S(2)}) copy-start(bf16[1,3,8,24,720]{4,3,2,1,0:T(8,128)(2,1)} %field_ref.1) | copy-start | bytes 2488324
  1.3 37.9 %copy-start.3 = (s32[2]{0:T(128)S(1)}, s32[2]{0:T(128)}, u32[]{:S(2)}) copy-start(s32[2]{0:T(128)} %param.6) | copy-start | bytes 28
  1.5 12.7 %collective-permute-start.3 = (bf16[16,104,128]{2,1,0:T(8,128)(2,1)S(1)}, bf16[16,104,128]{2,1,0:T(8,128)(2,1)}, u32[]{:S(2)}, u32[]{:S(2)}) collective-permute-start(bf16[16,104,128]{2,1,0:T(8,128)(2,1)S(1)} %get-tuple-element.10), channel_id=1, source_target_pairs={{0,256},{16,272},{32,288},{48,304},{64,320},{80,336},{96,352},{112... | collective-permute-start | bytes 1277960 | tf_op jit(solution)/shard_map/ppermute | solution.py:267
  4.6 9.6 %collective-permute-start.2 = (bf16[16,104,128]{2,1,0:T(8,128)(2,1)S(1)}, bf16[16,104,128]{2,1,0:T(8,128)(2,1)}, u32[]{:S(2)}, u32[]{:S(2)}) collective-permute-start(bf16[16,104,128]{2,1,0:T(8,128)(2,1)S(1)} %get-tuple-element.9), channel_id=1, source_target_pairs={{240,224},{496,480},{241,225},{497,481},{242,226},{498,482},{243,2... | collective-permute-start | bytes 1277960 | tf_op jit(solution)/shard_map/ppermute | solution.py:268
  16.0 74.2 %copy-start.2 = (s32[24,720]{1,0:T(8,128)S(1)}, s32[24,720]{1,0:T(8,128)}, u32[]{:S(2)}) copy-start(s32[24,720]{1,0:T(8,128)} %mask_ref.5) | copy-start | bytes 207364
  16.0 33.3 %all-to-all-start = ((bf16[16,104,128]{2,1,0:T(8,128)(2,1)}), bf16[16,104,128]{2,1,0:T(8,128)(2,1)S(1)}, u32[]{:S(2)}, u32[]{:S(2)}) async-start(bf16[16,104,128]{2,1,0:T(8,128)(2,1)} %select_select_fusion), calls=%async_computation | async-start | bytes 851968 | tf_op jit(solution)/shard_map/all_to_all | solution.py:276
  31.3 12.4 %collective-permute-start.1 = (f32[4,8,720]{2,1,0:T(8,128)S(1)}, f32[4,8,720]{2,1,0:T(8,128)S(1)}, u32[]{:S(2)}, u32[]{:S(2)}) collective-permute-start(f32[4,8,720]{2,1,0:T(8,128)S(1)} %get-tuple-element.19), channel_id=1, source_target_pairs={{0,1},{1,0},{2,3},{3,2},{4,5},{5,4},{6,7},{7,6},{8,9},{9,8},{10,11... | collective-permute-start | bytes 276488 | tf_op jit(solution)/shard_map/ppermute | solution.py:260
  35.0 9.8 %collective-permute-start = (f32[4,8,720]{2,1,0:T(8,128)S(1)}, f32[4,8,720]{2,1,0:T(8,128)S(1)}, u32[]{:S(2)}, u32[]{:S(2)}) collective-permute-start(f32[4,8,720]{2,1,0:T(8,128)S(1)} %get-tuple-element.20), channel_id=1, source_target_pairs={{1,2},{2,1},{3,4},{4,3},{5,6},{6,5},{7,8},{8,7},{9,10},{10,9},{11,... | collective-permute-start | bytes 276488 | tf_op jit(solution)/shard_map/ppermute | solution.py:259
  81.4 8.9 %collective-permute-start.4 = (bf16[16,104,128]{2,1,0:T(8,128)(2,1)S(1)}, bf16[16,104,128]{2,1,0:T(8,128)(2,1)S(1)}, u32[]{:S(2)}, u32[]{:S(2)}) collective-permute-start(bf16[16,104,128]{2,1,0:T(8,128)(2,1)S(1)} %get-tuple-element.16.own_ref), channel_id=1, source_target_pairs={{0,256},{16,272},{32,288},{48,304},{64,320},{80,336},{96,352},{112... | collective-permute-start | bytes 1277960 | tf_op jit(solution)/shard_map/ppermute | solution.py:281
  83.5 26.0 %collective-permute-start.7 = (bf16[16,104,128]{2,1,0:T(8,128)(2,1)S(1)}, bf16[16,104,128]{2,1,0:T(8,128)(2,1)S(1)}, u32[]{:S(2)}, u32[]{:S(2)}) collective-permute-start(bf16[16,104,128]{2,1,0:T(8,128)(2,1)S(1)} %get-tuple-element.15.own_ref), channel_id=1, source_target_pairs={{0,256},{16,272},{32,288},{48,304},{64,320},{80,336},{96,352},{112... | collective-permute-start | bytes 1277960 | tf_op jit(solution)/shard_map/ppermute | solution.py:281
  90.9 18.6 %collective-permute-start.5 = (f32[4,8,720]{2,1,0:T(8,128)S(1)}, f32[4,8,720]{2,1,0:T(8,128)S(1)}, u32[]{:S(2)}, u32[]{:S(2)}) collective-permute-start(f32[4,8,720]{2,1,0:T(8,128)S(1)} %get-tuple-element.11), channel_id=1, source_target_pairs={{1,2},{2,1},{3,4},{4,3},{5,6},{6,5},{7,8},{8,7},{9,10},{10,9},{11,... | collective-permute-start | bytes 276488 | tf_op jit(solution)/shard_map/ppermute | solution.py:259
  105.2 4.3 %collective-permute-start.6 = (f32[4,8,720]{2,1,0:T(8,128)S(1)}, f32[4,8,720]{2,1,0:T(8,128)S(1)}, u32[]{:S(2)}, u32[]{:S(2)}) collective-permute-start(f32[4,8,720]{2,1,0:T(8,128)S(1)} %get-tuple-element.12), channel_id=1, source_target_pairs={{0,1},{1,0},{2,3},{3,2},{4,5},{5,4},{6,7},{7,6},{8,9},{9,8},{10,11... | collective-permute-start | bytes 276488 | tf_op jit(solution)/shard_map/ppermute | solution.py:260

commit v13 on v12

--- a/solution.py
+++ b/solution.py
@@ -75,6 +75,29 @@
         compiler_params=pltpu.CompilerParams(vmem_limit_bytes=VMEM_LIMIT),
         name="pack",
     )(trajectory)
+
+
+def offer_kernel(choice_ref, keep_ref, crossed_ref, moved_ref, offered_ref, done):
+    for i, ref in enumerate((keep_ref, crossed_ref, moved_ref)):
+
+        @pl.when(choice_ref[0] == i)
+        def _():
+            copy = pltpu.make_async_copy(ref, offered_ref, done)
+            copy.start()
+            copy.wait()
+
+
+def offer(choice, *halves):
+    anywhere = pl.BlockSpec(memory_space=pl.ANY)
+    return pl.pallas_call(
+        offer_kernel,
+        out_shape=jax.ShapeDtypeStruct(halves[0].shape, halves[0].dtype),
+        in_specs=[pl.BlockSpec(memory_space=pltpu.SMEM)] + [anywhere] * len(halves),
+        out_specs=anywhere,
+        scratch_shapes=[pltpu.SemaphoreType.DMA],
+        compiler_params=pltpu.CompilerParams(vmem_limit_bytes=VMEM_LIMIT),
+        name="offer",
+    )(choice, *halves)
 
 
 def lanes_next(x):
@@ -270,7 +293,8 @@
     both = asked == end
     z = lax.axis_index("vec") % RING
     own_there = jnp.where(z == end, (column == 1) & ~both, asked // RING == column)
-    offered = jnp.where((z == end - 1) & both, moved, jnp.where(own_there, keep, crossed))
+    choice = jnp.where((z == end - 1) & both, 2, jnp.where(own_there, 0, 1)).astype(jnp.int32)
+    offered = offer(choice[None], keep, crossed, moved)
     place = jnp.where(both & (hour_slot // RING == column), end - 1, hour_slot % RING)
 
     pieces = lax.all_to_all(offered, "vec", 0, 0, axis_index_groups=rings, tiled=True)

time: 114 us -> 114 us (level)
  other arithmetic: 1.87 us -> 0.04 us
  Pallas kernels: 6.58 us -> 8.11 us
    select_n x1 -> x0, other arithmetic: 1.82 us -> none  [shards(): jnp.where((z == end - 1) & both, moved, jnp.where(own_there, keep, crossed))]
where the time goes in v13:
time: 114 us; the launch traced here: 113 us
  starting transfers between devices  49.1 us (43%)
  blocking collectives  32 us (28%)
  waiting for transfers between devices  12.5 us (11%)
  Pallas kernels  8.11 us (7%)
  between operations  6.48 us (6%)
  local copies, waits for them, and re-layouts  4.6 us (4%)
    all_gather x1, blocking collectives, shards(): gathered = lax.all_gather(picked, 'vec', axis=0, axis_index_groups=rings)  32 us
    ppermute x2, starting transfers between devices, halos(): far = lax.ppermute(to_far, 'lat', between)  18.6 us
    all_to_all x1, starting transfers between devices, shards(): lax.all_to_all(offered, 'vec', 0, 0, axis_index_groups=rings, tiled=True)  15.1 us
    pallas_call x3, Pallas kernels, on_band(): pl.pallas_call(kernel, out_shape=outs, in_specs=[vmem] * len(args), out_s...  6.39 us
    ppermute x2, starting transfers between devices, halos(): return (far, lax.ppermute(to_near, 'lat', on_chip))  5.66 us
    ppermute x1, waiting for transfers between devices, shards(): crossed = lax.ppermute(send, 'vec', swap)  5.6 us
    ppermute x2, starting transfers between devices, shards(): other = [lax.ppermute(half, 'vec', swap) for half in own]  5.28 us
    ppermute x2, waiting for transfers between devices, shards(): other = [lax.ppermute(half, 'vec', swap) for half in own]  3.58 us
  transfers between devices with their start and end apart: 9, of which 4 were waited for; matrix products, arithmetic and copies ran while one was open for 3% of the time, Pallas kernels for 3%

profile of v13, /device:TPU:25, one launch (start us, length us, event | category | flops | bytes accessed | tf_op | source)
XLA Modules:
  0.0 112.8 jit_solution(9370940088364423187)
XLA Ops:
  0.0 1.3 %copy-done.1 = bf16[1,3,8,24,720]{4,3,2,1,0:T(8,128)(2,1)S(1)} copy-done((bf16[1,3,8,24,720]{4,3,2,1,0:T(8,128)(2,1)S(1)}, bf16[1,3,8,24,720]{4,3,2,1,0:T(8,128)(2,1)}, u32[]{:S(2)}) %copy-start.1) | copy-done | bytes 829464
  1.3 0.9 pack.1
  2.3 3.1 %collective-permute-start.2 = (bf16[16,104,128]{2,1,0:T(8,128)(2,1)}, bf16[16,104,128]{2,1,0:T(8,128)(2,1)S(1)}, u32[]{:S(2)}, u32[]{:S(2)}) collective-permute-start(bf16[16,104,128]{2,1,0:T(8,128)(2,1)} %get-tuple-element.10), channel_id=1, source_target_pairs={{0,256},{16,272},{32,288},{48,304},{64,320},{80,336},{96,352},{112... | collective-permute-start | bytes 1277960 | tf_op jit(solution)/shard_map/ppermute | solution.py:290
  5.4 1.4 %collective-permute-start.3 = (bf16[16,104,128]{2,1,0:T(8,128)(2,1)S(1)}, bf16[16,104,128]{2,1,0:T(8,128)(2,1)}, u32[]{:S(2)}, u32[]{:S(2)}) collective-permute-start(bf16[16,104,128]{2,1,0:T(8,128)(2,1)S(1)} %get-tuple-element.9.keep_ref), channel_id=1, source_target_pairs={{240,224},{496,480},{241,225},{497,481},{242,226},{498,482},{243,2... | collective-permute-start | bytes 1277960 | tf_op jit(solution)/shard_map/ppermute | solution.py:291
  6.8 1.4 %fusion.2 = (s32[1]{0:T(128)}, s32[1]{0:T(128)}) fusion(s32[2]{0:T(128)} %param.6), kind=kLoop, calls=%fused_computation.15 | loop fusion | bytes 16 | tf_op jit(solution)/shard_map/slice | solution.py:292
  9.4 5.6 %collective-permute-done.2.crossed_ref = bf16[16,104,128]{2,1,0:T(8,128)(2,1)S(1)} collective-permute-done((bf16[16,104,128]{2,1,0:T(8,128)(2,1)}, bf16[16,104,128]{2,1,0:T(8,128)(2,1)S(1)}, u32[]{:S(2)}, u32[]{:S(2)}) %collective-permute-start.2) | collective-permute-done | bytes 426016 | tf_op jit(solution)/shard_map/ppermute | solution.py:290
  15.1 0.8 offer.1
  15.8 15.1 %all-to-all-start = ((bf16[16,104,128]{2,1,0:T(8,128)(2,1)}), bf16[16,104,128]{2,1,0:T(8,128)(2,1)S(1)}, u32[]{:S(2)}, u32[]{:S(2)}) async-start(bf16[16,104,128]{2,1,0:T(8,128)(2,1)} %offer.1), calls=%async_computation | async-start | bytes 851968 | tf_op jit(solution)/shard_map/all_to_all | solution.py:300
  31.1 3.7 %collective-permute-start.1 = (f32[4,8,720]{2,1,0:T(8,128)S(1)}, f32[4,8,720]{2,1,0:T(8,128)S(1)}, u32[]{:S(2)}, u32[]{:S(2)}) collective-permute-start(f32[4,8,720]{2,1,0:T(8,128)S(1)} %get-tuple-element.19), channel_id=1, source_target_pairs={{0,1},{1,0},{2,3},{3,2},{4,5},{5,4},{6,7},{7,6},{8,9},{9,8},{10,11... | collective-permute-start | bytes 276488 | tf_op jit(solution)/shard_map/ppermute | solution.py:283
  34.8 4.2 %collective-permute-start = (f32[4,8,720]{2,1,0:T(8,128)S(1)}, f32[4,8,720]{2,1,0:T(8,128)S(1)}, u32[]{:S(2)}, u32[]{:S(2)}) collective-permute-start(f32[4,8,720]{2,1,0:T(8,128)S(1)} %get-tuple-element.20), channel_id=1, source_target_pairs={{1,2},{2,1},{3,4},{4,3},{5,6},{6,5},{7,8},{8,7},{9,10},{10,9},{11,... | collective-permute-start | bytes 276488 | tf_op jit(solution)/shard_map/ppermute | solution.py:282
  39.1 0.6 fusion.1
  43.5 0.5 slice.41
  44.0 0.7 collective-permute-done.far_ref
  44.7 0.5 slice.40
  46.5 2.7 %all-to-all-done = bf16[16,104,128]{2,1,0:T(8,128)(2,1)S(1)} async-done(((bf16[16,104,128]{2,1,0:T(8,128)(2,1)}), bf16[16,104,128]{2,1,0:T(8,128)(2,1)S(1)}, u32[]{:S(2)}, u32[]{:S(2)}) %all-to-all-start) | async-done | bytes 426016 | tf_op jit(solution)/shard_map/all_to_all | solution.py:300
  49.2 32.0 %all_gather.4 = bf16[16,2,104,128]{3,2,0,1:T(8,128)(2,1)S(1)} all-gather(bf16[1,2,104,128]{3,2,0,1:T(8,128)(2,1)S(1)} %maximum_add_fusion), channel_id=1, replica_groups={{0,16,32,48,64,80,96,112,128,144,160,176,192,208,224,240},{256,272,288,..., dimensions={0}, use_global_device_ids=true | all-gather | bytes 905216 | tf_op jit(solution)/shard_map/all_gather | solution.py:303
  81.2 3.1 %collective-permute-start.4 = (bf16[16,104,128]{2,1,0:T(8,128)(2,1)S(1)}, bf16[16,104,128]{2,1,0:T(8,128)(2,1)S(1)}, u32[]{:S(2)}, u32[]{:S(2)}) collective-permute-start(bf16[16,104,128]{2,1,0:T(8,128)(2,1)S(1)} %get-tuple-element.16.own_ref), channel_id=1, source_target_pairs={{0,256},{16,272},{32,288},{48,304},{64,320},{80,336},{96,352},{112... | collective-permute-start | bytes 1277960 | tf_op jit(solution)/shard_map/ppermute | solution.py:305
  84.3 2.2 %collective-permute-start.7 = (bf16[16,104,128]{2,1,0:T(8,128)(2,1)S(1)}, bf16[16,104,128]{2,1,0:T(8,128)(2,1)S(1)}, u32[]{:S(2)}, u32[]{:S(2)}) collective-permute-start(bf16[16,104,128]{2,1,0:T(8,128)(2,1)S(1)} %get-tuple-element.15.own_ref), channel_id=1, source_target_pairs={{0,256},{16,272},{32,288},{48,304},{64,320},{80,336},{96,352},{112... | collective-permute-start | bytes 1277960 | tf_op jit(solution)/shard_map/ppermute | solution.py:305
  86.5 3.6 %collective-permute-done.4.other_ref = bf16[16,104,128]{2,1,0:T(8,128)(2,1)S(1)} collective-permute-done((bf16[16,104,128]{2,1,0:T(8,128)(2,1)S(1)}, bf16[16,104,128]{2,1,0:T(8,128)(2,1)S(1)}, u32[]{:S(2)}, u32[]{:S(2)}) %collective-permute-start.4) | collective-permute-done | bytes 426016 | tf_op jit(solution)/shard_map/ppermute | solution.py:305
  90.1 0.6 edge_rows.1
  90.7 14.4 %collective-permute-start.5 = (f32[4,8,720]{2,1,0:T(8,128)S(1)}, f32[4,8,720]{2,1,0:T(8,128)S(1)}, u32[]{:S(2)}, u32[]{:S(2)}) collective-permute-start(f32[4,8,720]{2,1,0:T(8,128)S(1)} %get-tuple-element.11), channel_id=1, source_target_pairs={{1,2},{2,1},{3,4},{4,3},{5,6},{6,5},{7,8},{8,7},{9,10},{10,9},{11,... | collective-permute-start | bytes 276488 | tf_op jit(solution)/shard_map/ppermute | solution.py:282
  105.0 1.9 %collective-permute-start.6 = (f32[4,8,720]{2,1,0:T(8,128)S(1)}, f32[4,8,720]{2,1,0:T(8,128)S(1)}, u32[]{:S(2)}, u32[]{:S(2)}) collective-permute-start(f32[4,8,720]{2,1,0:T(8,128)S(1)} %get-tuple-element.12), channel_id=1, source_target_pairs={{0,1},{1,0},{2,3},{3,2},{4,5},{5,4},{6,7},{7,6},{8,9},{9,8},{10,11... | collective-permute-start | bytes 276488 | tf_op jit(solution)/shard_map/ppermute | solution.py:283
  107.0 2.3 %one_hour.1.q_ref = f32[4,8,24,720]{3,2,1,0:T(8,128)S(1)} custom-call(f32[4,8,24,720]{3,2,1,0:T(8,128)S(1)} %copy-done, f32[4,8,720]{2,1,0:T(8,128)S(1)} %collective-permute-done.far_ref, f32[4,8,720]{2,1,0:T(8,128)S(1)} %collective-permute-done.1.near_ref, s32[24,720]{1,0:T(8,128)S(1)} %copy-done.2, bf16[16,104,128]{2,1,0:T(8,128)(2,1)S(1)} %get-tuple-element.16.own_ref, ...), custom_call_target="tpu_custom_call" | custom-call | flops 11059200 | bytes 5529088 | tf_op jit(solution)/shard_map/one_hour/pallas_call | solution.py:236
  109.3 3.5 %last_hour.1 = f32[4,8,24,720]{3,2,1,0:T(8,128)} custom-call(f32[4,8,24,720]{3,2,1,0:T(8,128)S(1)} %one_hour.1.q_ref, f32[4,8,720]{2,1,0:T(8,128)S(1)} %collective-permute-done.5.far_ref, f32[4,8,720]{2,1,0:T(8,128)S(1)} %collective-permute-done.6.near_ref, s32[24,720]{1,0:T(8,128)S(1)} %copy-done.2, bf16[16,104,128]{2,1,0:T(8,128)(2,1)S(1)} %get-tuple-element.15.own_ref, ...), custom_call_target="tpu_custom_call" | custom-call | flops 11059200 | bytes 5529088 | tf_op jit(solution)/shard_map/last_hour/pallas_call | solution.py:236
  (18 shorter events, 0.3 us)
Async XLA Ops:
  0.0 30.9 %copy-start = (f32[4,8,24,720]{3,2,1,0:T(8,128)S(1)}, f32[4,8,24,720]{3,2,1,0:T(8,128)}, u32[]{:S(2)}) copy-start(f32[4,8,24,720]{3,2,1,0:T(8,128)} %q_ref.3) | copy-start | bytes 6635524
  0.0 1.3 %copy-start.1 = (bf16[1,3,8,24,720]{4,3,2,1,0:T(8,128)(2,1)S(1)}, bf16[1,3,8,24,720]{4,3,2,1,0:T(8,128)(2,1)}, u32[]{:S(2)}) copy-start(bf16[1,3,8,24,720]{4,3,2,1,0:T(8,128)(2,1)} %field_ref.1) | copy-start | bytes 2488324
  1.3 37.7 %copy-start.3 = (s32[2]{0:T(128)S(1)}, s32[2]{0:T(128)}, u32[]{:S(2)}) copy-start(s32[2]{0:T(128)} %param.6) | copy-start | bytes 28
  2.3 12.8 %collective-permute-start.2 = (bf16[16,104,128]{2,1,0:T(8,128)(2,1)}, bf16[16,104,128]{2,1,0:T(8,128)(2,1)S(1)}, u32[]{:S(2)}, u32[]{:S(2)}) collective-permute-start(bf16[16,104,128]{2,1,0:T(8,128)(2,1)} %get-tuple-element.10), channel_id=1, source_target_pairs={{0,256},{16,272},{32,288},{48,304},{64,320},{80,336},{96,352},{112... | collective-permute-start | bytes 1277960 | tf_op jit(solution)/shard_map/ppermute | solution.py:290
  5.4 9.7 %collective-permute-start.3 = (bf16[16,104,128]{2,1,0:T(8,128)(2,1)S(1)}, bf16[16,104,128]{2,1,0:T(8,128)(2,1)}, u32[]{:S(2)}, u32[]{:S(2)}) collective-permute-start(bf16[16,104,128]{2,1,0:T(8,128)(2,1)S(1)} %get-tuple-element.9.keep_ref), channel_id=1, source_target_pairs={{240,224},{496,480},{241,225},{497,481},{242,226},{498,482},{243,2... | collective-permute-start | bytes 1277960 | tf_op jit(solution)/shard_map/ppermute | solution.py:291
  15.8 74.2 %copy-start.2 = (s32[24,720]{1,0:T(8,128)S(1)}, s32[24,720]{1,0:T(8,128)}, u32[]{:S(2)}) copy-start(s32[24,720]{1,0:T(8,128)} %mask_ref.5) | copy-start | bytes 207364
  15.8 33.3 %all-to-all-start = ((bf16[16,104,128]{2,1,0:T(8,128)(2,1)}), bf16[16,104,128]{2,1,0:T(8,128)(2,1)S(1)}, u32[]{:S(2)}, u32[]{:S(2)}) async-start(bf16[16,104,128]{2,1,0:T(8,128)(2,1)} %offer.1), calls=%async_computation | async-start | bytes 851968 | tf_op jit(solution)/shard_map/all_to_all | solution.py:300
  31.1 12.4 %collective-permute-start.1 = (f32[4,8,720]{2,1,0:T(8,128)S(1)}, f32[4,8,720]{2,1,0:T(8,128)S(1)}, u32[]{:S(2)}, u32[]{:S(2)}) collective-permute-start(f32[4,8,720]{2,1,0:T(8,128)S(1)} %get-tuple-element.19), channel_id=1, source_target_pairs={{0,1},{1,0},{2,3},{3,2},{4,5},{5,4},{6,7},{7,6},{8,9},{9,8},{10,11... | collective-permute-start | bytes 276488 | tf_op jit(solution)/shard_map/ppermute | solution.py:283
  34.8 9.8 %collective-permute-start = (f32[4,8,720]{2,1,0:T(8,128)S(1)}, f32[4,8,720]{2,1,0:T(8,128)S(1)}, u32[]{:S(2)}, u32[]{:S(2)}) collective-permute-start(f32[4,8,720]{2,1,0:T(8,128)S(1)} %get-tuple-element.20), channel_id=1, source_target_pairs={{1,2},{2,1},{3,4},{4,3},{5,6},{6,5},{7,8},{8,7},{9,10},{10,9},{11,... | collective-permute-start | bytes 276488 | tf_op jit(solution)/shard_map/ppermute | solution.py:282
  81.2 8.9 %collective-permute-start.4 = (bf16[16,104,128]{2,1,0:T(8,128)(2,1)S(1)}, bf16[16,104,128]{2,1,0:T(8,128)(2,1)S(1)}, u32[]{:S(2)}, u32[]{:S(2)}) collective-permute-start(bf16[16,104,128]{2,1,0:T(8,128)(2,1)S(1)} %get-tuple-element.16.own_ref), channel_id=1, source_target_pairs={{0,256},{16,272},{32,288},{48,304},{64,320},{80,336},{96,352},{112... | collective-permute-start | bytes 1277960 | tf_op jit(solution)/shard_map/ppermute | solution.py:305
  84.3 25.0 %collective-permute-start.7 = (bf16[16,104,128]{2,1,0:T(8,128)(2,1)S(1)}, bf16[16,104,128]{2,1,0:T(8,128)(2,1)S(1)}, u32[]{:S(2)}, u32[]{:S(2)}) collective-permute-start(bf16[16,104,128]{2,1,0:T(8,128)(2,1)S(1)} %get-tuple-element.15.own_ref), channel_id=1, source_target_pairs={{0,256},{16,272},{32,288},{48,304},{64,320},{80,336},{96,352},{112... | collective-permute-start | bytes 1277960 | tf_op jit(solution)/shard_map/ppermute | solution.py:305
  90.7 18.6 %collective-permute-start.5 = (f32[4,8,720]{2,1,0:T(8,128)S(1)}, f32[4,8,720]{2,1,0:T(8,128)S(1)}, u32[]{:S(2)}, u32[]{:S(2)}) collective-permute-start(f32[4,8,720]{2,1,0:T(8,128)S(1)} %get-tuple-element.11), channel_id=1, source_target_pairs={{1,2},{2,1},{3,4},{4,3},{5,6},{6,5},{7,8},{8,7},{9,10},{10,9},{11,... | collective-permute-start | bytes 276488 | tf_op jit(solution)/shard_map/ppermute | solution.py:282
  105.0 4.3 %collective-permute-start.6 = (f32[4,8,720]{2,1,0:T(8,128)S(1)}, f32[4,8,720]{2,1,0:T(8,128)S(1)}, u32[]{:S(2)}, u32[]{:S(2)}) collective-permute-start(f32[4,8,720]{2,1,0:T(8,128)S(1)} %get-tuple-element.12), channel_id=1, source_target_pairs={{0,1},{1,0},{2,3},{3,2},{4,5},{5,4},{6,7},{7,6},{8,9},{9,8},{10,11... | collective-permute-start | bytes 276488 | tf_op jit(solution)/shard_map/ppermute | solution.py:283

commit v14 on v13

--- a/solution.py
+++ b/solution.py
@@ -49,18 +49,25 @@
     return parts
 
 
-def pack_kernel(field_ref, keep_ref, send_ref):
-    _, levs, rows, lon = field_ref.shape[1:]
+def pack_kernel(stored_ref, keep_ref, send_ref, field_ref, landed):
+    _, levs, rows, lon = stored_ref.shape[1:]
+
+    def landing(level):
+        return pltpu.make_async_copy(stored_ref.at[0, :, level], field_ref.at[:, level], landed.at[level])
+
+    for level in range(levs):
+        landing(level).start()
     for own in range(COLUMNS):
 
         @pl.when(this_column() == own)
         def _():
             for level in range(levs):
+                landing(level).wait()
                 for half in range(2):
                     for k, lane, lanes, lo, hi, column, at, at_lane in field_parts(rows, half):
                         piece_ref = keep_ref if column == own else send_ref
                         piece_ref[level * 2 + half, at : at + hi - lo, at_lane : at_lane + lanes] = field_ref[
-                            0, k, level, lo:hi, lane : lane + lanes
+                            k, level, lo:hi, lane : lane + lanes
                         ]
 
 
@@ -70,8 +77,12 @@
     return pl.pallas_call(
         pack_kernel,
         out_shape=(half, half),
-        in_specs=[vmem],
+        in_specs=[pl.BlockSpec(memory_space=pl.ANY)],
         out_specs=(vmem, vmem),
+        scratch_shapes=[
+            pltpu.VMEM(trajectory.shape[1:], trajectory.dtype),
+            pltpu.SemaphoreType.DMA((trajectory.shape[2],)),
+        ],
         compiler_params=pltpu.CompilerParams(vmem_limit_bytes=VMEM_LIMIT),
         name="pack",
     )(trajectory)

time: 114 us -> 115 us (level)
  no operation moved by 1% of the time
where the time goes in v14:
time: 115 us; the launch traced here: 114 us
  starting transfers between devices  49.1 us (43%)
  blocking collectives  32 us (28%)
  waiting for transfers between devices  12.5 us (11%)
  Pallas kernels  9.14 us (8%)
  between operations  6.48 us (6%)
  local copies, waits for them, and re-layouts  4.6 us (4%)
    all_gather x1, blocking collectives, shards(): gathered = lax.all_gather(picked, 'vec', axis=0, axis_index_groups=rings)  32 us
    ppermute x2, starting transfers between devices, halos(): far = lax.ppermute(to_far, 'lat', between)  18.6 us
    all_to_all x1, starting transfers between devices, shards(): lax.all_to_all(offered, 'vec', 0, 0, axis_index_groups=rings, tiled=True)  15.1 us
    pallas_call x3, Pallas kernels, on_band(): pl.pallas_call(kernel, out_shape=outs, in_specs=[vmem] * len(args), out_s...  6.39 us
    ppermute x2, starting transfers between devices, halos(): return (far, lax.ppermute(to_near, 'lat', on_chip))  5.66 us
    ppermute x1, waiting for transfers between devices, shards(): crossed = lax.ppermute(send, 'vec', swap)  5.6 us
    ppermute x2, starting transfers between devices, shards(): other = [lax.ppermute(half, 'vec', swap) for half in own]  5.28 us
    ppermute x2, waiting for transfers between devices, shards(): other = [lax.ppermute(half, 'vec', swap) for half in own]  3.58 us
  transfers between devices with their start and end apart: 9, of which 4 were waited for; matrix products, arithmetic and copies ran while one was open for 3% of the time, Pallas kernels for 3%

profile of v14, /device:TPU:25, one launch (start us, length us, event | category | flops | bytes accessed | tf_op | source)
XLA Modules:
  0.0 113.9 jit_solution(2060063465518256832)
XLA Ops:
  0.0 1.3 %copy-done.1 = bf16[1,3,8,24,720]{4,3,2,1,0:T(8,128)(2,1)S(1)} copy-done((bf16[1,3,8,24,720]{4,3,2,1,0:T(8,128)(2,1)S(1)}, bf16[1,3,8,24,720]{4,3,2,1,0:T(8,128)(2,1)}, u32[]{:S(2)}) %copy-start.1) | copy-done | bytes 829464
  1.3 2.0 %pack.1 = (bf16[16,104,128]{2,1,0:T(8,128)(2,1)S(1)}, bf16[16,104,128]{2,1,0:T(8,128)(2,1)}) custom-call(bf16[1,3,8,24,720]{4,3,2,1,0:T(8,128)(2,1)S(1)} %copy-done.1), custom_call_target="tpu_custom_call" | custom-call | tf_op jit(solution)/shard_map/pack/pallas_call | solution.py:77
  3.3 3.1 %collective-permute-start.2 = (bf16[16,104,128]{2,1,0:T(8,128)(2,1)}, bf16[16,104,128]{2,1,0:T(8,128)(2,1)S(1)}, u32[]{:S(2)}, u32[]{:S(2)}) collective-permute-start(bf16[16,104,128]{2,1,0:T(8,128)(2,1)} %get-tuple-element.10), channel_id=1, source_target_pairs={{0,256},{16,272},{32,288},{48,304},{64,320},{80,336},{96,352},{112... | collective-permute-start | bytes 1277960 | tf_op jit(solution)/shard_map/ppermute | solution.py:301
  6.4 1.4 %collective-permute-start.3 = (bf16[16,104,128]{2,1,0:T(8,128)(2,1)S(1)}, bf16[16,104,128]{2,1,0:T(8,128)(2,1)}, u32[]{:S(2)}, u32[]{:S(2)}) collective-permute-start(bf16[16,104,128]{2,1,0:T(8,128)(2,1)S(1)} %get-tuple-element.9.keep_ref), channel_id=1, source_target_pairs={{240,224},{496,480},{241,225},{497,481},{242,226},{498,482},{243,2... | collective-permute-start | bytes 1277960 | tf_op jit(solution)/shard_map/ppermute | solution.py:302
  7.9 1.4 %fusion.2 = (s32[1]{0:T(128)}, s32[1]{0:T(128)}) fusion(s32[2]{0:T(128)} %param.6), kind=kLoop, calls=%fused_computation.15 | loop fusion | bytes 16 | tf_op jit(solution)/shard_map/slice | solution.py:303
  10.5 5.6 %collective-permute-done.2.crossed_ref = bf16[16,104,128]{2,1,0:T(8,128)(2,1)S(1)} collective-permute-done((bf16[16,104,128]{2,1,0:T(8,128)(2,1)}, bf16[16,104,128]{2,1,0:T(8,128)(2,1)S(1)}, u32[]{:S(2)}, u32[]{:S(2)}) %collective-permute-start.2) | collective-permute-done | bytes 426016 | tf_op jit(solution)/shard_map/ppermute | solution.py:301
  16.1 0.8 offer.1
  16.9 15.1 %all-to-all-start = ((bf16[16,104,128]{2,1,0:T(8,128)(2,1)}), bf16[16,104,128]{2,1,0:T(8,128)(2,1)S(1)}, u32[]{:S(2)}, u32[]{:S(2)}) async-start(bf16[16,104,128]{2,1,0:T(8,128)(2,1)} %offer.1), calls=%async_computation | async-start | bytes 851968 | tf_op jit(solution)/shard_map/all_to_all | solution.py:311
  32.2 3.7 %collective-permute-start.1 = (f32[4,8,720]{2,1,0:T(8,128)S(1)}, f32[4,8,720]{2,1,0:T(8,128)S(1)}, u32[]{:S(2)}, u32[]{:S(2)}) collective-permute-start(f32[4,8,720]{2,1,0:T(8,128)S(1)} %get-tuple-element.19), channel_id=1, source_target_pairs={{0,1},{1,0},{2,3},{3,2},{4,5},{5,4},{6,7},{7,6},{8,9},{9,8},{10,11... | collective-permute-start | bytes 276488 | tf_op jit(solution)/shard_map/ppermute | solution.py:294
  35.9 4.2 %collective-permute-start = (f32[4,8,720]{2,1,0:T(8,128)S(1)}, f32[4,8,720]{2,1,0:T(8,128)S(1)}, u32[]{:S(2)}, u32[]{:S(2)}) collective-permute-start(f32[4,8,720]{2,1,0:T(8,128)S(1)} %get-tuple-element.20), channel_id=1, source_target_pairs={{1,2},{2,1},{3,4},{4,3},{5,6},{6,5},{7,8},{8,7},{9,10},{10,9},{11,... | collective-permute-start | bytes 276488 | tf_op jit(solution)/shard_map/ppermute | solution.py:293
  40.1 0.6 fusion.1
  44.5 0.5 slice.41
  45.1 0.7 collective-permute-done.far_ref
  45.7 0.5 slice.40
  47.5 2.7 %all-to-all-done = bf16[16,104,128]{2,1,0:T(8,128)(2,1)S(1)} async-done(((bf16[16,104,128]{2,1,0:T(8,128)(2,1)}), bf16[16,104,128]{2,1,0:T(8,128)(2,1)S(1)}, u32[]{:S(2)}, u32[]{:S(2)}) %all-to-all-start) | async-done | bytes 426016 | tf_op jit(solution)/shard_map/all_to_all | solution.py:311
  50.2 32.0 %all_gather.4 = bf16[16,2,104,128]{3,2,0,1:T(8,128)(2,1)S(1)} all-gather(bf16[1,2,104,128]{3,2,0,1:T(8,128)(2,1)S(1)} %maximum_add_fusion), channel_id=1, replica_groups={{0,16,32,48,64,80,96,112,128,144,160,176,192,208,224,240},{256,272,288,..., dimensions={0}, use_global_device_ids=true | all-gather | bytes 905216 | tf_op jit(solution)/shard_map/all_gather | solution.py:314
  82.2 3.1 %collective-permute-start.4 = (bf16[16,104,128]{2,1,0:T(8,128)(2,1)S(1)}, bf16[16,104,128]{2,1,0:T(8,128)(2,1)S(1)}, u32[]{:S(2)}, u32[]{:S(2)}) collective-permute-start(bf16[16,104,128]{2,1,0:T(8,128)(2,1)S(1)} %get-tuple-element.16.own_ref), channel_id=1, source_target_pairs={{0,256},{16,272},{32,288},{48,304},{64,320},{80,336},{96,352},{112... | collective-permute-start | bytes 1277960 | tf_op jit(solution)/shard_map/ppermute | solution.py:316
  85.4 2.2 %collective-permute-start.7 = (bf16[16,104,128]{2,1,0:T(8,128)(2,1)S(1)}, bf16[16,104,128]{2,1,0:T(8,128)(2,1)S(1)}, u32[]{:S(2)}, u32[]{:S(2)}) collective-permute-start(bf16[16,104,128]{2,1,0:T(8,128)(2,1)S(1)} %get-tuple-element.15.own_ref), channel_id=1, source_target_pairs={{0,256},{16,272},{32,288},{48,304},{64,320},{80,336},{96,352},{112... | collective-permute-start | bytes 1277960 | tf_op jit(solution)/shard_map/ppermute | solution.py:316
  87.5 3.6 %collective-permute-done.4.other_ref = bf16[16,104,128]{2,1,0:T(8,128)(2,1)S(1)} collective-permute-done((bf16[16,104,128]{2,1,0:T(8,128)(2,1)S(1)}, bf16[16,104,128]{2,1,0:T(8,128)(2,1)S(1)}, u32[]{:S(2)}, u32[]{:S(2)}) %collective-permute-start.4) | collective-permute-done | bytes 426016 | tf_op jit(solution)/shard_map/ppermute | solution.py:316
  91.1 0.6 edge_rows.1
  91.7 14.4 %collective-permute-start.5 = (f32[4,8,720]{2,1,0:T(8,128)S(1)}, f32[4,8,720]{2,1,0:T(8,128)S(1)}, u32[]{:S(2)}, u32[]{:S(2)}) collective-permute-start(f32[4,8,720]{2,1,0:T(8,128)S(1)} %get-tuple-element.11), channel_id=1, source_target_pairs={{1,2},{2,1},{3,4},{4,3},{5,6},{6,5},{7,8},{8,7},{9,10},{10,9},{11,... | collective-permute-start | bytes 276488 | tf_op jit(solution)/shard_map/ppermute | solution.py:293
  106.1 1.9 %collective-permute-start.6 = (f32[4,8,720]{2,1,0:T(8,128)S(1)}, f32[4,8,720]{2,1,0:T(8,128)S(1)}, u32[]{:S(2)}, u32[]{:S(2)}) collective-permute-start(f32[4,8,720]{2,1,0:T(8,128)S(1)} %get-tuple-element.12), channel_id=1, source_target_pairs={{0,1},{1,0},{2,3},{3,2},{4,5},{5,4},{6,7},{7,6},{8,9},{9,8},{10,11... | collective-permute-start | bytes 276488 | tf_op jit(solution)/shard_map/ppermute | solution.py:294
  108.0 2.3 %one_hour.1.q_ref = f32[4,8,24,720]{3,2,1,0:T(8,128)S(1)} custom-call(f32[4,8,24,720]{3,2,1,0:T(8,128)S(1)} %copy-done, f32[4,8,720]{2,1,0:T(8,128)S(1)} %collective-permute-done.far_ref, f32[4,8,720]{2,1,0:T(8,128)S(1)} %collective-permute-done.1.near_ref, s32[24,720]{1,0:T(8,128)S(1)} %copy-done.2, bf16[16,104,128]{2,1,0:T(8,128)(2,1)S(1)} %get-tuple-element.16.own_ref, ...), custom_call_target="tpu_custom_call" | custom-call | flops 11059200 | bytes 5529088 | tf_op jit(solution)/shard_map/one_hour/pallas_call | solution.py:247
  110.4 3.5 %last_hour.1 = f32[4,8,24,720]{3,2,1,0:T(8,128)} custom-call(f32[4,8,24,720]{3,2,1,0:T(8,128)S(1)} %one_hour.1.q_ref, f32[4,8,720]{2,1,0:T(8,128)S(1)} %collective-permute-done.5.far_ref, f32[4,8,720]{2,1,0:T(8,128)S(1)} %collective-permute-done.6.near_ref, s32[24,720]{1,0:T(8,128)S(1)} %copy-done.2, bf16[16,104,128]{2,1,0:T(8,128)(2,1)S(1)} %get-tuple-element.15.own_ref, ...), custom_call_target="tpu_custom_call" | custom-call | flops 11059200 | bytes 5529088 | tf_op jit(solution)/shard_map/last_hour/pallas_call | solution.py:247
  (18 shorter events, 0.3 us)
Async XLA Ops:
  0.0 32.0 %copy-start = (f32[4,8,24,720]{3,2,1,0:T(8,128)S(1)}, f32[4,8,24,720]{3,2,1,0:T(8,128)}, u32[]{:S(2)}) copy-start(f32[4,8,24,720]{3,2,1,0:T(8,128)} %q_ref.3) | copy-start | bytes 6635524
  0.0 1.3 %copy-start.1 = (bf16[1,3,8,24,720]{4,3,2,1,0:T(8,128)(2,1)S(1)}, bf16[1,3,8,24,720]{4,3,2,1,0:T(8,128)(2,1)}, u32[]{:S(2)}) copy-start(bf16[1,3,8,24,720]{4,3,2,1,0:T(8,128)(2,1)} %stored_ref.1) | copy-start | bytes 2488324
  1.3 38.8 %copy-start.3 = (s32[2]{0:T(128)S(1)}, s32[2]{0:T(128)}, u32[]{:S(2)}) copy-start(s32[2]{0:T(128)} %param.6) | copy-start | bytes 28
  3.3 12.8 %collective-permute-start.2 = (bf16[16,104,128]{2,1,0:T(8,128)(2,1)}, bf16[16,104,128]{2,1,0:T(8,128)(2,1)S(1)}, u32[]{:S(2)}, u32[]{:S(2)}) collective-permute-start(bf16[16,104,128]{2,1,0:T(8,128)(2,1)} %get-tuple-element.10), channel_id=1, source_target_pairs={{0,256},{16,272},{32,288},{48,304},{64,320},{80,336},{96,352},{112... | collective-permute-start | bytes 1277960 | tf_op jit(solution)/shard_map/ppermute | solution.py:301
  6.4 9.7 %collective-permute-start.3 = (bf16[16,104,128]{2,1,0:T(8,128)(2,1)S(1)}, bf16[16,104,128]{2,1,0:T(8,128)(2,1)}, u32[]{:S(2)}, u32[]{:S(2)}) collective-permute-start(bf16[16,104,128]{2,1,0:T(8,128)(2,1)S(1)} %get-tuple-element.9.keep_ref), channel_id=1, source_target_pairs={{240,224},{496,480},{241,225},{497,481},{242,226},{498,482},{243,2... | collective-permute-start | bytes 1277960 | tf_op jit(solution)/shard_map/ppermute | solution.py:302
  16.9 74.2 %copy-start.2 = (s32[24,720]{1,0:T(8,128)S(1)}, s32[24,720]{1,0:T(8,128)}, u32[]{:S(2)}) copy-start(s32[24,720]{1,0:T(8,128)} %mask_ref.5) | copy-start | bytes 207364
  16.9 33.3 %all-to-all-start = ((bf16[16,104,128]{2,1,0:T(8,128)(2,1)}), bf16[16,104,128]{2,1,0:T(8,128)(2,1)S(1)}, u32[]{:S(2)}, u32[]{:S(2)}) async-start(bf16[16,104,128]{2,1,0:T(8,128)(2,1)} %offer.1), calls=%async_computation | async-start | bytes 851968 | tf_op jit(solution)/shard_map/all_to_all | solution.py:311
  32.2 12.4 %collective-permute-start.1 = (f32[4,8,720]{2,1,0:T(8,128)S(1)}, f32[4,8,720]{2,1,0:T(8,128)S(1)}, u32[]{:S(2)}, u32[]{:S(2)}) collective-permute-start(f32[4,8,720]{2,1,0:T(8,128)S(1)} %get-tuple-element.19), channel_id=1, source_target_pairs={{0,1},{1,0},{2,3},{3,2},{4,5},{5,4},{6,7},{7,6},{8,9},{9,8},{10,11... | collective-permute-start | bytes 276488 | tf_op jit(solution)/shard_map/ppermute | solution.py:294
  35.9 9.8 %collective-permute-start = (f32[4,8,720]{2,1,0:T(8,128)S(1)}, f32[4,8,720]{2,1,0:T(8,128)S(1)}, u32[]{:S(2)}, u32[]{:S(2)}) collective-permute-start(f32[4,8,720]{2,1,0:T(8,128)S(1)} %get-tuple-element.20), channel_id=1, source_target_pairs={{1,2},{2,1},{3,4},{4,3},{5,6},{6,5},{7,8},{8,7},{9,10},{10,9},{11,... | collective-permute-start | bytes 276488 | tf_op jit(solution)/shard_map/ppermute | solution.py:293
  82.2 8.9 %collective-permute-start.4 = (bf16[16,104,128]{2,1,0:T(8,128)(2,1)S(1)}, bf16[16,104,128]{2,1,0:T(8,128)(2,1)S(1)}, u32[]{:S(2)}, u32[]{:S(2)}) collective-permute-start(bf16[16,104,128]{2,1,0:T(8,128)(2,1)S(1)} %get-tuple-element.16.own_ref), channel_id=1, source_target_pairs={{0,256},{16,272},{32,288},{48,304},{64,320},{80,336},{96,352},{112... | collective-permute-start | bytes 1277960 | tf_op jit(solution)/shard_map/ppermute | solution.py:316
  85.4 25.0 %collective-permute-start.7 = (bf16[16,104,128]{2,1,0:T(8,128)(2,1)S(1)}, bf16[16,104,128]{2,1,0:T(8,128)(2,1)S(1)}, u32[]{:S(2)}, u32[]{:S(2)}) collective-permute-start(bf16[16,104,128]{2,1,0:T(8,128)(2,1)S(1)} %get-tuple-element.15.own_ref), channel_id=1, source_target_pairs={{0,256},{16,272},{32,288},{48,304},{64,320},{80,336},{96,352},{112... | collective-permute-start | bytes 1277960 | tf_op jit(solution)/shard_map/ppermute | solution.py:316
  91.7 18.6 %collective-permute-start.5 = (f32[4,8,720]{2,1,0:T(8,128)S(1)}, f32[4,8,720]{2,1,0:T(8,128)S(1)}, u32[]{:S(2)}, u32[]{:S(2)}) collective-permute-start(f32[4,8,720]{2,1,0:T(8,128)S(1)} %get-tuple-element.11), channel_id=1, source_target_pairs={{1,2},{2,1},{3,4},{4,3},{5,6},{6,5},{7,8},{8,7},{9,10},{10,9},{11,... | collective-permute-start | bytes 276488 | tf_op jit(solution)/shard_map/ppermute | solution.py:293
  106.1 4.3 %collective-permute-start.6 = (f32[4,8,720]{2,1,0:T(8,128)S(1)}, f32[4,8,720]{2,1,0:T(8,128)S(1)}, u32[]{:S(2)}, u32[]{:S(2)}) collective-permute-start(f32[4,8,720]{2,1,0:T(8,128)S(1)} %get-tuple-element.12), channel_id=1, source_target_pairs={{0,1},{1,0},{2,3},{3,2},{4,5},{5,4},{6,7},{7,6},{8,9},{9,8},{10,11... | collective-permute-start | bytes 276488 | tf_op jit(solution)/shard_map/ppermute | solution.py:294

commit v15 on v13

--- a/solution.py
+++ b/solution.py
@@ -1,3 +1,5 @@
+import functools
+
 import jax
 import jax.numpy as jnp
 from jax import lax
@@ -138,9 +140,9 @@
         north_ref[...] = near_ref[...]
 
 
-def rows_kernel(
-    q_ref, far_ref, near_ref, mask_ref, own_ref, other_ref,
-    to_far_ref, to_near_ref, field_ref, south_ref, north_ref,
+def row_kernel(
+    to_near, q_ref, far_ref, near_ref, mask_ref, own_ref, other_ref,
+    row_ref, field_ref, south_ref, north_ref,
 ):
     vecs, levs, rows, lon = q_ref.shape
     lev = lax.broadcasted_iota(jnp.int32, (levs, lon), 0)
@@ -151,40 +153,35 @@
         return jnp.concatenate([q_ref[v, z, r : r + 1] for z in range(levs)], axis=0)
 
     for r, step in ((0, 1), (rows - 1, -1)):
-        for own in range(COLUMNS):
-
-            @pl.when(own_column == own)
-            def _():
-                for half in range(2):
-                    for k, lane, lanes, lo, hi, column, at, at_lane in field_parts(rows, half):
-                        if lo <= r < hi:
-                            piece_ref = own_ref if column == own else other_ref
-                            base = at + (r - lo) // 8 * 8
-                            for z in range(levs):
-                                eight = piece_ref[z * 2 + half, base : base + 8].astype(jnp.float32)
-                                i = (r - lo) % 8
-                                field_ref[k, z : z + 1, lane : lane + lanes] = eight[
-                                    i : i + 1, at_lane : at_lane + lanes
-                                ]
-
-        weight = weights(*(field_ref[k, :, :lon] for k in range(FIELDS)), mask_ref[r : r + 1].astype(jnp.float32))
-        new = []
-        for v in range(vecs):
-            c, inner = row_of(v, r), row_of(v, r + step)
-            n, s = (inner, south_ref[v]) if r == 0 else (north_ref[v], inner)
-            u = jnp.where(lev == 0, c, pltpu.roll(c, 1, 0))
-            b = jnp.where(lev == levs - 1, c, pltpu.roll(c, levs - 1, 0))
-            new.append(advance(c, n, s, u, b, weight))
-
-        @pl.when(odd == (1 if r == 0 else 0))
-        def _():
+
+        @pl.when(odd == (1 if (r == 0) == to_near else 0))
+        def _(r=r, step=step):
+            for own in range(COLUMNS):
+
+                @pl.when(own_column == own)
+                def _():
+                    for half in range(2):
+                        for k, lane, lanes, lo, hi, column, at, at_lane in field_parts(rows, half):
+                            if lo <= r < hi:
+                                piece_ref = own_ref if column == own else other_ref
+                                base = at + (r - lo) // 8 * 8
+                                for z in range(levs):
+                                    eight = piece_ref[z * 2 + half, base : base + 8].astype(jnp.float32)
+                                    i = (r - lo) % 8
+                                    field_ref[k, z : z + 1, lane : lane + lanes] = eight[
+                                        i : i + 1, at_lane : at_lane + lanes
+                                    ]
+
+            weight = weights(*(field_ref[k, :, :lon] for k in range(FIELDS)), mask_ref[r : r + 1].astype(jnp.float32))
+            new = []
             for v in range(vecs):
-                to_near_ref[v] = new[v]
-
-        @pl.when(odd == (0 if r == 0 else 1))
-        def _():
+                c, inner = row_of(v, r), row_of(v, r + step)
+                n, s = (inner, south_ref[v]) if r == 0 else (north_ref[v], inner)
+                u = jnp.where(lev == 0, c, pltpu.roll(c, 1, 0))
+                b = jnp.where(lev == levs - 1, c, pltpu.roll(c, levs - 1, 0))
+                new.append(advance(c, n, s, u, b, weight))
             for v in range(vecs):
-                to_far_ref[v] = new[v]
+                row_ref[v] = new[v]
 
 
 def hour_kernel(
@@ -250,10 +247,12 @@
     )(*args)
 
 
-def edge_rows(*args):
+def edge_row(to_near, *args):
     vecs, levs, _, lon = args[0].shape
     edge = jax.ShapeDtypeStruct((vecs, levs, lon), jnp.float32)
-    return on_band(rows_kernel, "edge_rows", (edge, edge), pltpu.VMEM, levs, 30 * edge.size, args)
+    name = "near_row" if to_near else "far_row"
+    kernel = functools.partial(row_kernel, to_near)
+    return on_band(kernel, name, (edge,), pltpu.VMEM, levs, 30 * edge.size, args)[0]
 
 
 def one_hour(*args):
@@ -305,7 +304,7 @@
     other = [lax.ppermute(half, "vec", swap) for half in own]
 
     args = (perturb, *halo, sea_mask, own[0], other[0])
-    halo = halos(*edge_rows(*args))
+    halo = halos(edge_row(False, *args), edge_row(True, *args))
     return last_hour(one_hour(*args), *halo, sea_mask, own[1], other[1])
 
 

time: 114 us -> 113 us (level)
    pallas_call x3 -> x4, Pallas kernels: 6.39 us -> 6.42 us  [on_band(): pl.pallas_call(kernel, out_shape=outs, in_specs=[vmem] * len(args), out_s...]
where the time goes in v15:
time: 113 us
  starting transfers between devices  49.1 us (43%)
  blocking collectives  32 us (28%)
  waiting for transfers between devices  12.9 us (11%)
  Pallas kernels  8.14 us (7%)
  between operations  6.21 us (5%)
  local copies, waits for them, and re-layouts  4.48 us (4%)
    all_gather x1, blocking collectives, shards(): gathered = lax.all_gather(picked, 'vec', axis=0, axis_index_groups=rings)  32 us
    ppermute x2, starting transfers between devices, halos(): far = lax.ppermute(to_far, 'lat', between)  18.6 us
    all_to_all x1, starting transfers between devices, shards(): lax.all_to_all(offered, 'vec', 0, 0, axis_index_groups=rings, tiled=True)  15.1 us
    pallas_call x4, Pallas kernels, on_band(): pl.pallas_call(kernel, out_shape=outs, in_specs=[vmem] * len(args), out_s...  6.42 us
    ppermute x1, waiting for transfers between devices, shards(): crossed = lax.ppermute(send, 'vec', swap)  5.67 us
    ppermute x2, starting transfers between devices, halos(): return (far, lax.ppermute(to_near, 'lat', on_chip))  5.66 us
    ppermute x2, starting transfers between devices, shards(): other = [lax.ppermute(half, 'vec', swap) for half in own]  5.28 us
    ppermute x2, waiting for transfers between devices, shards(): other = [lax.ppermute(half, 'vec', swap) for half in own]  3.58 us
  transfers between devices with their start and end apart: 9, of which 4 were waited for; matrix products, arithmetic and copies ran while one was open for 3% of the time, Pallas kernels for 3%

profile of v15, /device:TPU:25, one launch (start us, length us, event | category | flops | bytes accessed | tf_op | source)
XLA Modules:
  0.0 112.8 jit_solution(836699677328908077)
XLA Ops:
  0.0 1.3 %copy-done.2 = bf16[1,3,8,24,720]{4,3,2,1,0:T(8,128)(2,1)S(1)} copy-done((bf16[1,3,8,24,720]{4,3,2,1,0:T(8,128)(2,1)S(1)}, bf16[1,3,8,24,720]{4,3,2,1,0:T(8,128)(2,1)}, u32[]{:S(2)}) %copy-start.2) | copy-done | bytes 829464
  1.3 0.9 pack.1
  2.3 3.1 %collective-permute-start.2 = (bf16[16,104,128]{2,1,0:T(8,128)(2,1)}, bf16[16,104,128]{2,1,0:T(8,128)(2,1)S(1)}, u32[]{:S(2)}, u32[]{:S(2)}) collective-permute-start(bf16[16,104,128]{2,1,0:T(8,128)(2,1)} %get-tuple-element.8), channel_id=1, source_target_pairs={{0,256},{16,272},{32,288},{48,304},{64,320},{80,336},{96,352},{112... | collective-permute-start | bytes 1277960 | tf_op jit(solution)/shard_map/ppermute | solution.py:289
  5.4 1.4 %collective-permute-start.3 = (bf16[16,104,128]{2,1,0:T(8,128)(2,1)S(1)}, bf16[16,104,128]{2,1,0:T(8,128)(2,1)}, u32[]{:S(2)}, u32[]{:S(2)}) collective-permute-start(bf16[16,104,128]{2,1,0:T(8,128)(2,1)S(1)} %get-tuple-element.7.keep_ref), channel_id=1, source_target_pairs={{240,224},{496,480},{241,225},{497,481},{242,226},{498,482},{243,2... | collective-permute-start | bytes 1277960 | tf_op jit(solution)/shard_map/ppermute | solution.py:290
  6.8 1.3 %fusion.2 = (s32[1]{0:T(128)}, s32[1]{0:T(128)}) fusion(s32[2]{0:T(128)} %param.6), kind=kLoop, calls=%fused_computation.15 | loop fusion | bytes 16 | tf_op jit(solution)/shard_map/slice | solution.py:291
  9.4 5.7 %collective-permute-done.2.crossed_ref = bf16[16,104,128]{2,1,0:T(8,128)(2,1)S(1)} collective-permute-done((bf16[16,104,128]{2,1,0:T(8,128)(2,1)}, bf16[16,104,128]{2,1,0:T(8,128)(2,1)S(1)}, u32[]{:S(2)}, u32[]{:S(2)}) %collective-permute-start.2) | collective-permute-done | bytes 426016 | tf_op jit(solution)/shard_map/ppermute | solution.py:289
  15.1 0.8 offer.1
  15.8 15.1 %all-to-all-start = ((bf16[16,104,128]{2,1,0:T(8,128)(2,1)}), bf16[16,104,128]{2,1,0:T(8,128)(2,1)S(1)}, u32[]{:S(2)}, u32[]{:S(2)}) async-start(bf16[16,104,128]{2,1,0:T(8,128)(2,1)} %offer.1), calls=%async_computation | async-start | bytes 851968 | tf_op jit(solution)/shard_map/all_to_all | solution.py:299
  31.1 3.7 %collective-permute-start.1 = (f32[4,8,720]{2,1,0:T(8,128)S(1)}, f32[4,8,720]{2,1,0:T(8,128)S(1)}, u32[]{:S(2)}, u32[]{:S(2)}) collective-permute-start(f32[4,8,720]{2,1,0:T(8,128)S(1)} %get-tuple-element.15), channel_id=1, source_target_pairs={{0,1},{1,0},{2,3},{3,2},{4,5},{5,4},{6,7},{7,6},{8,9},{9,8},{10,11... | collective-permute-start | bytes 276488 | tf_op jit(solution)/shard_map/ppermute | solution.py:282
  34.8 4.2 %collective-permute-start = (f32[4,8,720]{2,1,0:T(8,128)S(1)}, f32[4,8,720]{2,1,0:T(8,128)S(1)}, u32[]{:S(2)}, u32[]{:S(2)}) collective-permute-start(f32[4,8,720]{2,1,0:T(8,128)S(1)} %get-tuple-element.16), channel_id=1, source_target_pairs={{1,2},{2,1},{3,4},{4,3},{5,6},{6,5},{7,8},{8,7},{9,10},{10,9},{11,... | collective-permute-start | bytes 276488 | tf_op jit(solution)/shard_map/ppermute | solution.py:281
  39.1 0.6 fusion.1
  43.3 0.5 slice.41
  43.8 0.9 collective-permute-done.far_ref
  44.7 0.5 slice.40
  46.4 2.8 %all-to-all-done = bf16[16,104,128]{2,1,0:T(8,128)(2,1)S(1)} async-done(((bf16[16,104,128]{2,1,0:T(8,128)(2,1)}), bf16[16,104,128]{2,1,0:T(8,128)(2,1)S(1)}, u32[]{:S(2)}, u32[]{:S(2)}) %all-to-all-start) | async-done | bytes 426016 | tf_op jit(solution)/shard_map/all_to_all | solution.py:299
  49.2 32.0 %all_gather.4 = bf16[16,2,104,128]{3,2,0,1:T(8,128)(2,1)S(1)} all-gather(bf16[1,2,104,128]{3,2,0,1:T(8,128)(2,1)S(1)} %maximum_add_fusion), channel_id=1, replica_groups={{0,16,32,48,64,80,96,112,128,144,160,176,192,208,224,240},{256,272,288,..., dimensions={0}, use_global_device_ids=true | all-gather | bytes 905216 | tf_op jit(solution)/shard_map/all_gather | solution.py:302
  81.2 3.1 %collective-permute-start.4 = (bf16[16,104,128]{2,1,0:T(8,128)(2,1)S(1)}, bf16[16,104,128]{2,1,0:T(8,128)(2,1)S(1)}, u32[]{:S(2)}, u32[]{:S(2)}) collective-permute-start(bf16[16,104,128]{2,1,0:T(8,128)(2,1)S(1)} %get-tuple-element.12.own_ref), channel_id=1, source_target_pairs={{0,256},{16,272},{32,288},{48,304},{64,320},{80,336},{96,352},{112... | collective-permute-start | bytes 1277960 | tf_op jit(solution)/shard_map/ppermute | solution.py:304
  84.3 2.2 %collective-permute-start.7 = (bf16[16,104,128]{2,1,0:T(8,128)(2,1)S(1)}, bf16[16,104,128]{2,1,0:T(8,128)(2,1)S(1)}, u32[]{:S(2)}, u32[]{:S(2)}) collective-permute-start(bf16[16,104,128]{2,1,0:T(8,128)(2,1)S(1)} %get-tuple-element.11.own_ref), channel_id=1, source_target_pairs={{0,256},{16,272},{32,288},{48,304},{64,320},{80,336},{96,352},{112... | collective-permute-start | bytes 1277960 | tf_op jit(solution)/shard_map/ppermute | solution.py:304
  86.5 3.6 %collective-permute-done.4.other_ref = bf16[16,104,128]{2,1,0:T(8,128)(2,1)S(1)} collective-permute-done((bf16[16,104,128]{2,1,0:T(8,128)(2,1)S(1)}, bf16[16,104,128]{2,1,0:T(8,128)(2,1)S(1)}, u32[]{:S(2)}, u32[]{:S(2)}) %collective-permute-start.4) | collective-permute-done | bytes 426016 | tf_op jit(solution)/shard_map/ppermute | solution.py:304
  90.4 14.4 %collective-permute-start.5 = (f32[4,8,720]{2,1,0:T(8,128)S(1)}, f32[4,8,720]{2,1,0:T(8,128)S(1)}, u32[]{:S(2)}, u32[]{:S(2)}) collective-permute-start(f32[4,8,720]{2,1,0:T(8,128)S(1)} %far_row.1), channel_id=1, source_target_pairs={{1,2},{2,1},{3,4},{4,3},{5,6},{6,5},{7,8},{8,7},{9,10},{10,9},{11,... | collective-permute-start | bytes 276488 | tf_op jit(solution)/shard_map/ppermute | solution.py:281
  104.7 0.3 near_row.1
  105.1 1.9 %collective-permute-start.6 = (f32[4,8,720]{2,1,0:T(8,128)S(1)}, f32[4,8,720]{2,1,0:T(8,128)S(1)}, u32[]{:S(2)}, u32[]{:S(2)}) collective-permute-start(f32[4,8,720]{2,1,0:T(8,128)S(1)} %near_row.1), channel_id=1, source_target_pairs={{0,1},{1,0},{2,3},{3,2},{4,5},{5,4},{6,7},{7,6},{8,9},{9,8},{10,11... | collective-permute-start | bytes 276488 | tf_op jit(solution)/shard_map/ppermute | solution.py:282
  107.0 2.3 %one_hour.1.q_ref = f32[4,8,24,720]{3,2,1,0:T(8,128)S(1)} custom-call(f32[4,8,24,720]{3,2,1,0:T(8,128)S(1)} %copy-done, f32[4,8,720]{2,1,0:T(8,128)S(1)} %collective-permute-done.far_ref, f32[4,8,720]{2,1,0:T(8,128)S(1)} %collective-permute-done.1.near_ref, s32[24,720]{1,0:T(8,128)S(1)} %copy-done.1, bf16[16,104,128]{2,1,0:T(8,128)(2,1)S(1)} %get-tuple-element.12.own_ref, ...), custom_call_target="tpu_custom_call" | custom-call | flops 11059200 | bytes 5529088 | tf_op jit(solution)/shard_map/one_hour/pallas_call | solution.py:233
  109.4 3.5 %last_hour.1 = f32[4,8,24,720]{3,2,1,0:T(8,128)} custom-call(f32[4,8,24,720]{3,2,1,0:T(8,128)S(1)} %one_hour.1.q_ref, f32[4,8,720]{2,1,0:T(8,128)S(1)} %collective-permute-done.5.far_ref, f32[4,8,720]{2,1,0:T(8,128)S(1)} %collective-permute-done.6.near_ref, s32[24,720]{1,0:T(8,128)S(1)} %copy-done.1, bf16[16,104,128]{2,1,0:T(8,128)(2,1)S(1)} %get-tuple-element.11.own_ref, ...), custom_call_target="tpu_custom_call" | custom-call | flops 11059200 | bytes 5529088 | tf_op jit(solution)/shard_map/last_hour/pallas_call | solution.py:233
  (19 shorter events, 0.6 us)
Async XLA Ops:
  0.0 30.9 %copy-start = (f32[4,8,24,720]{3,2,1,0:T(8,128)S(1)}, f32[4,8,24,720]{3,2,1,0:T(8,128)}, u32[]{:S(2)}) copy-start(f32[4,8,24,720]{3,2,1,0:T(8,128)} %q_ref.5) | copy-start | bytes 6635524
  0.0 1.3 %copy-start.2 = (bf16[1,3,8,24,720]{4,3,2,1,0:T(8,128)(2,1)S(1)}, bf16[1,3,8,24,720]{4,3,2,1,0:T(8,128)(2,1)}, u32[]{:S(2)}) copy-start(bf16[1,3,8,24,720]{4,3,2,1,0:T(8,128)(2,1)} %field_ref.1) | copy-start | bytes 2488324
  1.3 37.7 %copy-start.3 = (s32[2]{0:T(128)S(1)}, s32[2]{0:T(128)}, u32[]{:S(2)}) copy-start(s32[2]{0:T(128)} %param.6) | copy-start | bytes 28
  2.3 12.8 %collective-permute-start.2 = (bf16[16,104,128]{2,1,0:T(8,128)(2,1)}, bf16[16,104,128]{2,1,0:T(8,128)(2,1)S(1)}, u32[]{:S(2)}, u32[]{:S(2)}) collective-permute-start(bf16[16,104,128]{2,1,0:T(8,128)(2,1)} %get-tuple-element.8), channel_id=1, source_target_pairs={{0,256},{16,272},{32,288},{48,304},{64,320},{80,336},{96,352},{112... | collective-permute-start | bytes 1277960 | tf_op jit(solution)/shard_map/ppermute | solution.py:289
  5.4 9.7 %collective-permute-start.3 = (bf16[16,104,128]{2,1,0:T(8,128)(2,1)S(1)}, bf16[16,104,128]{2,1,0:T(8,128)(2,1)}, u32[]{:S(2)}, u32[]{:S(2)}) collective-permute-start(bf16[16,104,128]{2,1,0:T(8,128)(2,1)S(1)} %get-tuple-element.7.keep_ref), channel_id=1, source_target_pairs={{240,224},{496,480},{241,225},{497,481},{242,226},{498,482},{243,2... | collective-permute-start | bytes 1277960 | tf_op jit(solution)/shard_map/ppermute | solution.py:290
  15.8 74.2 %copy-start.1 = (s32[24,720]{1,0:T(8,128)S(1)}, s32[24,720]{1,0:T(8,128)}, u32[]{:S(2)}) copy-start(s32[24,720]{1,0:T(8,128)} %mask_ref.7) | copy-start | bytes 207364
  15.8 33.3 %all-to-all-start = ((bf16[16,104,128]{2,1,0:T(8,128)(2,1)}), bf16[16,104,128]{2,1,0:T(8,128)(2,1)S(1)}, u32[]{:S(2)}, u32[]{:S(2)}) async-start(bf16[16,104,128]{2,1,0:T(8,128)(2,1)} %offer.1), calls=%async_computation | async-start | bytes 851968 | tf_op jit(solution)/shard_map/all_to_all | solution.py:299
  31.1 12.1 %collective-permute-start.1 = (f32[4,8,720]{2,1,0:T(8,128)S(1)}, f32[4,8,720]{2,1,0:T(8,128)S(1)}, u32[]{:S(2)}, u32[]{:S(2)}) collective-permute-start(f32[4,8,720]{2,1,0:T(8,128)S(1)} %get-tuple-element.15), channel_id=1, source_target_pairs={{0,1},{1,0},{2,3},{3,2},{4,5},{5,4},{6,7},{7,6},{8,9},{9,8},{10,11... | collective-permute-start | bytes 276488 | tf_op jit(solution)/shard_map/ppermute | solution.py:282
  34.8 9.8 %collective-permute-start = (f32[4,8,720]{2,1,0:T(8,128)S(1)}, f32[4,8,720]{2,1,0:T(8,128)S(1)}, u32[]{:S(2)}, u32[]{:S(2)}) collective-permute-start(f32[4,8,720]{2,1,0:T(8,128)S(1)} %get-tuple-element.16), channel_id=1, source_target_pairs={{1,2},{2,1},{3,4},{4,3},{5,6},{6,5},{7,8},{8,7},{9,10},{10,9},{11,... | collective-permute-start | bytes 276488 | tf_op jit(solution)/shard_map/ppermute | solution.py:281
  81.2 8.9 %collective-permute-start.4 = (bf16[16,104,128]{2,1,0:T(8,128)(2,1)S(1)}, bf16[16,104,128]{2,1,0:T(8,128)(2,1)S(1)}, u32[]{:S(2)}, u32[]{:S(2)}) collective-permute-start(bf16[16,104,128]{2,1,0:T(8,128)(2,1)S(1)} %get-tuple-element.12.own_ref), channel_id=1, source_target_pairs={{0,256},{16,272},{32,288},{48,304},{64,320},{80,336},{96,352},{112... | collective-permute-start | bytes 1277960 | tf_op jit(solution)/shard_map/ppermute | solution.py:304
  84.3 25.0 %collective-permute-start.7 = (bf16[16,104,128]{2,1,0:T(8,128)(2,1)S(1)}, bf16[16,104,128]{2,1,0:T(8,128)(2,1)S(1)}, u32[]{:S(2)}, u32[]{:S(2)}) collective-permute-start(bf16[16,104,128]{2,1,0:T(8,128)(2,1)S(1)} %get-tuple-element.11.own_ref), channel_id=1, source_target_pairs={{0,256},{16,272},{32,288},{48,304},{64,320},{80,336},{96,352},{112... | collective-permute-start | bytes 1277960 | tf_op jit(solution)/shard_map/ppermute | solution.py:304
  90.4 19.0 %collective-permute-start.5 = (f32[4,8,720]{2,1,0:T(8,128)S(1)}, f32[4,8,720]{2,1,0:T(8,128)S(1)}, u32[]{:S(2)}, u32[]{:S(2)}) collective-permute-start(f32[4,8,720]{2,1,0:T(8,128)S(1)} %far_row.1), channel_id=1, source_target_pairs={{1,2},{2,1},{3,4},{4,3},{5,6},{6,5},{7,8},{8,7},{9,10},{10,9},{11,... | collective-permute-start | bytes 276488 | tf_op jit(solution)/shard_map/ppermute | solution.py:281
  105.1 4.3 %collective-permute-start.6 = (f32[4,8,720]{2,1,0:T(8,128)S(1)}, f32[4,8,720]{2,1,0:T(8,128)S(1)}, u32[]{:S(2)}, u32[]{:S(2)}) collective-permute-start(f32[4,8,720]{2,1,0:T(8,128)S(1)} %near_row.1), channel_id=1, source_target_pairs={{0,1},{1,0},{2,3},{3,2},{4,5},{5,4},{6,7},{7,6},{8,9},{9,8},{10,11... | collective-permute-start | bytes 276488 | tf_op jit(solution)/shard_map/ppermute | solution.py:282
